TPU v7x, 512 devices: a whole 4x4x16 slice. The times are simulated.
512 devices in a mesh: replica: 16 (over z_lo, y), fsdp: 32 (over z_hi, x, core).
Axes of the slice: x: 4, y: 4, z: 16 (z_hi: 4, z_lo: 4; z = z_hi * 4 + z_lo), core: 2. Of those that a mesh axis runs over, the one named last changes fastest.
Arguments:
- weights: bfloat16 [16, 8192, 512], P('replica', 'fsdp'), may hold values from -0.0625 to 0.0625
- first_moment: float32 [16, 8192, 512], P('replica', 'fsdp'), may hold values from -0.09375 to 0.09375
- second_moment: float32 [16, 8192, 512], P('replica', 'fsdp'), may hold values from 2.4414062e-06 to 0.00024414062
- anchor: float32 [8192, 512], P(('fsdp', 'replica')), may hold values from -0.0625 to 0.0625
- momentum: float32 [8192, 512], P(('fsdp', 'replica')), may hold values from -0.03 to 0.03
- inputs: bfloat16 [16, 4096, 8192], P('replica', 'fsdp'), may hold values from -6 to 6
- targets: bfloat16 [16, 4096, 512], P('replica', 'fsdp'), may hold values from -6 to 6
- keep_mask: int32 [16, 4096], P('replica', 'fsdp'), may hold values 0 or 1
Outputs:
- new_weights: bfloat16 [16, 8192, 512], P('replica', 'fsdp')
- new_first: float32 [16, 8192, 512], P('replica', 'fsdp')
- new_anchor: float32 [8192, 512], P(('fsdp', 'replica'))
- new_momentum: float32 [8192, 512], P(('fsdp', 'replica'))
All inputs are finite; a program needn't handle non-finite values. No bound on the sum of `keep_mask` on one device may be relied on, other than what follows from the above.
Results may differ from a plain program's by a relative error of at most 0.01.
Values may be sent and summed in bfloat16 or wider, within the bound.
No kernel may reach another device: no remote copies, remote signals or barrier semaphores. Data moves between devices by JAX's collectives and lax.ppermute only.
A program may use at most 64 MiB of HBM per device.

v0:
```python
import jax
import jax.numpy as jnp
from jax import lax
from jax.sharding import PartitionSpec as P

BETA_FIRST = 0.9
BETA_SECOND = 0.95
EPSILON = 1e-08
INNER_RATE = 0.002
WEIGHT_DECAY = 0.1
OUTER_RATE = 0.7
NESTEROV = 0.9
MIXING = 0.5


def shards(weights, first_moment, second_moment, anchor, momentum, inputs, targets, keep_mask):
    initial = weights[0]
    tokens = inputs[0]
    goal_rows = targets[0]
    mask_rows = keep_mask[0].astype(jnp.float32)[:, None]
    token_count = tokens.shape[0] * lax.axis_size("fsdp")
    block_width = initial.shape[0]
    out_width = initial.shape[1]
    columns = lax.all_to_all(tokens, "fsdp", split_axis=1, concat_axis=0, tiled=True)
    pieces = lax.all_gather(initial, "fsdp", axis=0, tiled=True)
    block_count = pieces.shape[0] // block_width
    slab_cols = tokens
    slab_cols = slab_cols.reshape(tokens.shape[0], block_count, block_width)
    piece_blocks = pieces.reshape(block_count, block_width, out_width)
    partials = jnp.einsum(
        "tbf,bfk->btk", slab_cols, piece_blocks, preferred_element_type=jnp.float32
    )
    rounded = lax.optimization_barrier(partials.astype(jnp.bfloat16))
    projected = jnp.sum(rounded.astype(jnp.float32), 0)
    residual = ((projected - goal_rows.astype(jnp.float32)) * mask_rows / token_count).astype(
        jnp.bfloat16
    )
    gradient = lax.dot_general(
        columns,
        lax.all_gather(residual, "fsdp", axis=0, tiled=True),
        (((0,), (0,)), ((), ())),
        preferred_element_type=jnp.float32,
    )
    weight_f = initial.astype(jnp.float32)
    first_new = BETA_FIRST * first_moment[0] + (1.0 - BETA_FIRST) * gradient
    second_new = BETA_SECOND * second_moment[0] + (1.0 - BETA_SECOND) * gradient * gradient
    moved = weight_f - INNER_RATE * (
        first_new / (jnp.sqrt(second_new) + EPSILON) + WEIGHT_DECAY * weight_f
    )
    inner_weight = moved.astype(jnp.bfloat16)
    workers = lax.axis_size("replica")
    share_rows = anchor.shape[0]
    share_start = lax.axis_index("replica") * share_rows
    weight_mean = lax.psum(weight_f, "replica") / workers
    anchor_block, moment_block = (
        lax.all_gather(anchor, "replica", axis=0, tiled=True),
        lax.all_gather(momentum, "replica", axis=0, tiled=True),
    )
    pseudo_grad = anchor_block - weight_mean
    moment_next = NESTEROV * moment_block + pseudo_grad
    block_anchor = anchor_block - OUTER_RATE * (pseudo_grad + NESTEROV * moment_next)
    new_anchor = lax.dynamic_slice_in_dim(block_anchor, share_start, share_rows, 0)
    new_momentum = lax.dynamic_slice_in_dim(moment_next, share_start, share_rows, 0)
    mixed = ((1.0 - MIXING) * block_anchor + MIXING * inner_weight.astype(jnp.float32)).astype(
        jnp.bfloat16
    )
    return (mixed[None], first_new[None], new_anchor, new_momentum)


def solution(mesh):
    return jax.shard_map(
        shards,
        mesh=mesh,
        in_specs=(
            P("replica", "fsdp", None),
            P("replica", "fsdp", None),
            P("replica", "fsdp", None),
            P(("fsdp", "replica"), None),
            P(("fsdp", "replica"), None),
            P("replica", "fsdp", None),
            P("replica", "fsdp", None),
            P("replica", "fsdp"),
        ),
        out_specs=(
            P("replica", "fsdp", None),
            P("replica", "fsdp", None),
            P(("fsdp", "replica"), None),
            P(("fsdp", "replica"), None),
        ),
        check_vma=False,
    )
```

profile of v0, /device:TPU:1, one launch (start us, length us, event | category | flops | bytes accessed | tf_op | source)
XLA Modules:
  0.0 360.8 jit_solution(431012148547076615)
XLA Ops:
  8.0 0.0 all-gather.6.cloned.1.call-start
  8.0 0.7 all-gather.6.cloned.1.call-update
  8.7 0.0 copy-start.1
  8.7 0.0 copy-start.5
  8.8 4.1 %copy.47 = bf16[1,128,8192]{1,2,0:T(8,128)(2,1)} copy(bf16[1,128,8192]{2,1,0:T(8,128)(2,1)} %param.13) | data formatting | bytes 4194304 | tf_op args[5]
  12.9 19.2 %all-to-all-start = ((bf16[128,32,256]{0,2,1:T(8,128)(2,1)}), bf16[128,32,256]{0,2,1:T(8,128)(2,1)S(1)}, u32[]{:S(2)}, u32[]{:S(2)}) async-start(bf16[128,32,256]{0,2,1:T(8,128)(2,1)} %bitcast.3), calls=%async_computation | async-start | bytes 4194304 | tf_op jit(solution)/shard_map/all_to_all | solution.py:24
  32.1 0.0 all-reduce.2.cloned.1.call-start
  32.1 0.0 copy-done.1
  32.1 0.1 copy.42
  32.3 0.8 bitcast_convert_fusion
  33.1 0.0 all-reduce.2.cloned.1.call-update
  33.1 0.0 all-gather.4.cloned.1.call-start
  33.2 0.0 copy-done.5
  33.2 199.8 %all-gather.6.cloned.1.call-done = bf16[1,8192,512]{2,1,0:T(8,128)(2,1)} async-done(((bf16[1,256,512]{2,1,0:T(8,128)(2,1)}), bf16[1,8192,512]{2,1,0:T(8,128)(2,1)}) %all-gather.6.cloned.1.call-update) | async-done | bytes 8388624 | tf_op jit(solution)/shard_map/all_gather | solution.py:25
  233.0 5.4 %convolution_convert_fusion = bf16[32,128,512]{2,1,0:T(8,128)(2,1)S(1)} fusion(bf16[128,32,256]{0,2,1:T(8,128)(2,1)} %bitcast.3, bf16[32,256,512]{2,1,0:T(8,128)(2,1)} %bitcast.40), kind=kOutput, calls=%fused_computation.1 | convolution fusion | flops 1075838976 | bytes 14680064 | tf_op jit(solution)/shard_map/tbf,bfk->btk/dot_general | solution.py:30
  238.5 0.0 copy-start.2
  238.5 0.0 copy-start.3
  238.5 0.0 copy-start.4
  238.5 0.6 convert_reduce_fusion
  239.1 0.3 copy-done.2
  239.4 0.7 fusion.12
  240.1 0.0 all-gather.4.cloned.1.call-update
  240.2 0.0 copy-done.3
  240.2 41.0 %all_gather.13 = f32[256,512]{1,0:T(8,128)S(1)} all-gather(f32[16,512]{1,0:T(8,128)S(1)} %copy-done.3), channel_id=1, replica_groups=mesh['replica'=16,'fsdp'=32] {'replica'}, dimensions={0}, use_global_device_ids=true | all-gather | bytes 557056 | tf_op jit(solution)/shard_map/all_gather | solution.py:57
  281.2 0.2 copy.44
  281.4 0.0 copy-done.4
  281.4 55.5 %all_gather.12 = f32[256,512]{1,0:T(8,128)S(1)} all-gather(f32[16,512]{1,0:T(8,128)S(1)} %copy-done.4), channel_id=1, replica_groups=mesh['replica'=16,'fsdp'=32] {'replica'}, dimensions={0}, use_global_device_ids=true | all-gather | bytes 557056 | tf_op jit(solution)/shard_map/all_gather | solution.py:56
  336.9 1.0 copy.45
  337.9 0.0 copy-start
  337.9 2.1 copy.46
  340.0 2.0 copy.50
  342.1 0.0 all-to-all-done
  342.1 2.9 copy.49
  344.9 0.0 all-reduce.2.cloned.1.call-done
  344.9 0.0 all-gather.4.cloned.1.call-done
  344.9 0.0 copy-done
  344.9 4.9 %fusion.9 = (bf16[1,256,512]{1,2,0:T(8,128)(2,1)S(1)}, f32[256,512]{0,1:T(8,128)S(1)}, f32[256,512]{0,1:T(8,128)S(1)}, f32[1,256,512]{1,2,0:T(8,128)S(1)}) fusion(f32[1,256,512]{1,2,0:T(8,128)} %copy.50, f32[1,256,512]{1,2,0:T(8,128)} %copy.46, bf16[1,256,512]{1,2,0:T(8,128)(2,1)S(1)} %copy.42, f32[256,512]{0,1:T(8,128)S(1)} %copy-done, ...), kind=kOutput, calls=%fused_computation.18 | convolution fusion | flops 1077280768 | bytes 11010048 | tf_op jit(solution)/shard_map/dot_general | solution.py:38
  349.8 0.2 constant_dynamic-slice_fusion
  350.0 0.7 copy.53
  350.8 0.7 copy.54
  351.5 1.0 copy.52
  352.5 0.8 copy.51
  (1 shorter events, 0.0 us)
Async XLA Ops:
  8.0 225.0 %all-gather.6.cloned.1.call-start = ((), (), s32[]{:S(2)}) async-start(), calls=%async_computation.3 | async-start | bytes 8650752 | tf_op jit(solution)/shard_map/all_gather | solution.py:25
  8.7 23.4 %copy-start.1 = (bf16[1,256,512]{2,1,0:T(8,128)(2,1)S(1)}, bf16[1,256,512]{2,1,0:T(8,128)(2,1)}, u32[]{:S(2)}) copy-start(bf16[1,256,512]{2,1,0:T(8,128)(2,1)} %param.8) | copy-start | bytes 786436
  8.7 24.4 %copy-start.5 = (s32[1,128]{1,0:T(1,128)S(1)}, s32[1,128]{1,0:T(1,128)}, u32[]{:S(2)}) copy-start(s32[1,128]{1,0:T(1,128)} %param.15) | copy-start | bytes 1540
  12.9 329.2 %all-to-all-start = ((bf16[128,32,256]{0,2,1:T(8,128)(2,1)}), bf16[128,32,256]{0,2,1:T(8,128)(2,1)S(1)}, u32[]{:S(2)}, u32[]{:S(2)}) async-start(bf16[128,32,256]{0,2,1:T(8,128)(2,1)} %bitcast.3), calls=%async_computation | async-start | bytes 4194304 | tf_op jit(solution)/shard_map/all_to_all | solution.py:24
  32.1 312.9 %all-reduce.2.cloned.1.call-start = ((), (), s32[]{:S(2)}) async-start(), calls=%async_computation.1 | async-start | bytes 1048576 | tf_op jit(solution)/shard_map/psum | solution.py:54
  33.1 311.8 %all-gather.4.cloned.1.call-start = ((), (), s32[]{:S(2)}) async-start(), calls=%async_computation.2 | async-start | bytes 4325376 | tf_op jit(solution)/shard_map/all_gather | solution.py:40
  238.5 0.9 copy-start.2
  238.5 1.7 copy-start.3
  238.5 42.9 %copy-start.4 = (f32[16,512]{1,0:T(8,128)S(1)}, f32[16,512]{1,0:T(8,128)}, u32[]{:S(2)}) copy-start(f32[16,512]{1,0:T(8,128)} %param.11) | copy-start | bytes 98308
  337.9 7.0 %copy-start = (f32[256,512]{0,1:T(8,128)S(1)}, f32[256,512]{0,1:T(8,128)}, u32[]{:S(2)}) copy-start(f32[256,512]{0,1:T(8,128)} %copy.45) | copy-start | bytes 1572868
Sparse Core Ops, SparseCore 0:
  12.4 220.5 all-gather.5
  240.3 95.3 all-gather.3
Sparse Core Ops, SparseCore 1:
  35.5 297.0 all-reduce.1
where the time goes:
time: 368 us; the launch traced here: 361 us
  waiting for transfers between devices  201 us (55%)
  blocking collectives  96.5 us (26%)
  starting transfers between devices  19.3 us (5%)
  local copies, waits for them, and re-layouts  16.2 us (4%)
  between operations  15.6 us (4%)
  matrix products  10.3 us (3%)
    all_gather x1, waiting for transfers between devices, shards(): pieces = lax.all_gather(initial, 'fsdp', axis=0, tiled=True)  200 us
    all_gather x1, blocking collectives, shards(): lax.all_gather(anchor, 'replica', axis=0, tiled=True)  55.5 us
    all_gather x1, blocking collectives, shards(): lax.all_gather(momentum, 'replica', axis=0, tiled=True)  41 us
    all_to_all x1, starting transfers between devices, shards(): lax.all_to_all(tokens, 'fsdp', split_axis=1, concat_axis=0, tiled=True)  19.2 us
    unnamed x20, local copies, waits for them, and re-layouts  12 us
  transfers between devices with their start and end apart: 4, of which 1 were waited for; matrix products, arithmetic and copies ran while one was open for 6% of the time, Pallas kernels for 0%

commit v1 on v0

v1 whole, which is shorter than its diff:
```python
import jax
import jax.numpy as jnp
from jax import lax
from jax.experimental import pallas as pl
from jax.experimental.pallas import tpu as pltpu
from jax.sharding import PartitionSpec as P

BETA_FIRST = 0.9
BETA_SECOND = 0.95
EPSILON = 1e-08
INNER_RATE = 0.002
WEIGHT_DECAY = 0.1
OUTER_RATE = 0.7
NESTEROV = 0.9
MIXING = 0.5

SLABS = 4
PLANE = 8
PLANES = [[z * PLANE + i for i in range(PLANE)] for z in range(SLABS)]


def shift_z(value, step):
    pairs = [
        (z * PLANE + i, (z + step) % SLABS * PLANE + i)
        for z in range(SLABS)
        for i in range(PLANE)
    ]
    return lax.ppermute(value, "fsdp", pairs)


def pack_kernel(slab_ref, tokens_ref, packed_ref):
    width = packed_ref.shape[2]
    for i in range(PLANE):
        packed_ref[i] = tokens_ref[:, i * width : (i + 1) * width]


def pack(tokens, slabs, width):
    rows = tokens.shape[0]
    return pl.pallas_call(
        pack_kernel,
        out_shape=jax.ShapeDtypeStruct((PLANE, rows, SLABS * width), tokens.dtype),
        grid_spec=pltpu.PrefetchScalarGridSpec(
            num_scalar_prefetch=1,
            grid=(SLABS,),
            in_specs=[pl.BlockSpec((rows, PLANE * width), lambda k, s: (0, s[k]))],
            out_specs=pl.BlockSpec((PLANE, rows, width), lambda k, s: (0, 0, k)),
        ),
        name="pack_columns",
    )(slabs, tokens)


def project_kernel(x_ref, w0_ref, w1_ref, w2_ref, w3_ref, out_ref):
    width = w0_ref.shape[0]
    total = None
    for k, w_ref in enumerate((w0_ref, w1_ref, w2_ref, w3_ref)):
        part = jnp.dot(
            x_ref[:, k * width : (k + 1) * width],
            w_ref[...],
            preferred_element_type=jnp.float32,
        )
        total = part if total is None else total + part
    out_ref[...] = total.astype(out_ref.dtype)


def project(columns, pieces):
    out_width = pieces[0].shape[1]
    return pl.pallas_call(
        project_kernel,
        out_shape=jax.ShapeDtypeStruct((columns.shape[0], out_width), jnp.bfloat16),
        compiler_params=pltpu.CompilerParams(vmem_limit_bytes=32 << 20),
        name="project",
    )(columns, *pieces)


def shards(weights, first_moment, second_moment, anchor, momentum, inputs, targets, keep_mask):
    initial = weights[0]
    tokens = inputs[0]
    goal_rows = targets[0]
    mask_rows = keep_mask[0].astype(jnp.float32)[:, None]
    rows = tokens.shape[0]
    width, out_width = initial.shape
    token_count = rows * lax.axis_size("fsdp")
    workers = lax.axis_size("replica")
    half = width // 2
    slab = lax.axis_index("fsdp") // PLANE

    before = shift_z(initial, 1)
    after = shift_z(initial, -1)
    opposite = jnp.concatenate(
        [shift_z(before[:half], 1), shift_z(after[half:], -1)], axis=0
    )
    order = jnp.stack([slab, (slab + 3) % SLABS, (slab + 1) % SLABS, (slab + 2) % SLABS])

    packed = pack(tokens, order.astype(jnp.int32), width)
    columns = lax.all_to_all(packed, "fsdp", 0, 0, axis_index_groups=PLANES)
    columns = columns.reshape(PLANE * rows, SLABS * width)

    share_rows = anchor.shape[0]
    every = lax.all_to_all(
        initial.reshape(workers, share_rows, out_width), "replica", 0, 0
    )
    weight_mean = jnp.sum(every.astype(jnp.float32), 0) / workers
    pseudo_grad = anchor - weight_mean
    new_momentum = NESTEROV * momentum + pseudo_grad
    new_anchor = anchor - OUTER_RATE * (pseudo_grad + NESTEROV * new_momentum)
    block_anchor = lax.all_to_all(
        jnp.broadcast_to(new_anchor[None], (workers, share_rows, out_width)), "replica", 0, 0
    ).reshape(width, out_width)

    partials = project(columns, (initial, before, after, opposite))
    mine = lax.all_to_all(
        partials.reshape(PLANE, rows, out_width), "fsdp", 0, 0, axis_index_groups=PLANES
    )
    projected = jnp.sum(mine.astype(jnp.float32), 0)
    residual = ((projected - goal_rows.astype(jnp.float32)) * mask_rows / token_count).astype(
        jnp.bfloat16
    )
    residuals = lax.all_to_all(
        jnp.broadcast_to(residual[None], (PLANE, rows, out_width)),
        "fsdp",
        0,
        0,
        axis_index_groups=PLANES,
    ).reshape(PLANE * rows, out_width)
    gradients = lax.dot_general(
        columns, residuals, (((0,), (0,)), ((), ())), preferred_element_type=jnp.float32
    )
    own, to_before, to_after, far = jnp.split(gradients, SLABS, axis=0)
    far = far.astype(jnp.bfloat16)
    passing_up = shift_z(far[:half], 1).astype(jnp.float32)
    passing_down = shift_z(far[half:], -1).astype(jnp.float32)
    up = jnp.concatenate([to_after[:half] + passing_up, to_after[half:]], axis=0)
    down = jnp.concatenate([to_before[:half], to_before[half:] + passing_down], axis=0)
    from_before = shift_z(up.astype(jnp.bfloat16), 1)
    from_after = shift_z(down.astype(jnp.bfloat16), -1)
    gradient = own + (from_before.astype(jnp.float32) + from_after.astype(jnp.float32))

    weight_f = initial.astype(jnp.float32)
    first_new = BETA_FIRST * first_moment[0] + (1.0 - BETA_FIRST) * gradient
    second_new = BETA_SECOND * second_moment[0] + (1.0 - BETA_SECOND) * gradient * gradient
    moved = weight_f - INNER_RATE * (
        first_new / (jnp.sqrt(second_new) + EPSILON) + WEIGHT_DECAY * weight_f
    )
    inner_weight = moved.astype(jnp.bfloat16)
    mixed = ((1.0 - MIXING) * block_anchor + MIXING * inner_weight.astype(jnp.float32)).astype(
        jnp.bfloat16
    )
    return (mixed[None], first_new[None], new_anchor, new_momentum)


def solution(mesh):
    return jax.shard_map(
        shards,
        mesh=mesh,
        in_specs=(
            P("replica", "fsdp", None),
            P("replica", "fsdp", None),
            P("replica", "fsdp", None),
            P(("fsdp", "replica"), None),
            P(("fsdp", "replica"), None),
            P("replica", "fsdp", None),
            P("replica", "fsdp", None),
            P("replica", "fsdp"),
        ),
        out_specs=(
            P("replica", "fsdp", None),
            P("replica", "fsdp", None),
            P(("fsdp", "replica"), None),
            P(("fsdp", "replica"), None),
        ),
        check_vma=False,
    )
```

time: 368 us -> 194 us (0.53)
  the two profiles are of different devices: /device:TPU:1 before, /device:TPU:65 now
where the time goes in v1:
time: 194 us; the launch traced here: 193 us
  waiting for transfers between devices  83.6 us (43%)
  starting transfers between devices  72.7 us (37%)
  blocking collectives  20 us (10%)
  Pallas kernels  6.76 us (3%)
  other arithmetic  4.18 us (2%)
  matrix products  2.5 us (1%)
  local copies, waits for them, and re-layouts  2.36 us (1%)
    ppermute x8, waiting for transfers between devices, shift_z(): return lax.ppermute(value, 'fsdp', pairs)  60.4 us
    ppermute x8, starting transfers between devices, shift_z(): return lax.ppermute(value, 'fsdp', pairs)  40.4 us
    all_to_all x1, blocking collectives, shards(): lax.all_to_all(partials.reshape(PLANE, rows, out_width), 'fsdp', 0, 0, ax...  20 us
    all_to_all x1, starting transfers between devices, shards(): lax.all_to_all(initial.reshape(workers, share_rows, out_width), 'replica'...  17.8 us
    all_to_all x1, waiting for transfers between devices, shards(): lax.all_to_all(jnp.broadcast_to(residual[None], (PLANE, rows, out_width))...  14.4 us
    all_to_all x1, waiting for transfers between devices, shards(): lax.all_to_all(initial.reshape(workers, share_rows, out_width), 'replica'...  8.72 us
    all_to_all x1, starting transfers between devices, shards(): lax.all_to_all(jnp.broadcast_to(new_anchor[None], (workers, share_rows, o...  4.99 us
    all_to_all x1, starting transfers between devices, shards(): columns = lax.all_to_all(packed, 'fsdp', 0, 0, axis_index_groups=PLANES)  4.97 us
  transfers between devices with their start and end apart: 12, of which 8 were waited for; matrix products, arithmetic and copies ran while one was open for 2% of the time, Pallas kernels for 0%

profile of v1, /device:TPU:65, one launch (start us, length us, event | category | flops | bytes accessed | tf_op | source)
XLA Modules:
  0.0 193.1 jit_solution(13371894111616587640)
XLA Ops:
  0.7 0.7 pad_add_fusion.slab_ref
  1.4 4.6 %pack_columns.1 = bf16[8,128,1024]{2,1,0:T(8,128)(2,1)} custom-call(s32[4]{0:T(128)} %pad_add_fusion.slab_ref, bf16[128,8192]{1,0:T(8,128)(2,1)} %bitcast.51), custom_call_target="tpu_custom_call" | custom-call | tf_op jit(solution)/shard_map/pack_columns/pallas_call | solution.py:39
  5.9 5.0 %all-to-all-start.2 = ((bf16[8,128,1024]{2,1,0:T(8,128)(2,1)}), bf16[8,128,1024]{2,1,0:T(8,128)(2,1)S(1)}, u32[]{:S(2)}, u32[]{:S(2)}) async-start(bf16[8,128,1024]{2,1,0:T(8,128)(2,1)} %pack_columns.1), calls=%async_computation.2 | async-start | bytes 4194304 | tf_op jit(solution)/shard_map/all_to_all | solution.py:95
  10.9 8.8 %collective-permute-start = (bf16[256,512]{1,0:T(8,128)(2,1)}, bf16[256,512]{1,0:T(8,128)(2,1)S(1)}, u32[]{:S(2)}, u32[]{:S(2)}) collective-permute-start(bf16[256,512]{1,0:T(8,128)(2,1)} %bitcast.2.w0_ref), channel_id=1, source_target_pairs={{0,8},{1,9},{2,10},{3,11},{4,12},{5,13},{6,14},{7,15},{8,16},{9,17... | collective-permute-start | bytes 786440 | tf_op jit(solution)/shard_map/ppermute | solution.py:28
  19.7 3.8 %collective-permute-start.1 = (bf16[256,512]{1,0:T(8,128)(2,1)}, bf16[256,512]{1,0:T(8,128)(2,1)S(1)}, u32[]{:S(2)}, u32[]{:S(2)}) collective-permute-start(bf16[256,512]{1,0:T(8,128)(2,1)} %bitcast.2.w0_ref), channel_id=1, source_target_pairs={{0,24},{1,25},{2,26},{3,27},{4,28},{5,29},{6,30},{7,31},{8,0},{9,1... | collective-permute-start | bytes 786440 | tf_op jit(solution)/shard_map/ppermute | solution.py:28
  23.5 18.7 %collective-permute-done.w1_ref = bf16[256,512]{1,0:T(8,128)(2,1)S(1)} collective-permute-done((bf16[256,512]{1,0:T(8,128)(2,1)}, bf16[256,512]{1,0:T(8,128)(2,1)S(1)}, u32[]{:S(2)}, u32[]{:S(2)}) %collective-permute-start) | collective-permute-done | bytes 262176 | tf_op jit(solution)/shard_map/ppermute | solution.py:28
  42.2 4.6 %collective-permute-start.2 = (bf16[128,512]{1,0:T(8,128)(2,1)S(1)}, bf16[128,512]{1,0:T(8,128)(2,1)S(1)}, u32[]{:S(2)}, u32[]{:S(2)}) collective-permute-start(bf16[128,512]{1,0:T(8,128)(2,1)S(1)} %slice.40), channel_id=1, source_target_pairs={{0,8},{1,9},{2,10},{3,11},{4,12},{5,13},{6,14},{7,15},{8,16},{9,17... | collective-permute-start | bytes 393224 | tf_op jit(solution)/shard_map/ppermute | solution.py:28
  46.8 0.0 collective-permute-done.1.w2_ref
  46.8 4.6 %collective-permute-start.3 = (bf16[128,512]{1,0:T(8,128)(2,1)S(1)}, bf16[128,512]{1,0:T(8,128)(2,1)S(1)}, u32[]{:S(2)}, u32[]{:S(2)}) collective-permute-start(bf16[128,512]{1,0:T(8,128)(2,1)S(1)} %slice.41), channel_id=1, source_target_pairs={{0,24},{1,25},{2,26},{3,27},{4,28},{5,29},{6,30},{7,31},{8,0},{9,1... | collective-permute-start | bytes 393224 | tf_op jit(solution)/shard_map/ppermute | solution.py:28
  51.5 7.1 %collective-permute-done.2 = bf16[128,512]{1,0:T(8,128)(2,1)S(1)} collective-permute-done((bf16[128,512]{1,0:T(8,128)(2,1)S(1)}, bf16[128,512]{1,0:T(8,128)(2,1)S(1)}, u32[]{:S(2)}, u32[]{:S(2)}) %collective-permute-start.2) | collective-permute-done | bytes 131104 | tf_op jit(solution)/shard_map/ppermute | solution.py:28
  58.5 0.0 collective-permute-done.3
  58.6 0.0 all-to-all-done.2
  58.6 2.2 %project.1 = bf16[1024,512]{1,0:T(8,128)(2,1)S(1)} custom-call(bf16[1024,1024]{1,0:T(8,128)(2,1)S(1)} %bitcast.49, bf16[256,512]{1,0:T(8,128)(2,1)} %bitcast.2.w0_ref, bf16[256,512]{1,0:T(8,128)(2,1)S(1)} %collective-permute-done.w1_ref, bf16[256,512]{1,0:T(8,128)(2,1)S(1)} %collective-permute-done.1.w2_ref, bf16[256,512]{1,0:T(8,128)(2,1)S(1)} %pad_maximum_fusion.w3_ref), custom_call_target="tpu_custom_call" | custom-call | tf_op jit(solution)/shard_map/project/pallas_call | solution.py:67
  60.8 0.0 copy-start.8
  60.8 0.0 copy-start.4
  60.8 20.0 %all_to_all.25 = bf16[8,128,512]{2,1,0:T(8,128)(2,1)S(1)} all-to-all(bf16[8,128,512]{2,1,0:T(8,128)(2,1)S(1)} %bitcast.50), channel_id=1, replica_groups={{0,1,2,3,4,5,6,7},{8,9,10,11,12,13,14,15},{16,17,18,19,20,21,22,23},{24..., dimensions={0} | all-to-all | bytes 2097152 | tf_op jit(solution)/shard_map/all_to_all | solution.py:111
  80.8 17.8 %all-to-all-start = ((bf16[16,16,512]{2,1,0:T(8,128)(2,1)}), bf16[16,16,512]{2,1,0:T(8,128)(2,1)S(1)}, u32[]{:S(2)}, u32[]{:S(2)}) async-start(bf16[16,16,512]{2,1,0:T(8,128)(2,1)} %bitcast), calls=%async_computation | async-start | bytes 524288 | tf_op jit(solution)/shard_map/all_to_all | solution.py:99
  98.6 0.0 copy-done.8
  98.6 0.1 convert_reduce_fusion
  98.8 0.0 copy-done.4
  98.8 0.1 fusion.15
  98.9 0.0 copy-start.6
  98.9 0.0 copy-start.7
  98.9 8.7 %all-to-all-done = bf16[16,16,512]{2,1,0:T(8,128)(2,1)S(1)} async-done(((bf16[16,16,512]{2,1,0:T(8,128)(2,1)}), bf16[16,16,512]{2,1,0:T(8,128)(2,1)S(1)}, u32[]{:S(2)}, u32[]{:S(2)}) %all-to-all-start) | async-done | bytes 262176 | tf_op jit(solution)/shard_map/all_to_all | solution.py:99
  107.6 1.1 broadcast_in_dim.23
  108.7 4.6 %all-to-all-start.4 = ((bf16[8,128,512]{2,1,0:T(8,128)(2,1)}), bf16[8,128,512]{2,1,0:T(8,128)(2,1)S(1)}, u32[]{:S(2)}, u32[]{:S(2)}) async-start(bf16[8,128,512]{2,1,0:T(8,128)(2,1)} %broadcast_in_dim.23), calls=%async_computation.4 | async-start | bytes 2097152 | tf_op jit(solution)/shard_map/all_to_all | solution.py:118
  113.3 0.0 copy-done.6
  113.3 0.0 copy-done.7
  113.4 0.6 multiply_subtract_fusion
  114.0 0.0 copy-start.5
  114.0 14.4 %all-to-all-done.4 = bf16[8,128,512]{2,1,0:T(8,128)(2,1)S(1)} async-done(((bf16[8,128,512]{2,1,0:T(8,128)(2,1)}), bf16[8,128,512]{2,1,0:T(8,128)(2,1)S(1)}, u32[]{:S(2)}, u32[]{:S(2)}) %all-to-all-start.4) | async-done | bytes 1048608 | tf_op jit(solution)/shard_map/all_to_all | solution.py:118
  128.4 0.0 copy-start
  128.4 0.9 broadcast_in_dim.10
  129.3 0.2 copy-done
  129.6 5.0 %all-to-all-start.1 = ((f32[16,16,512]{2,1,0:T(8,128)}), f32[16,16,512]{2,1,0:T(8,128)S(1)}, u32[]{:S(2)}, u32[]{:S(2)}) async-start(f32[16,16,512]{2,1,0:T(8,128)} %broadcast_in_dim.10), calls=%async_computation.1 | async-start | bytes 1048576 | tf_op jit(solution)/shard_map/all_to_all | solution.py:106
  134.6 2.5 %fusion.17 = (bf16[1024,512]{1,0:T(8,128)(2,1)S(1)}, f32[1024,512]{1,0:T(8,128)S(1)}) fusion(bf16[8,128,1024]{2,1,0:T(8,128)(2,1)S(1)} %all-to-all-done.2, bf16[8,128,512]{2,1,0:T(8,128)(2,1)} %copy-done), kind=kOutput, calls=%fused_computation.37 | convolution fusion | flops 1074266112 | bytes 6291456 | tf_op jit(solution)/shard_map/dot_general | solution.py:125
  137.1 0.0 copy-done.5
  137.1 0.0 copy-start.3
  137.1 0.0 copy-start.1
  137.1 0.0 copy-start.2
  137.2 4.6 %collective-permute-start.4 = (bf16[128,512]{1,0:T(8,128)(2,1)S(1)}, bf16[128,512]{1,0:T(8,128)(2,1)S(1)}, u32[]{:S(2)}, u32[]{:S(2)}) collective-permute-start(bf16[128,512]{1,0:T(8,128)(2,1)S(1)} %get-tuple-element.10), channel_id=1, source_target_pairs={{0,8},{1,9},{2,10},{3,11},{4,12},{5,13},{6,14},{7,15},{8,16},{9,17... | collective-permute-start | bytes 393224 | tf_op jit(solution)/shard_map/ppermute | solution.py:28
  141.8 4.9 %collective-permute-start.6 = (bf16[128,512]{1,0:T(8,128)(2,1)S(1)}, bf16[128,512]{1,0:T(8,128)(2,1)S(1)}, u32[]{:S(2)}, u32[]{:S(2)}) collective-permute-start(bf16[128,512]{1,0:T(8,128)(2,1)S(1)} %get-tuple-element.11), channel_id=1, source_target_pairs={{0,24},{1,25},{2,26},{3,27},{4,28},{5,29},{6,30},{7,31},{8,0},{9,1... | collective-permute-start | bytes 393224 | tf_op jit(solution)/shard_map/ppermute | solution.py:28
  146.7 8.2 %collective-permute-done.4 = bf16[128,512]{1,0:T(8,128)(2,1)S(1)} collective-permute-done((bf16[128,512]{1,0:T(8,128)(2,1)S(1)}, bf16[128,512]{1,0:T(8,128)(2,1)S(1)}, u32[]{:S(2)}, u32[]{:S(2)}) %collective-permute-start.4) | collective-permute-done | bytes 131104 | tf_op jit(solution)/shard_map/ppermute | solution.py:28
  154.9 5.7 %collective-permute-done.6 = bf16[128,512]{1,0:T(8,128)(2,1)S(1)} collective-permute-done((bf16[128,512]{1,0:T(8,128)(2,1)S(1)}, bf16[128,512]{1,0:T(8,128)(2,1)S(1)}, u32[]{:S(2)}, u32[]{:S(2)}) %collective-permute-start.6) | collective-permute-done | bytes 131104 | tf_op jit(solution)/shard_map/ppermute | solution.py:28
  160.6 0.1 fusion.11
  160.7 1.9 collective-permute-start.5
  162.6 0.0 copy-done.3
  162.7 7.3 %collective-permute-start.7 = (bf16[256,512]{1,0:T(8,128)(2,1)S(1)}, bf16[256,512]{1,0:T(8,128)(2,1)S(1)}, u32[]{:S(2)}, u32[]{:S(2)}) collective-permute-start(bf16[256,512]{1,0:T(8,128)(2,1)S(1)} %pad_maximum_fusion.2), channel_id=1, source_target_pairs={{0,24},{1,25},{2,26},{3,27},{4,28},{5,29},{6,30},{7,31},{8,0},{9,1... | collective-permute-start | bytes 786440 | tf_op jit(solution)/shard_map/ppermute | solution.py:28
  169.9 0.0 all-to-all-done.1
  169.9 11.5 %collective-permute-done.5 = bf16[256,512]{1,0:T(8,128)(2,1)S(1)} collective-permute-done((bf16[256,512]{1,0:T(8,128)(2,1)S(1)}, bf16[256,512]{1,0:T(8,128)(2,1)S(1)}, u32[]{:S(2)}, u32[]{:S(2)}) %collective-permute-start.5) | collective-permute-done | bytes 262176 | tf_op jit(solution)/shard_map/ppermute | solution.py:28
  181.4 9.2 %collective-permute-done.7 = bf16[256,512]{1,0:T(8,128)(2,1)S(1)} collective-permute-done((bf16[256,512]{1,0:T(8,128)(2,1)S(1)}, bf16[256,512]{1,0:T(8,128)(2,1)S(1)}, u32[]{:S(2)}, u32[]{:S(2)}) %collective-permute-start.7) | collective-permute-done | bytes 262176 | tf_op jit(solution)/shard_map/ppermute | solution.py:28
  190.6 0.0 copy-done.1
  190.6 0.0 copy-done.2
  190.6 2.5 %fusion.9 = (f32[1,256,512]{2,1,0:T(8,128)}, bf16[256,512]{1,0:T(8,128)(2,1)}) fusion(f32[1,256,512]{2,1,0:T(8,128)S(1)} %copy-done.1, bf16[256,512]{1,0:T(8,128)(2,1)S(1)} %collective-permute-done.7, bf16[256,512]{1,0:T(8,128)(2,1)S(1)} %collective-permute-done.5, f32[1024,512]{1,0:T(8,128)} %copy-done.3, f32[1,256,512]{2,1,0:T(8,128)S(1)} %copy-done.2, ...), kind=kLoop, calls=%fused_computation.18 | loop fusion | flops 3014656 | bytes 3670016 | tf_op jit(solution)/shard_map/broadcast_in_dim | solution.py:148
  (8 shorter events, 0.2 us)
Async XLA Ops:
  5.9 52.6 %all-to-all-start.2 = ((bf16[8,128,1024]{2,1,0:T(8,128)(2,1)}), bf16[8,128,1024]{2,1,0:T(8,128)(2,1)S(1)}, u32[]{:S(2)}, u32[]{:S(2)}) async-start(bf16[8,128,1024]{2,1,0:T(8,128)(2,1)} %pack_columns.1), calls=%async_computation.2 | async-start | bytes 4194304 | tf_op jit(solution)/shard_map/all_to_all | solution.py:95
  10.9 31.3 %collective-permute-start = (bf16[256,512]{1,0:T(8,128)(2,1)}, bf16[256,512]{1,0:T(8,128)(2,1)S(1)}, u32[]{:S(2)}, u32[]{:S(2)}) collective-permute-start(bf16[256,512]{1,0:T(8,128)(2,1)} %bitcast.2.w0_ref), channel_id=1, source_target_pairs={{0,8},{1,9},{2,10},{3,11},{4,12},{5,13},{6,14},{7,15},{8,16},{9,17... | collective-permute-start | bytes 786440 | tf_op jit(solution)/shard_map/ppermute | solution.py:28
  19.7 27.1 %collective-permute-start.1 = (bf16[256,512]{1,0:T(8,128)(2,1)}, bf16[256,512]{1,0:T(8,128)(2,1)S(1)}, u32[]{:S(2)}, u32[]{:S(2)}) collective-permute-start(bf16[256,512]{1,0:T(8,128)(2,1)} %bitcast.2.w0_ref), channel_id=1, source_target_pairs={{0,24},{1,25},{2,26},{3,27},{4,28},{5,29},{6,30},{7,31},{8,0},{9,1... | collective-permute-start | bytes 786440 | tf_op jit(solution)/shard_map/ppermute | solution.py:28
  42.2 16.3 %collective-permute-start.2 = (bf16[128,512]{1,0:T(8,128)(2,1)S(1)}, bf16[128,512]{1,0:T(8,128)(2,1)S(1)}, u32[]{:S(2)}, u32[]{:S(2)}) collective-permute-start(bf16[128,512]{1,0:T(8,128)(2,1)S(1)} %slice.40), channel_id=1, source_target_pairs={{0,8},{1,9},{2,10},{3,11},{4,12},{5,13},{6,14},{7,15},{8,16},{9,17... | collective-permute-start | bytes 393224 | tf_op jit(solution)/shard_map/ppermute | solution.py:28
  46.8 11.7 %collective-permute-start.3 = (bf16[128,512]{1,0:T(8,128)(2,1)S(1)}, bf16[128,512]{1,0:T(8,128)(2,1)S(1)}, u32[]{:S(2)}, u32[]{:S(2)}) collective-permute-start(bf16[128,512]{1,0:T(8,128)(2,1)S(1)} %slice.41), channel_id=1, source_target_pairs={{0,24},{1,25},{2,26},{3,27},{4,28},{5,29},{6,30},{7,31},{8,0},{9,1... | collective-permute-start | bytes 393224 | tf_op jit(solution)/shard_map/ppermute | solution.py:28
  60.8 37.8 %copy-start.8 = (s32[1,128]{1,0:T(1,128)S(1)}, s32[1,128]{1,0:T(1,128)}, u32[]{:S(2)}) copy-start(s32[1,128]{1,0:T(1,128)} %param.15) | copy-start | bytes 1540
  60.8 38.0 %copy-start.4 = (bf16[1,128,512]{2,1,0:T(8,128)(2,1)S(1)}, bf16[1,128,512]{2,1,0:T(8,128)(2,1)}, u32[]{:S(2)}) copy-start(bf16[1,128,512]{2,1,0:T(8,128)(2,1)} %param.14) | copy-start | bytes 393220
  80.8 26.8 %all-to-all-start = ((bf16[16,16,512]{2,1,0:T(8,128)(2,1)}), bf16[16,16,512]{2,1,0:T(8,128)(2,1)S(1)}, u32[]{:S(2)}, u32[]{:S(2)}) async-start(bf16[16,16,512]{2,1,0:T(8,128)(2,1)} %bitcast), calls=%async_computation | async-start | bytes 524288 | tf_op jit(solution)/shard_map/all_to_all | solution.py:99
  98.9 14.5 %copy-start.6 = (f32[16,512]{1,0:T(8,128)S(1)}, f32[16,512]{1,0:T(8,128)}, u32[]{:S(2)}) copy-start(f32[16,512]{1,0:T(8,128)} %param.11) | copy-start | bytes 98308
  98.9 14.5 %copy-start.7 = (f32[16,512]{1,0:T(8,128)S(1)}, f32[16,512]{1,0:T(8,128)}, u32[]{:S(2)}) copy-start(f32[16,512]{1,0:T(8,128)} %param.12) | copy-start | bytes 98308
  108.7 19.7 %all-to-all-start.4 = ((bf16[8,128,512]{2,1,0:T(8,128)(2,1)}), bf16[8,128,512]{2,1,0:T(8,128)(2,1)S(1)}, u32[]{:S(2)}, u32[]{:S(2)}) async-start(bf16[8,128,512]{2,1,0:T(8,128)(2,1)} %broadcast_in_dim.23), calls=%async_computation.4 | async-start | bytes 2097152 | tf_op jit(solution)/shard_map/all_to_all | solution.py:118
  114.0 23.1 %copy-start.5 = (f32[16,512]{1,0:T(8,128)}, f32[16,512]{1,0:T(8,128)S(1)}, u32[]{:S(2)}) copy-start(f32[16,512]{1,0:T(8,128)S(1)} %get-tuple-element.4) | copy-start | bytes 98308
  128.4 1.2 copy-start
  129.6 40.3 %all-to-all-start.1 = ((f32[16,16,512]{2,1,0:T(8,128)}), f32[16,16,512]{2,1,0:T(8,128)S(1)}, u32[]{:S(2)}, u32[]{:S(2)}) async-start(f32[16,16,512]{2,1,0:T(8,128)} %broadcast_in_dim.10), calls=%async_computation.1 | async-start | bytes 1048576 | tf_op jit(solution)/shard_map/all_to_all | solution.py:106
  137.1 25.5 %copy-start.3 = (f32[1024,512]{1,0:T(8,128)}, f32[1024,512]{1,0:T(8,128)S(1)}, u32[]{:S(2)}) copy-start(f32[1024,512]{1,0:T(8,128)S(1)} %get-tuple-element.15) | copy-start | bytes 6291460
  137.1 53.5 %copy-start.1 = (f32[1,256,512]{2,1,0:T(8,128)S(1)}, f32[1,256,512]{2,1,0:T(8,128)}, u32[]{:S(2)}) copy-start(f32[1,256,512]{2,1,0:T(8,128)} %param.9) | copy-start | bytes 1572868
  137.1 53.5 %copy-start.2 = (f32[1,256,512]{2,1,0:T(8,128)S(1)}, f32[1,256,512]{2,1,0:T(8,128)}, u32[]{:S(2)}) copy-start(f32[1,256,512]{2,1,0:T(8,128)} %param.10) | copy-start | bytes 1572868
  137.2 17.7 %collective-permute-start.4 = (bf16[128,512]{1,0:T(8,128)(2,1)S(1)}, bf16[128,512]{1,0:T(8,128)(2,1)S(1)}, u32[]{:S(2)}, u32[]{:S(2)}) collective-permute-start(bf16[128,512]{1,0:T(8,128)(2,1)S(1)} %get-tuple-element.10), channel_id=1, source_target_pairs={{0,8},{1,9},{2,10},{3,11},{4,12},{5,13},{6,14},{7,15},{8,16},{9,17... | collective-permute-start | bytes 393224 | tf_op jit(solution)/shard_map/ppermute | solution.py:28
  141.8 18.8 %collective-permute-start.6 = (bf16[128,512]{1,0:T(8,128)(2,1)S(1)}, bf16[128,512]{1,0:T(8,128)(2,1)S(1)}, u32[]{:S(2)}, u32[]{:S(2)}) collective-permute-start(bf16[128,512]{1,0:T(8,128)(2,1)S(1)} %get-tuple-element.11), channel_id=1, source_target_pairs={{0,24},{1,25},{2,26},{3,27},{4,28},{5,29},{6,30},{7,31},{8,0},{9,1... | collective-permute-start | bytes 393224 | tf_op jit(solution)/shard_map/ppermute | solution.py:28
  160.7 20.7 %collective-permute-start.5 = (bf16[256,512]{1,0:T(8,128)(2,1)S(1)}, bf16[256,512]{1,0:T(8,128)(2,1)S(1)}, u32[]{:S(2)}, u32[]{:S(2)}) collective-permute-start(bf16[256,512]{1,0:T(8,128)(2,1)S(1)} %pad_maximum_fusion.1), channel_id=1, source_target_pairs={{0,8},{1,9},{2,10},{3,11},{4,12},{5,13},{6,14},{7,15},{8,16},{9,17... | collective-permute-start | bytes 786440 | tf_op jit(solution)/shard_map/ppermute | solution.py:28
  162.7 28.0 %collective-permute-start.7 = (bf16[256,512]{1,0:T(8,128)(2,1)S(1)}, bf16[256,512]{1,0:T(8,128)(2,1)S(1)}, u32[]{:S(2)}, u32[]{:S(2)}) collective-permute-start(bf16[256,512]{1,0:T(8,128)(2,1)S(1)} %pad_maximum_fusion.2), channel_id=1, source_target_pairs={{0,24},{1,25},{2,26},{3,27},{4,28},{5,29},{6,30},{7,31},{8,0},{9,1... | collective-permute-start | bytes 786440 | tf_op jit(solution)/shard_map/ppermute | solution.py:28

commit v2 on v0

v2 whole, which is shorter than its diff:
```python
import functools

import jax
import jax.numpy as jnp
from jax import lax
from jax.experimental import pallas as pl
from jax.experimental.pallas import tpu as pltpu
from jax.sharding import PartitionSpec as P

BETA_FIRST = 0.9
BETA_SECOND = 0.95
EPSILON = 1e-08
INNER_RATE = 0.002
WEIGHT_DECAY = 0.1
OUTER_RATE = 0.7
NESTEROV = 0.9
MIXING = 0.5

SLABS = 4
PLANE = 8
PARTS = 1
PLANES = [[z * PLANE + i for i in range(PLANE)] for z in range(SLABS)]


def shift_z(value, step):
    pairs = [
        (z * PLANE + i, (z + step) % SLABS * PLANE + i)
        for z in range(SLABS)
        for i in range(PLANE)
    ]
    return lax.ppermute(value, "fsdp", pairs)


def shift_replica(value, z_step, y_step):
    pairs = [
        (z * 4 + y, (z + z_step) % 4 * 4 + (y + y_step) % 4) for z in range(4) for y in range(4)
    ]
    return lax.ppermute(value, "replica", pairs)


def pack_kernel(tokens_ref, weights_ref, packed_ref, *refs):
    share_refs, columns_ref, rows_ref, sems = refs[:4], refs[4], refs[5], refs[6]
    slab = lax.axis_index("fsdp") // PLANE
    y = lax.rem(lax.axis_index("replica"), 4)
    width = packed_ref.shape[2] // SLABS
    loads = []
    for k, step in enumerate((0, 3, 1, 2)):
        start = pl.multiple_of(lax.rem(slab + step, SLABS) * (PLANE * width), PLANE * width)
        loads.append(
            pltpu.make_async_copy(
                tokens_ref.at[:, pl.ds(start, PLANE * width)], columns_ref.at[k], sems.at[k]
            )
        )
    loads.append(pltpu.make_async_copy(weights_ref, rows_ref, sems.at[SLABS]))
    for load in loads:
        load.start()
    stores = []
    for k in range(SLABS):
        loads[k].wait()
        for i in range(PLANE):
            stores.append(
                pltpu.make_async_copy(
                    columns_ref.at[k, :, pl.ds(i * width, width)],
                    packed_ref.at[i, :, pl.ds(k * width, width)],
                    sems.at[SLABS + 1],
                )
            )
            stores[-1].start()
    loads[SLABS].wait()
    for step, share_ref in enumerate(share_refs):
        stores.append(
            pltpu.make_async_copy(
                rows_ref.at[:, lax.rem(y + step, 4)], share_ref, sems.at[SLABS + 1]
            )
        )
        stores[-1].start()
    for store in stores:
        store.wait()


def pack(tokens, weights):
    rows, width = tokens.shape[0], weights.shape[0]
    weights = weights.reshape(4, 4, width // 16, weights.shape[1])
    share = jax.ShapeDtypeStruct((4,) + weights.shape[2:], weights.dtype)
    packed, *shares = pl.pallas_call(
        pack_kernel,
        out_shape=[
            jax.ShapeDtypeStruct((PLANE, rows, SLABS * width), tokens.dtype),
            *[share] * 4,
        ],
        in_specs=[pl.BlockSpec(memory_space=pltpu.HBM)] * 2,
        out_specs=[pl.BlockSpec(memory_space=pltpu.HBM)] * 5,
        scratch_shapes=[
            pltpu.VMEM((SLABS, rows, PLANE * width), tokens.dtype),
            pltpu.VMEM(weights.shape, weights.dtype),
            pltpu.SemaphoreType.DMA((SLABS + 2,)),
        ],
        compiler_params=pltpu.CompilerParams(vmem_limit_bytes=16 << 20),
        name="pack_columns",
    )(tokens, weights)
    return packed, shares


def add_kernel(*refs):
    z = lax.axis_index("replica") // 4
    for step in range(4):
        at = lax.rem(z + step, 4)
        total = refs[0][at].astype(jnp.float32)
        for ref in refs[1:4]:
            total += ref[at].astype(jnp.float32)
        refs[4 + step][...] = total


def add_shares(shares):
    return pl.pallas_call(
        add_kernel,
        out_shape=[jax.ShapeDtypeStruct(shares[0].shape[1:], jnp.float32)] * 4,
        name="add_shares",
    )(*shares)


def place_kernel(*refs):
    z, y = lax.axis_index("replica") // 4, lax.rem(lax.axis_index("replica"), 4)
    out_ref = refs[4]
    rows = refs[0].shape[1]
    for y_step in range(4):
        for z_step in range(4):
            at = lax.rem(z + 4 - z_step, 4) * 4 + lax.rem(y + 4 - y_step, 4)
            out_ref[pl.ds(pl.multiple_of(at * rows, rows), rows), :] = refs[y_step][z_step]


def place_shares(shares):
    _, rows, out_width = shares[0].shape
    return pl.pallas_call(
        place_kernel,
        out_shape=jax.ShapeDtypeStruct((16 * rows, out_width), shares[0].dtype),
        name="place_shares",
    )(*shares)


def project_kernel(x_ref, w0_ref, w1_ref, w2_ref, w3_ref, *out_refs):
    width = w0_ref.shape[0]
    part_width = out_refs[0].shape[2]
    for h, out_ref in enumerate(out_refs):
        total = None
        for k, w_ref in enumerate((w0_ref, w1_ref, w2_ref, w3_ref)):
            part = jnp.dot(
                x_ref[:, k * width : (k + 1) * width],
                w_ref[:, h * part_width : (h + 1) * part_width],
                preferred_element_type=jnp.float32,
            )
            total = part if total is None else total + part
        out_ref[...] = total.astype(out_ref.dtype).reshape(out_ref.shape)


def project(columns, pieces):
    shape = (PLANE, columns.shape[0] // PLANE, pieces[0].shape[1] // PARTS)
    return pl.pallas_call(
        project_kernel,
        out_shape=[jax.ShapeDtypeStruct(shape, jnp.bfloat16)] * PARTS,
        compiler_params=pltpu.CompilerParams(vmem_limit_bytes=32 << 20),
        name="project",
    )(columns, *pieces)


def gradient_kernel(slabs, columns_ref, rows_ref, *out_refs):
    width, part_width = out_refs[0].shape
    rows = rows_ref[:, :, :part_width].reshape(columns_ref.shape[0], part_width)
    for k, out_ref in zip(slabs, out_refs):
        total = lax.dot_general(
            columns_ref[:, k * width : (k + 1) * width],
            rows,
            (((0,), (0,)), ((), ())),
            preferred_element_type=jnp.float32,
        )
        out_ref[...] = total.astype(out_ref.dtype)


def gradient_of(columns, residuals, slabs, width, part_width, dtype):
    return pl.pallas_call(
        functools.partial(gradient_kernel, slabs),
        out_shape=[jax.ShapeDtypeStruct((width, part_width), dtype)] * len(slabs),
        compiler_params=pltpu.CompilerParams(vmem_limit_bytes=32 << 20),
        name="gradient",
    )(columns, residuals)


def to_plane(value):
    return lax.all_to_all(value, "fsdp", 0, 0, axis_index_groups=PLANES)


def scatter_z(blocks):
    own, to_before, to_after, far = blocks
    half = own.shape[0] // 2
    passing_up = shift_z(far[:half], 1).astype(jnp.float32)
    passing_down = shift_z(far[half:], -1).astype(jnp.float32)
    up = jnp.concatenate([to_after[:half] + passing_up, to_after[half:]], axis=0)
    down = jnp.concatenate([to_before[:half], to_before[half:] + passing_down], axis=0)
    from_before = shift_z(up.astype(jnp.bfloat16), 1)
    from_after = shift_z(down.astype(jnp.bfloat16), -1)
    return own + (from_before.astype(jnp.float32) + from_after.astype(jnp.float32))


def shards(weights, first_moment, second_moment, anchor, momentum, inputs, targets, keep_mask):
    initial = weights[0]
    tokens = inputs[0]
    goal_rows = targets[0]
    mask_rows = keep_mask[0].astype(jnp.float32)[:, None]
    rows = tokens.shape[0]
    width, out_width = initial.shape
    token_count = rows * lax.axis_size("fsdp")
    workers = lax.axis_size("replica")
    half = width // 2

    packed, shares = pack(tokens, initial)
    columns = to_plane(packed).reshape(PLANE * rows, SLABS * width)
    shares[1:] = [shift_replica(shares[i], 0, i) for i in (1, 2, 3)]
    sums = add_shares(shares)

    before, after = shift_z(initial, 1), shift_z(initial, -1)
    before, after, *sums = lax.optimization_barrier((before, after, *sums))
    opposite = jnp.concatenate(
        [shift_z(before[:half], 1), shift_z(after[half:], -1)], axis=0
    )
    partials = list(project(columns, (initial, before, after, opposite)))

    partials[0], *sums = lax.optimization_barrier((partials[0], *sums))
    sums[1:] = [shift_replica(sums[i], i, 0) for i in (1, 2, 3)]
    weight_mean = (sums[0] + sums[1] + sums[2] + sums[3]) / workers
    pseudo_grad = anchor - weight_mean
    new_momentum = NESTEROV * momentum + pseudo_grad
    new_anchor = anchor - OUTER_RATE * (pseudo_grad + NESTEROV * new_momentum)

    part_width = out_width // PARTS

    def residual_of(mine, h):
        goal = goal_rows[:, h * part_width : (h + 1) * part_width].astype(jnp.float32)
        projected = jnp.sum(mine.astype(jnp.float32), 0)
        residual = ((projected - goal) * mask_rows / token_count).astype(jnp.bfloat16)
        return jnp.broadcast_to(residual[None], mine.shape)

    received = to_plane(partials[0])
    gradient = []
    for h in range(PARTS):
        out = residual_of(received[:, :, -part_width:], h)
        if h + 1 < PARTS:
            out = jnp.concatenate([out, partials[h + 1]], axis=2)
        if h == 0:
            out, shared = lax.optimization_barrier((out, new_anchor))
            shared = [shared] + [shift_replica(shared, i, 0) for i in (1, 2, 3)]
        received = to_plane(out)
        if h == 0:
            received, *shared = lax.optimization_barrier((received, *shared))
        (far,) = gradient_of(columns, received, (3,), width, part_width, jnp.bfloat16)
        near = gradient_of(columns, received, (0, 1, 2), width, part_width, jnp.float32)
        gradient.append(scatter_z((*near, far)))
    gradient = jnp.concatenate(gradient, axis=1)
    shared = jnp.stack(shared)
    block_anchor = place_shares(
        [shared] + [shift_replica(shared, 0, i) for i in (1, 2, 3)]
    )

    weight_f = initial.astype(jnp.float32)
    first_new = BETA_FIRST * first_moment[0] + (1.0 - BETA_FIRST) * gradient
    second_new = BETA_SECOND * second_moment[0] + (1.0 - BETA_SECOND) * gradient * gradient
    moved = weight_f - INNER_RATE * (
        first_new / (jnp.sqrt(second_new) + EPSILON) + WEIGHT_DECAY * weight_f
    )
    inner_weight = moved.astype(jnp.bfloat16)
    mixed = ((1.0 - MIXING) * block_anchor + MIXING * inner_weight.astype(jnp.float32)).astype(
        jnp.bfloat16
    )
    return (mixed[None], first_new[None], new_anchor, new_momentum)


def solution(mesh):
    return jax.shard_map(
        shards,
        mesh=mesh,
        in_specs=(
            P("replica", "fsdp", None),
            P("replica", "fsdp", None),
            P("replica", "fsdp", None),
            P(("fsdp", "replica"), None),
            P(("fsdp", "replica"), None),
            P("replica", "fsdp", None),
            P("replica", "fsdp", None),
            P("replica", "fsdp"),
        ),
        out_specs=(
            P("replica", "fsdp", None),
            P("replica", "fsdp", None),
            P(("fsdp", "replica"), None),
            P(("fsdp", "replica"), None),
        ),
        check_vma=False,
    )
```

time: 368 us -> 171 us (0.46)
  the two profiles are of different devices: /device:TPU:1 before, /device:TPU:33 now
where the time goes in v2:
time: 171 us; the launch traced here: 170 us
  starting transfers between devices  100 us (58%)
  waiting for transfers between devices  49.1 us (29%)
  Pallas kernels  7.94 us (5%)
  local copies, waits for them, and re-layouts  7.76 us (5%)
  other arithmetic  4.2 us (2%)
    ppermute x12, starting transfers between devices, shift_replica(): return lax.ppermute(value, 'replica', pairs)  42 us
    ppermute x8, starting transfers between devices, shift_z(): return lax.ppermute(value, 'fsdp', pairs)  38.7 us
    ppermute x8, waiting for transfers between devices, shift_z(): return lax.ppermute(value, 'fsdp', pairs)  34.4 us
    all_to_all x3, starting transfers between devices, to_plane(): return lax.all_to_all(value, 'fsdp', 0, 0, axis_index_groups=PLANES)  19.5 us
    ppermute x12, waiting for transfers between devices, shift_replica(): return lax.ppermute(value, 'replica', pairs)  11.4 us
    unnamed x38, local copies, waits for them, and re-layouts  6.59 us
  transfers between devices with their start and end apart: 23, of which 13 were waited for; matrix products, arithmetic and copies ran while one was open for 1% of the time, Pallas kernels for 3%

profile of v2, /device:TPU:33, one launch (start us, length us, event | category | flops | bytes accessed | tf_op | source)
XLA Modules:
  0.0 170.2 jit_solution(9120228969861835901)
XLA Ops:
  0.6 0.0 copy-start
  0.6 0.9 copy-done
  1.6 1.6 copy-done.2
  3.2 0.6 pack_columns.1
  3.8 1.3 copy-done.3
  5.2 0.6 copy-done.6
  5.8 5.1 %all-to-all-start = ((bf16[8,128,1024]{2,1,0:T(8,128)(2,1)}), bf16[8,128,1024]{2,1,0:T(8,128)(2,1)S(1)}, u32[]{:S(2)}, u32[]{:S(2)}) async-start(bf16[8,128,1024]{2,1,0:T(8,128)(2,1)} %copy-done.3), calls=%async_computation | async-start | bytes 4194304 | tf_op jit(solution)/shard_map/all_to_all | solution.py:189
  10.9 8.8 %collective-permute-start = (bf16[256,512]{1,0:T(8,128)(2,1)S(1)}, bf16[256,512]{1,0:T(8,128)(2,1)S(1)}, u32[]{:S(2)}, u32[]{:S(2)}) collective-permute-start(bf16[256,512]{1,0:T(8,128)(2,1)S(1)} %bitcast.43), channel_id=1, source_target_pairs={{0,8},{1,9},{2,10},{3,11},{4,12},{5,13},{6,14},{7,15},{8,16},{9,17... | collective-permute-start | bytes 786440 | tf_op jit(solution)/shard_map/ppermute | solution.py:31
  19.7 4.7 %collective-permute-start.1 = (bf16[256,512]{1,0:T(8,128)(2,1)S(1)}, bf16[256,512]{1,0:T(8,128)(2,1)S(1)}, u32[]{:S(2)}, u32[]{:S(2)}) collective-permute-start(bf16[256,512]{1,0:T(8,128)(2,1)S(1)} %bitcast.44), channel_id=1, source_target_pairs={{0,24},{1,25},{2,26},{3,27},{4,28},{5,29},{6,30},{7,31},{8,0},{9,1... | collective-permute-start | bytes 786440 | tf_op jit(solution)/shard_map/ppermute | solution.py:31
  24.4 3.2 %collective-permute-start.2 = (bf16[4,16,512]{2,1,0:T(8,128)(2,1)S(1)}, bf16[4,16,512]{2,1,0:T(8,128)(2,1)S(1)}, u32[]{:S(2)}, u32[]{:S(2)}) collective-permute-start(bf16[4,16,512]{2,1,0:T(8,128)(2,1)S(1)} %get-tuple-element.36), channel_id=1, source_target_pairs={{0,32},{32,64},{64,96},{96,0},{128,160},{160,192},{192,224},{224,1... | collective-permute-start | bytes 196616 | tf_op jit(solution)/shard_map/ppermute | solution.py:38
  27.6 4.5 %collective-permute-start.3 = (bf16[4,16,512]{2,1,0:T(8,128)(2,1)S(1)}, bf16[4,16,512]{2,1,0:T(8,128)(2,1)S(1)}, u32[]{:S(2)}, u32[]{:S(2)}) collective-permute-start(bf16[4,16,512]{2,1,0:T(8,128)(2,1)S(1)} %get-tuple-element.37), channel_id=1, source_target_pairs={{0,64},{32,96},{64,0},{96,32},{128,192},{160,224},{192,128},{224,1... | collective-permute-start | bytes 196616 | tf_op jit(solution)/shard_map/ppermute | solution.py:38
  32.1 3.0 %collective-permute-start.4 = (bf16[4,16,512]{2,1,0:T(8,128)(2,1)S(1)}, bf16[4,16,512]{2,1,0:T(8,128)(2,1)S(1)}, u32[]{:S(2)}, u32[]{:S(2)}) collective-permute-start(bf16[4,16,512]{2,1,0:T(8,128)(2,1)S(1)} %get-tuple-element.38), channel_id=1, source_target_pairs={{0,96},{32,0},{64,32},{96,64},{128,224},{160,128},{192,160},{224,1... | collective-permute-start | bytes 196616 | tf_op jit(solution)/shard_map/ppermute | solution.py:38
  35.1 0.0 copy-start.15
  35.1 0.0 collective-permute-done.3.refs_2_
  35.2 2.3 %collective-permute-done.4.refs_3_ = bf16[4,16,512]{2,1,0:T(8,128)(2,1)S(1)} collective-permute-done((bf16[4,16,512]{2,1,0:T(8,128)(2,1)S(1)}, bf16[4,16,512]{2,1,0:T(8,128)(2,1)S(1)}, u32[]{:S(2)}, u32[]{:S(2)}) %collective-permute-start.4) | collective-permute-done | bytes 65568 | tf_op jit(solution)/shard_map/ppermute | solution.py:38
  37.4 0.6 copy-done.17
  38.0 1.6 add_shares.1
  39.6 8.1 %collective-permute-done.1.w2_ref = bf16[256,512]{1,0:T(8,128)(2,1)S(1)} collective-permute-done((bf16[256,512]{1,0:T(8,128)(2,1)S(1)}, bf16[256,512]{1,0:T(8,128)(2,1)S(1)}, u32[]{:S(2)}, u32[]{:S(2)}) %collective-permute-start.1) | collective-permute-done | bytes 262176 | tf_op jit(solution)/shard_map/ppermute | solution.py:31
  47.8 4.0 %collective-permute-start.6 = (bf16[128,512]{1,0:T(8,128)(2,1)S(1)}, bf16[128,512]{1,0:T(8,128)(2,1)S(1)}, u32[]{:S(2)}, u32[]{:S(2)}) collective-permute-start(bf16[128,512]{1,0:T(8,128)(2,1)S(1)} %slice.27), channel_id=1, source_target_pairs={{0,24},{1,25},{2,26},{3,27},{4,28},{5,29},{6,30},{7,31},{8,0},{9,1... | collective-permute-start | bytes 393224 | tf_op jit(solution)/shard_map/ppermute | solution.py:31
  51.8 5.2 %collective-permute-start.5 = (bf16[128,512]{1,0:T(8,128)(2,1)S(1)}, bf16[128,512]{1,0:T(8,128)(2,1)S(1)}, u32[]{:S(2)}, u32[]{:S(2)}) collective-permute-start(bf16[128,512]{1,0:T(8,128)(2,1)S(1)} %slice.26), channel_id=1, source_target_pairs={{0,8},{1,9},{2,10},{3,11},{4,12},{5,13},{6,14},{7,15},{8,16},{9,17... | collective-permute-start | bytes 393224 | tf_op jit(solution)/shard_map/ppermute | solution.py:31
  57.0 7.4 %collective-permute-done.6 = bf16[128,512]{1,0:T(8,128)(2,1)S(1)} collective-permute-done((bf16[128,512]{1,0:T(8,128)(2,1)S(1)}, bf16[128,512]{1,0:T(8,128)(2,1)S(1)}, u32[]{:S(2)}, u32[]{:S(2)}) %collective-permute-start.6) | collective-permute-done | bytes 131104 | tf_op jit(solution)/shard_map/ppermute | solution.py:31
  64.4 0.9 collective-permute-done.5
  65.3 2.3 %project.1 = bf16[8,128,512]{2,1,0:T(8,128)(2,1)} custom-call(bf16[1024,1024]{1,0:T(8,128)(2,1)S(1)} %bitcast.39, bf16[256,512]{1,0:T(8,128)(2,1)S(1)} %bitcast.45, bf16[256,512]{1,0:T(8,128)(2,1)S(1)} %collective-permute-done.w1_ref, bf16[256,512]{1,0:T(8,128)(2,1)S(1)} %collective-permute-done.1.w2_ref, bf16[256,512]{1,0:T(8,128)(2,1)S(1)} %pad_maximum_fusion.w3_ref), custom_call_target="tpu_custom_call" | custom-call | tf_op jit(solution)/shard_map/project/pallas_call | solution.py:158
  67.5 10.0 %all-to-all-start.1 = ((bf16[8,128,512]{2,1,0:T(8,128)(2,1)}), bf16[8,128,512]{2,1,0:T(8,128)(2,1)S(1)}, u32[]{:S(2)}, u32[]{:S(2)}) async-start(bf16[8,128,512]{2,1,0:T(8,128)(2,1)} %project.1), calls=%async_computation.1 | async-start | bytes 2097152 | tf_op jit(solution)/shard_map/all_to_all | solution.py:189
  77.6 4.8 %collective-permute-start.9 = (f32[16,512]{1,0:T(8,128)}, f32[16,512]{1,0:T(8,128)S(1)}, u32[]{:S(2)}, u32[]{:S(2)}) collective-permute-start(f32[16,512]{1,0:T(8,128)} %get-tuple-element.53), channel_id=1, source_target_pairs={{0,384},{32,416},{64,448},{96,480},{128,0},{160,32},{192,64},{224,... | collective-permute-start | bytes 98312 | tf_op jit(solution)/shard_map/ppermute | solution.py:38
  82.4 1.9 %collective-permute-start.8 = (f32[16,512]{1,0:T(8,128)}, f32[16,512]{1,0:T(8,128)S(1)}, u32[]{:S(2)}, u32[]{:S(2)}) collective-permute-start(f32[16,512]{1,0:T(8,128)} %get-tuple-element.52), channel_id=1, source_target_pairs={{0,256},{32,288},{64,320},{96,352},{128,384},{160,416},{192,448},{... | collective-permute-start | bytes 98312 | tf_op jit(solution)/shard_map/ppermute | solution.py:38
  84.3 3.1 %collective-permute-start.7 = (f32[16,512]{1,0:T(8,128)}, f32[16,512]{1,0:T(8,128)S(1)}, u32[]{:S(2)}, u32[]{:S(2)}) collective-permute-start(f32[16,512]{1,0:T(8,128)} %get-tuple-element.51), channel_id=1, source_target_pairs={{0,128},{32,160},{64,192},{96,224},{128,256},{160,288},{192,320},{... | collective-permute-start | bytes 98312 | tf_op jit(solution)/shard_map/ppermute | solution.py:38
  87.5 1.0 collective-permute-done.8
  88.5 0.8 collective-permute-done.7
  89.3 1.4 multiply_subtract_fusion
  90.7 2.0 %all-to-all-done.1 = bf16[8,128,512]{2,1,0:T(8,128)(2,1)S(1)} async-done(((bf16[8,128,512]{2,1,0:T(8,128)(2,1)}), bf16[8,128,512]{2,1,0:T(8,128)(2,1)S(1)}, u32[]{:S(2)}, u32[]{:S(2)}) %all-to-all-start.1) | async-done | bytes 1048608 | tf_op jit(solution)/shard_map/all_to_all | solution.py:189
  92.7 0.1 convert_reduce_fusion
  92.8 0.1 fusion.12
  92.9 0.0 copy-start.14
  92.9 1.1 broadcast_in_dim.16
  94.0 4.3 %all-to-all-start.2 = ((bf16[8,128,512]{2,1,0:T(8,128)(2,1)}), bf16[8,128,512]{2,1,0:T(8,128)(2,1)S(1)}, u32[]{:S(2)}, u32[]{:S(2)}) async-start(bf16[8,128,512]{2,1,0:T(8,128)(2,1)} %broadcast_in_dim.16), calls=%async_computation.2 | async-start | bytes 2097152 | tf_op jit(solution)/shard_map/all_to_all | solution.py:189
  98.4 2.9 %collective-permute-start.10 = (f32[16,512]{1,0:T(8,128)S(1)}, f32[16,512]{1,0:T(8,128)S(1)}, u32[]{:S(2)}, u32[]{:S(2)}) collective-permute-start(f32[16,512]{1,0:T(8,128)S(1)} %copy-done.14), channel_id=1, source_target_pairs={{0,128},{32,160},{64,192},{96,224},{128,256},{160,288},{192,320},{... | collective-permute-start | bytes 98312 | tf_op jit(solution)/shard_map/ppermute | solution.py:38
  101.3 5.9 %collective-permute-start.11 = (f32[16,512]{1,0:T(8,128)S(1)}, f32[16,512]{1,0:T(8,128)S(1)}, u32[]{:S(2)}, u32[]{:S(2)}) collective-permute-start(f32[16,512]{1,0:T(8,128)S(1)} %copy-done.14), channel_id=1, source_target_pairs={{0,256},{32,288},{64,320},{96,352},{128,384},{160,416},{192,448},{... | collective-permute-start | bytes 98312 | tf_op jit(solution)/shard_map/ppermute | solution.py:38
  107.2 1.9 %collective-permute-start.12 = (f32[16,512]{1,0:T(8,128)S(1)}, f32[16,512]{1,0:T(8,128)S(1)}, u32[]{:S(2)}, u32[]{:S(2)}) collective-permute-start(f32[16,512]{1,0:T(8,128)S(1)} %copy-done.14), channel_id=1, source_target_pairs={{0,384},{32,416},{64,448},{96,480},{128,0},{160,32},{192,64},{224,... | collective-permute-start | bytes 98312 | tf_op jit(solution)/shard_map/ppermute | solution.py:38
  109.1 0.0 collective-permute-done.10
  109.1 0.0 collective-permute-done.11
  109.1 3.0 %collective-permute-done.12 = f32[16,512]{1,0:T(8,128)S(1)} collective-permute-done((f32[16,512]{1,0:T(8,128)S(1)}, f32[16,512]{1,0:T(8,128)S(1)}, u32[]{:S(2)}, u32[]{:S(2)}) %collective-permute-start.12) | collective-permute-done | bytes 32800 | tf_op jit(solution)/shard_map/ppermute | solution.py:38
  112.1 1.3 all-to-all-done.2.rows_ref
  113.5 0.5 gradient.3
  114.0 6.3 %collective-permute-start.18 = (bf16[128,512]{1,0:T(8,128)(2,1)S(1)}, bf16[128,512]{1,0:T(8,128)(2,1)S(1)}, u32[]{:S(2)}, u32[]{:S(2)}) collective-permute-start(bf16[128,512]{1,0:T(8,128)(2,1)S(1)} %get-tuple-element.69), channel_id=1, source_target_pairs={{0,24},{1,25},{2,26},{3,27},{4,28},{5,29},{6,30},{7,31},{8,0},{9,1... | collective-permute-start | bytes 393224 | tf_op jit(solution)/shard_map/ppermute | solution.py:31
  120.3 1.0 gradient.2
  121.3 0.0 copy-start.4
  121.3 0.8 copy-done.4
  122.2 3.0 %collective-permute-start.16 = (bf16[128,512]{1,0:T(8,128)(2,1)S(1)}, bf16[128,512]{1,0:T(8,128)(2,1)S(1)}, u32[]{:S(2)}, u32[]{:S(2)}) collective-permute-start(bf16[128,512]{1,0:T(8,128)(2,1)S(1)} %get-tuple-element.68), channel_id=1, source_target_pairs={{0,8},{1,9},{2,10},{3,11},{4,12},{5,13},{6,14},{7,15},{8,16},{9,17... | collective-permute-start | bytes 393224 | tf_op jit(solution)/shard_map/ppermute | solution.py:31
  125.2 5.0 %collective-permute-done.18 = bf16[128,512]{1,0:T(8,128)(2,1)S(1)} collective-permute-done((bf16[128,512]{1,0:T(8,128)(2,1)S(1)}, bf16[128,512]{1,0:T(8,128)(2,1)S(1)}, u32[]{:S(2)}, u32[]{:S(2)}) %collective-permute-start.18) | collective-permute-done | bytes 131104 | tf_op jit(solution)/shard_map/ppermute | solution.py:31
  130.3 4.8 %collective-permute-start.19 = (bf16[256,512]{1,0:T(8,128)(2,1)S(1)}, bf16[256,512]{1,0:T(8,128)(2,1)S(1)}, u32[]{:S(2)}, u32[]{:S(2)}) collective-permute-start(bf16[256,512]{1,0:T(8,128)(2,1)S(1)} %pad_maximum_fusion.2), channel_id=1, source_target_pairs={{0,24},{1,25},{2,26},{3,27},{4,28},{5,29},{6,30},{7,31},{8,0},{9,1... | collective-permute-start | bytes 786440 | tf_op jit(solution)/shard_map/ppermute | solution.py:31
  135.0 3.1 %collective-permute-done.16 = bf16[128,512]{1,0:T(8,128)(2,1)S(1)} collective-permute-done((bf16[128,512]{1,0:T(8,128)(2,1)S(1)}, bf16[128,512]{1,0:T(8,128)(2,1)S(1)}, u32[]{:S(2)}, u32[]{:S(2)}) %collective-permute-start.16) | collective-permute-done | bytes 131104 | tf_op jit(solution)/shard_map/ppermute | solution.py:31
  138.2 1.9 %collective-permute-start.17 = (bf16[256,512]{1,0:T(8,128)(2,1)S(1)}, bf16[256,512]{1,0:T(8,128)(2,1)S(1)}, u32[]{:S(2)}, u32[]{:S(2)}) collective-permute-start(bf16[256,512]{1,0:T(8,128)(2,1)S(1)} %pad_maximum_fusion.1), channel_id=1, source_target_pairs={{0,8},{1,9},{2,10},{3,11},{4,12},{5,13},{6,14},{7,15},{8,16},{9,17... | collective-permute-start | bytes 786440 | tf_op jit(solution)/shard_map/ppermute | solution.py:31
  140.2 0.0 copy-start.9
  140.2 3.2 %collective-permute-start.13 = (f32[4,16,512]{2,1,0:T(8,128)S(1)}, f32[4,16,512]{2,1,0:T(8,128)S(1)}, u32[]{:S(2)}, u32[]{:S(2)}) collective-permute-start(f32[4,16,512]{2,1,0:T(8,128)S(1)} %pad_maximum_fusion.3.refs_0_), channel_id=1, source_target_pairs={{0,32},{32,64},{64,96},{96,0},{128,160},{160,192},{192,224},{224,1... | collective-permute-start | bytes 393224 | tf_op jit(solution)/shard_map/ppermute | solution.py:38
  143.4 4.5 %collective-permute-start.14 = (f32[4,16,512]{2,1,0:T(8,128)S(1)}, f32[4,16,512]{2,1,0:T(8,128)S(1)}, u32[]{:S(2)}, u32[]{:S(2)}) collective-permute-start(f32[4,16,512]{2,1,0:T(8,128)S(1)} %pad_maximum_fusion.3.refs_0_), channel_id=1, source_target_pairs={{0,64},{32,96},{64,0},{96,32},{128,192},{160,224},{192,128},{224,1... | collective-permute-start | bytes 393224 | tf_op jit(solution)/shard_map/ppermute | solution.py:38
  147.9 3.0 %collective-permute-start.15 = (f32[4,16,512]{2,1,0:T(8,128)S(1)}, f32[4,16,512]{2,1,0:T(8,128)S(1)}, u32[]{:S(2)}, u32[]{:S(2)}) collective-permute-start(f32[4,16,512]{2,1,0:T(8,128)S(1)} %pad_maximum_fusion.3.refs_0_), channel_id=1, source_target_pairs={{0,96},{32,0},{64,32},{96,64},{128,224},{160,128},{192,160},{224,1... | collective-permute-start | bytes 393224 | tf_op jit(solution)/shard_map/ppermute | solution.py:38
  150.9 0.0 collective-permute-done.14.refs_2_
  150.9 4.2 %collective-permute-done.15.refs_3_ = f32[4,16,512]{2,1,0:T(8,128)S(1)} collective-permute-done((f32[4,16,512]{2,1,0:T(8,128)S(1)}, f32[4,16,512]{2,1,0:T(8,128)S(1)}, u32[]{:S(2)}, u32[]{:S(2)}) %collective-permute-start.15) | collective-permute-done | bytes 131104 | tf_op jit(solution)/shard_map/ppermute | solution.py:38
  155.2 0.6 copy-done.13
  155.8 2.0 %place_shares.1 = f32[256,512]{1,0:T(8,128)} custom-call(f32[4,16,512]{2,1,0:T(8,128)} %copy-done.9, f32[4,16,512]{2,1,0:T(8,128)} %copy-done.11, f32[4,16,512]{2,1,0:T(8,128)} %copy-done.12, f32[4,16,512]{2,1,0:T(8,128)} %copy-done.13), custom_call_target="tpu_custom_call" | custom-call | tf_op jit(solution)/shard_map/place_shares/pallas_call | solution.py:134
  157.8 0.0 collective-permute-done.19
  157.8 10.0 %collective-permute-done.17 = bf16[256,512]{1,0:T(8,128)(2,1)S(1)} collective-permute-done((bf16[256,512]{1,0:T(8,128)(2,1)S(1)}, bf16[256,512]{1,0:T(8,128)(2,1)S(1)}, u32[]{:S(2)}, u32[]{:S(2)}) %collective-permute-start.17) | collective-permute-done | bytes 262176 | tf_op jit(solution)/shard_map/ppermute | solution.py:31
  167.8 2.4 %fusion.7 = (f32[1,256,512]{2,1,0:T(8,128)}, bf16[1,256,512]{2,1,0:T(8,128)(2,1)}) fusion(f32[1,256,512]{2,1,0:T(8,128)S(1)} %copy-done.7, f32[256,512]{1,0:T(8,128)S(1)} %copy-done.5, bf16[256,512]{1,0:T(8,128)(2,1)S(1)} %collective-permute-done.19, bf16[256,512]{1,0:T(8,128)(2,1)S(1)} %collective-permute-done.17, f32[256,512]{1,0:T(8,128)} %place_shares.1, ...), kind=kLoop, calls=%fused_computation.14 | loop fusion | flops 3014656 | bytes 3670016 | tf_op jit(solution)/shard_map/broadcast_in_dim | solution.py:273
  (43 shorter events, 0.3 us)
Async XLA Ops:
  0.6 1.0 copy-start
  1.6 1.6 copy-start.2
  3.8 1.3 copy-start.3
  5.2 0.6 copy-start.6
  5.8 5.1 %copy-start.1 = (bf16[1,256,512]{2,1,0:T(8,128)(2,1)S(1)}, bf16[1,256,512]{2,1,0:T(8,128)(2,1)}, u32[]{:S(2)}) copy-start(bf16[1,256,512]{2,1,0:T(8,128)(2,1)} %param.8) | copy-start | bytes 786436
  5.8 59.5 %all-to-all-start = ((bf16[8,128,1024]{2,1,0:T(8,128)(2,1)}), bf16[8,128,1024]{2,1,0:T(8,128)(2,1)S(1)}, u32[]{:S(2)}, u32[]{:S(2)}) async-start(bf16[8,128,1024]{2,1,0:T(8,128)(2,1)} %copy-done.3), calls=%async_computation | async-start | bytes 4194304 | tf_op jit(solution)/shard_map/all_to_all | solution.py:189
  10.9 28.7 %collective-permute-start = (bf16[256,512]{1,0:T(8,128)(2,1)S(1)}, bf16[256,512]{1,0:T(8,128)(2,1)S(1)}, u32[]{:S(2)}, u32[]{:S(2)}) collective-permute-start(bf16[256,512]{1,0:T(8,128)(2,1)S(1)} %bitcast.43), channel_id=1, source_target_pairs={{0,8},{1,9},{2,10},{3,11},{4,12},{5,13},{6,14},{7,15},{8,16},{9,17... | collective-permute-start | bytes 786440 | tf_op jit(solution)/shard_map/ppermute | solution.py:31
  19.7 28.1 %collective-permute-start.1 = (bf16[256,512]{1,0:T(8,128)(2,1)S(1)}, bf16[256,512]{1,0:T(8,128)(2,1)S(1)}, u32[]{:S(2)}, u32[]{:S(2)}) collective-permute-start(bf16[256,512]{1,0:T(8,128)(2,1)S(1)} %bitcast.44), channel_id=1, source_target_pairs={{0,24},{1,25},{2,26},{3,27},{4,28},{5,29},{6,30},{7,31},{8,0},{9,1... | collective-permute-start | bytes 786440 | tf_op jit(solution)/shard_map/ppermute | solution.py:31
  24.4 10.7 %collective-permute-start.2 = (bf16[4,16,512]{2,1,0:T(8,128)(2,1)S(1)}, bf16[4,16,512]{2,1,0:T(8,128)(2,1)S(1)}, u32[]{:S(2)}, u32[]{:S(2)}) collective-permute-start(bf16[4,16,512]{2,1,0:T(8,128)(2,1)S(1)} %get-tuple-element.36), channel_id=1, source_target_pairs={{0,32},{32,64},{64,96},{96,0},{128,160},{160,192},{192,224},{224,1... | collective-permute-start | bytes 196616 | tf_op jit(solution)/shard_map/ppermute | solution.py:38
  27.6 7.5 %collective-permute-start.3 = (bf16[4,16,512]{2,1,0:T(8,128)(2,1)S(1)}, bf16[4,16,512]{2,1,0:T(8,128)(2,1)S(1)}, u32[]{:S(2)}, u32[]{:S(2)}) collective-permute-start(bf16[4,16,512]{2,1,0:T(8,128)(2,1)S(1)} %get-tuple-element.37), channel_id=1, source_target_pairs={{0,64},{32,96},{64,0},{96,32},{128,192},{160,224},{192,128},{224,1... | collective-permute-start | bytes 196616 | tf_op jit(solution)/shard_map/ppermute | solution.py:38
  32.1 5.3 %collective-permute-start.4 = (bf16[4,16,512]{2,1,0:T(8,128)(2,1)S(1)}, bf16[4,16,512]{2,1,0:T(8,128)(2,1)S(1)}, u32[]{:S(2)}, u32[]{:S(2)}) collective-permute-start(bf16[4,16,512]{2,1,0:T(8,128)(2,1)S(1)} %get-tuple-element.38), channel_id=1, source_target_pairs={{0,96},{32,0},{64,32},{96,64},{128,224},{160,128},{192,160},{224,1... | collective-permute-start | bytes 196616 | tf_op jit(solution)/shard_map/ppermute | solution.py:38
  35.1 2.3 %copy-start.15 = (bf16[4,16,512]{2,1,0:T(8,128)(2,1)}, bf16[4,16,512]{2,1,0:T(8,128)(2,1)S(1)}, u32[]{:S(2)}) copy-start(bf16[4,16,512]{2,1,0:T(8,128)(2,1)S(1)} %collective-permute-done.2.refs_1_) | copy-start | bytes 196612
  35.1 2.3 %copy-start.16 = (bf16[4,16,512]{2,1,0:T(8,128)(2,1)}, bf16[4,16,512]{2,1,0:T(8,128)(2,1)S(1)}, u32[]{:S(2)}) copy-start(bf16[4,16,512]{2,1,0:T(8,128)(2,1)S(1)} %collective-permute-done.3.refs_2_) | copy-start | bytes 196612
  37.4 0.6 copy-start.17
  47.8 16.6 %collective-permute-start.6 = (bf16[128,512]{1,0:T(8,128)(2,1)S(1)}, bf16[128,512]{1,0:T(8,128)(2,1)S(1)}, u32[]{:S(2)}, u32[]{:S(2)}) collective-permute-start(bf16[128,512]{1,0:T(8,128)(2,1)S(1)} %slice.27), channel_id=1, source_target_pairs={{0,24},{1,25},{2,26},{3,27},{4,28},{5,29},{6,30},{7,31},{8,0},{9,1... | collective-permute-start | bytes 393224 | tf_op jit(solution)/shard_map/ppermute | solution.py:31
  51.8 13.4 %collective-permute-start.5 = (bf16[128,512]{1,0:T(8,128)(2,1)S(1)}, bf16[128,512]{1,0:T(8,128)(2,1)S(1)}, u32[]{:S(2)}, u32[]{:S(2)}) collective-permute-start(bf16[128,512]{1,0:T(8,128)(2,1)S(1)} %slice.26), channel_id=1, source_target_pairs={{0,8},{1,9},{2,10},{3,11},{4,12},{5,13},{6,14},{7,15},{8,16},{9,17... | collective-permute-start | bytes 393224 | tf_op jit(solution)/shard_map/ppermute | solution.py:31
  67.5 19.9 %copy-start.18 = (s32[1,128]{1,0:T(1,128)S(1)}, s32[1,128]{1,0:T(1,128)}, u32[]{:S(2)}) copy-start(s32[1,128]{1,0:T(1,128)} %param.15) | copy-start | bytes 1540
  67.5 25.3 %copy-start.10 = (bf16[1,128,512]{2,1,0:T(8,128)(2,1)S(1)}, bf16[1,128,512]{2,1,0:T(8,128)(2,1)}, u32[]{:S(2)}) copy-start(bf16[1,128,512]{2,1,0:T(8,128)(2,1)} %param.14) | copy-start | bytes 393220
  67.5 25.1 %all-to-all-start.1 = ((bf16[8,128,512]{2,1,0:T(8,128)(2,1)}), bf16[8,128,512]{2,1,0:T(8,128)(2,1)S(1)}, u32[]{:S(2)}, u32[]{:S(2)}) async-start(bf16[8,128,512]{2,1,0:T(8,128)(2,1)} %project.1), calls=%async_computation.1 | async-start | bytes 2097152 | tf_op jit(solution)/shard_map/all_to_all | solution.py:189
  77.6 9.9 %collective-permute-start.9 = (f32[16,512]{1,0:T(8,128)}, f32[16,512]{1,0:T(8,128)S(1)}, u32[]{:S(2)}, u32[]{:S(2)}) collective-permute-start(f32[16,512]{1,0:T(8,128)} %get-tuple-element.53), channel_id=1, source_target_pairs={{0,384},{32,416},{64,448},{96,480},{128,0},{160,32},{192,64},{224,... | collective-permute-start | bytes 98312 | tf_op jit(solution)/shard_map/ppermute | solution.py:38
  82.4 6.1 %collective-permute-start.8 = (f32[16,512]{1,0:T(8,128)}, f32[16,512]{1,0:T(8,128)S(1)}, u32[]{:S(2)}, u32[]{:S(2)}) collective-permute-start(f32[16,512]{1,0:T(8,128)} %get-tuple-element.52), channel_id=1, source_target_pairs={{0,256},{32,288},{64,320},{96,352},{128,384},{160,416},{192,448},{... | collective-permute-start | bytes 98312 | tf_op jit(solution)/shard_map/ppermute | solution.py:38
  84.3 4.9 %collective-permute-start.7 = (f32[16,512]{1,0:T(8,128)}, f32[16,512]{1,0:T(8,128)S(1)}, u32[]{:S(2)}, u32[]{:S(2)}) collective-permute-start(f32[16,512]{1,0:T(8,128)} %get-tuple-element.51), channel_id=1, source_target_pairs={{0,128},{32,160},{64,192},{96,224},{128,256},{160,288},{192,320},{... | collective-permute-start | bytes 98312 | tf_op jit(solution)/shard_map/ppermute | solution.py:38
  92.9 5.4 %copy-start.14 = (f32[16,512]{1,0:T(8,128)S(1)}, f32[16,512]{1,0:T(8,128)}, u32[]{:S(2)}) copy-start(f32[16,512]{1,0:T(8,128)} %get-tuple-element.56) | copy-start | bytes 98308
  94.0 19.4 %all-to-all-start.2 = ((bf16[8,128,512]{2,1,0:T(8,128)(2,1)}), bf16[8,128,512]{2,1,0:T(8,128)(2,1)S(1)}, u32[]{:S(2)}, u32[]{:S(2)}) async-start(bf16[8,128,512]{2,1,0:T(8,128)(2,1)} %broadcast_in_dim.16), calls=%async_computation.2 | async-start | bytes 2097152 | tf_op jit(solution)/shard_map/all_to_all | solution.py:189
  98.4 10.8 %collective-permute-start.10 = (f32[16,512]{1,0:T(8,128)S(1)}, f32[16,512]{1,0:T(8,128)S(1)}, u32[]{:S(2)}, u32[]{:S(2)}) collective-permute-start(f32[16,512]{1,0:T(8,128)S(1)} %copy-done.14), channel_id=1, source_target_pairs={{0,128},{32,160},{64,192},{96,224},{128,256},{160,288},{192,320},{... | collective-permute-start | bytes 98312 | tf_op jit(solution)/shard_map/ppermute | solution.py:38
  101.3 7.8 %collective-permute-start.11 = (f32[16,512]{1,0:T(8,128)S(1)}, f32[16,512]{1,0:T(8,128)S(1)}, u32[]{:S(2)}, u32[]{:S(2)}) collective-permute-start(f32[16,512]{1,0:T(8,128)S(1)} %copy-done.14), channel_id=1, source_target_pairs={{0,256},{32,288},{64,320},{96,352},{128,384},{160,416},{192,448},{... | collective-permute-start | bytes 98312 | tf_op jit(solution)/shard_map/ppermute | solution.py:38
  107.2 5.0 %collective-permute-start.12 = (f32[16,512]{1,0:T(8,128)S(1)}, f32[16,512]{1,0:T(8,128)S(1)}, u32[]{:S(2)}, u32[]{:S(2)}) collective-permute-start(f32[16,512]{1,0:T(8,128)S(1)} %copy-done.14), channel_id=1, source_target_pairs={{0,384},{32,416},{64,448},{96,480},{128,0},{160,32},{192,64},{224,... | collective-permute-start | bytes 98312 | tf_op jit(solution)/shard_map/ppermute | solution.py:38
  114.0 16.2 %collective-permute-start.18 = (bf16[128,512]{1,0:T(8,128)(2,1)S(1)}, bf16[128,512]{1,0:T(8,128)(2,1)S(1)}, u32[]{:S(2)}, u32[]{:S(2)}) collective-permute-start(bf16[128,512]{1,0:T(8,128)(2,1)S(1)} %get-tuple-element.69), channel_id=1, source_target_pairs={{0,24},{1,25},{2,26},{3,27},{4,28},{5,29},{6,30},{7,31},{8,0},{9,1... | collective-permute-start | bytes 393224 | tf_op jit(solution)/shard_map/ppermute | solution.py:31
  121.3 0.8 copy-start.4
  122.1 45.7 %copy-start.7 = (f32[1,256,512]{2,1,0:T(8,128)S(1)}, f32[1,256,512]{2,1,0:T(8,128)}, u32[]{:S(2)}) copy-start(f32[1,256,512]{2,1,0:T(8,128)} %param.9) | copy-start | bytes 1572868
  122.1 45.7 %copy-start.8 = (f32[1,256,512]{2,1,0:T(8,128)S(1)}, f32[1,256,512]{2,1,0:T(8,128)}, u32[]{:S(2)}) copy-start(f32[1,256,512]{2,1,0:T(8,128)} %param.10) | copy-start | bytes 1572868
  122.1 45.7 %copy-start.5 = (f32[256,512]{1,0:T(8,128)S(1)}, f32[256,512]{1,0:T(8,128)}, u32[]{:S(2)}) copy-start(f32[256,512]{1,0:T(8,128)} %copy-done.4) | copy-start | bytes 1572868
  122.2 16.0 %collective-permute-start.16 = (bf16[128,512]{1,0:T(8,128)(2,1)S(1)}, bf16[128,512]{1,0:T(8,128)(2,1)S(1)}, u32[]{:S(2)}, u32[]{:S(2)}) collective-permute-start(bf16[128,512]{1,0:T(8,128)(2,1)S(1)} %get-tuple-element.68), channel_id=1, source_target_pairs={{0,8},{1,9},{2,10},{3,11},{4,12},{5,13},{6,14},{7,15},{8,16},{9,17... | collective-permute-start | bytes 393224 | tf_op jit(solution)/shard_map/ppermute | solution.py:31
  130.3 27.5 %collective-permute-start.19 = (bf16[256,512]{1,0:T(8,128)(2,1)S(1)}, bf16[256,512]{1,0:T(8,128)(2,1)S(1)}, u32[]{:S(2)}, u32[]{:S(2)}) collective-permute-start(bf16[256,512]{1,0:T(8,128)(2,1)S(1)} %pad_maximum_fusion.2), channel_id=1, source_target_pairs={{0,24},{1,25},{2,26},{3,27},{4,28},{5,29},{6,30},{7,31},{8,0},{9,1... | collective-permute-start | bytes 786440 | tf_op jit(solution)/shard_map/ppermute | solution.py:31
  138.2 29.6 %collective-permute-start.17 = (bf16[256,512]{1,0:T(8,128)(2,1)S(1)}, bf16[256,512]{1,0:T(8,128)(2,1)S(1)}, u32[]{:S(2)}, u32[]{:S(2)}) collective-permute-start(bf16[256,512]{1,0:T(8,128)(2,1)S(1)} %pad_maximum_fusion.1), channel_id=1, source_target_pairs={{0,8},{1,9},{2,10},{3,11},{4,12},{5,13},{6,14},{7,15},{8,16},{9,17... | collective-permute-start | bytes 786440 | tf_op jit(solution)/shard_map/ppermute | solution.py:31
  140.2 15.0 %copy-start.9 = (f32[4,16,512]{2,1,0:T(8,128)}, f32[4,16,512]{2,1,0:T(8,128)S(1)}, u32[]{:S(2)}) copy-start(f32[4,16,512]{2,1,0:T(8,128)S(1)} %pad_maximum_fusion.3.refs_0_) | copy-start | bytes 393220
  140.2 10.7 %collective-permute-start.13 = (f32[4,16,512]{2,1,0:T(8,128)S(1)}, f32[4,16,512]{2,1,0:T(8,128)S(1)}, u32[]{:S(2)}, u32[]{:S(2)}) collective-permute-start(f32[4,16,512]{2,1,0:T(8,128)S(1)} %pad_maximum_fusion.3.refs_0_), channel_id=1, source_target_pairs={{0,32},{32,64},{64,96},{96,0},{128,160},{160,192},{192,224},{224,1... | collective-permute-start | bytes 393224 | tf_op jit(solution)/shard_map/ppermute | solution.py:38
  143.4 7.6 %collective-permute-start.14 = (f32[4,16,512]{2,1,0:T(8,128)S(1)}, f32[4,16,512]{2,1,0:T(8,128)S(1)}, u32[]{:S(2)}, u32[]{:S(2)}) collective-permute-start(f32[4,16,512]{2,1,0:T(8,128)S(1)} %pad_maximum_fusion.3.refs_0_), channel_id=1, source_target_pairs={{0,64},{32,96},{64,0},{96,32},{128,192},{160,224},{192,128},{224,1... | collective-permute-start | bytes 393224 | tf_op jit(solution)/shard_map/ppermute | solution.py:38
  147.9 7.3 %collective-permute-start.15 = (f32[4,16,512]{2,1,0:T(8,128)S(1)}, f32[4,16,512]{2,1,0:T(8,128)S(1)}, u32[]{:S(2)}, u32[]{:S(2)}) collective-permute-start(f32[4,16,512]{2,1,0:T(8,128)S(1)} %pad_maximum_fusion.3.refs_0_), channel_id=1, source_target_pairs={{0,96},{32,0},{64,32},{96,64},{128,224},{160,128},{192,160},{224,1... | collective-permute-start | bytes 393224 | tf_op jit(solution)/shard_map/ppermute | solution.py:38
  150.9 4.3 %copy-start.11 = (f32[4,16,512]{2,1,0:T(8,128)}, f32[4,16,512]{2,1,0:T(8,128)S(1)}, u32[]{:S(2)}) copy-start(f32[4,16,512]{2,1,0:T(8,128)S(1)} %collective-permute-done.13.refs_1_) | copy-start | bytes 393220
  150.9 4.3 %copy-start.12 = (f32[4,16,512]{2,1,0:T(8,128)}, f32[4,16,512]{2,1,0:T(8,128)S(1)}, u32[]{:S(2)}) copy-start(f32[4,16,512]{2,1,0:T(8,128)S(1)} %collective-permute-done.14.refs_2_) | copy-start | bytes 393220
  155.2 0.6 copy-start.13

commit v3 on v2

--- a/solution.py
+++ b/solution.py
@@ -22,12 +22,12 @@
 PLANES = [[z * PLANE + i for i in range(PLANE)] for z in range(SLABS)]
 
 
-def shift_z(value, step):
-    pairs = [
-        (z * PLANE + i, (z + step) % SLABS * PLANE + i)
-        for z in range(SLABS)
-        for i in range(PLANE)
-    ]
+def shift_ring(value, step):
+    pairs = []
+    for z in range(SLABS):
+        for i in range(PLANE):
+            to = z + step if i % 2 == 0 else z - step
+            pairs.append((z * PLANE + i, to % SLABS * PLANE + i))
     return lax.ppermute(value, "fsdp", pairs)
 
 
@@ -58,10 +58,11 @@
     for k in range(SLABS):
         loads[k].wait()
         for i in range(PLANE):
+            place = (k, (0, 2, 1, 3)[k])[i % 2]
             stores.append(
                 pltpu.make_async_copy(
                     columns_ref.at[k, :, pl.ds(i * width, width)],
-                    packed_ref.at[i, :, pl.ds(k * width, width)],
+                    packed_ref.at[i, :, pl.ds(place * width, width)],
                     sems.at[SLABS + 1],
                 )
             )
@@ -189,16 +190,15 @@
     return lax.all_to_all(value, "fsdp", 0, 0, axis_index_groups=PLANES)
 
 
-def scatter_z(blocks):
-    own, to_before, to_after, far = blocks
-    half = own.shape[0] // 2
-    passing_up = shift_z(far[:half], 1).astype(jnp.float32)
-    passing_down = shift_z(far[half:], -1).astype(jnp.float32)
-    up = jnp.concatenate([to_after[:half] + passing_up, to_after[half:]], axis=0)
-    down = jnp.concatenate([to_before[:half], to_before[half:] + passing_down], axis=0)
-    from_before = shift_z(up.astype(jnp.bfloat16), 1)
-    from_after = shift_z(down.astype(jnp.bfloat16), -1)
-    return own + (from_before.astype(jnp.float32) + from_after.astype(jnp.float32))
+def scatter_ring(blocks, beside):
+    own, to_previous, to_next, far = blocks
+    passing = shift_ring(far, 1)
+    passing, *beside = lax.optimization_barrier((passing, *beside))
+    from_next = shift_ring(to_previous.astype(jnp.bfloat16), -1)
+    both = (to_next + passing.astype(jnp.float32)).astype(jnp.bfloat16)
+    from_previous = shift_ring(both, 1)
+    total = own + (from_previous.astype(jnp.float32) + from_next.astype(jnp.float32))
+    return total, beside
 
 
 def shards(weights, first_moment, second_moment, anchor, momentum, inputs, targets, keep_mask):
@@ -210,19 +210,16 @@
     width, out_width = initial.shape
     token_count = rows * lax.axis_size("fsdp")
     workers = lax.axis_size("replica")
-    half = width // 2
 
     packed, shares = pack(tokens, initial)
     columns = to_plane(packed).reshape(PLANE * rows, SLABS * width)
     shares[1:] = [shift_replica(shares[i], 0, i) for i in (1, 2, 3)]
     sums = add_shares(shares)
 
-    before, after = shift_z(initial, 1), shift_z(initial, -1)
-    before, after, *sums = lax.optimization_barrier((before, after, *sums))
-    opposite = jnp.concatenate(
-        [shift_z(before[:half], 1), shift_z(after[half:], -1)], axis=0
-    )
-    partials = list(project(columns, (initial, before, after, opposite)))
+    previous, following = shift_ring(initial, 1), shift_ring(initial, -1)
+    previous, *sums = lax.optimization_barrier((previous, *sums))
+    opposite = shift_ring(previous, 1)
+    partials = list(project(columns, (initial, previous, following, opposite)))
 
     partials[0], *sums = lax.optimization_barrier((partials[0], *sums))
     sums[1:] = [shift_replica(sums[i], i, 0) for i in (1, 2, 3)]
@@ -240,25 +237,17 @@
         return jnp.broadcast_to(residual[None], mine.shape)
 
     received = to_plane(partials[0])
-    gradient = []
-    for h in range(PARTS):
-        out = residual_of(received[:, :, -part_width:], h)
-        if h + 1 < PARTS:
-            out = jnp.concatenate([out, partials[h + 1]], axis=2)
-        if h == 0:
-            out, shared = lax.optimization_barrier((out, new_anchor))
-            shared = [shared] + [shift_replica(shared, i, 0) for i in (1, 2, 3)]
-        received = to_plane(out)
-        if h == 0:
-            received, *shared = lax.optimization_barrier((received, *shared))
-        (far,) = gradient_of(columns, received, (3,), width, part_width, jnp.bfloat16)
-        near = gradient_of(columns, received, (0, 1, 2), width, part_width, jnp.float32)
-        gradient.append(scatter_z((*near, far)))
-    gradient = jnp.concatenate(gradient, axis=1)
+    out = residual_of(received, 0)
+    out, shared = lax.optimization_barrier((out, new_anchor))
+    shared = [shared] + [shift_replica(shared, i, 0) for i in (1, 2, 3)]
+    received = to_plane(out)
+    received, *shared = lax.optimization_barrier((received, *shared))
+    (far,) = gradient_of(columns, received, (3,), width, part_width, jnp.bfloat16)
+    near = gradient_of(columns, received, (0, 1, 2), width, part_width, jnp.float32)
     shared = jnp.stack(shared)
-    block_anchor = place_shares(
-        [shared] + [shift_replica(shared, 0, i) for i in (1, 2, 3)]
-    )
+    shared = [shared] + [shift_replica(shared, 0, i) for i in (1, 2, 3)]
+    gradient, shared = scatter_ring((*near, far), shared)
+    block_anchor = place_shares(shared)
 
     weight_f = initial.astype(jnp.float32)
     first_new = BETA_FIRST * first_moment[0] + (1.0 - BETA_FIRST) * gradient

time: 171 us -> 163 us (0.953)
  the two profiles are of different devices: /device:TPU:33 before, /device:TPU:1 now
where the time goes in v3:
time: 163 us; the launch traced here: 162 us
  starting transfers between devices  90.3 us (55%)
  waiting for transfers between devices  50.6 us (31%)
  Pallas kernels  7.9 us (5%)
  local copies, waits for them, and re-layouts  7.66 us (5%)
  other arithmetic  4.18 us (3%)
    ppermute x6, waiting for transfers between devices, shift_ring(): return lax.ppermute(value, 'fsdp', pairs)  39.4 us
    ppermute x12, starting transfers between devices, shift_replica(): return lax.ppermute(value, 'replica', pairs)  37.4 us
    ppermute x6, starting transfers between devices, shift_ring(): return lax.ppermute(value, 'fsdp', pairs)  31.8 us
    all_to_all x3, starting transfers between devices, to_plane(): return lax.all_to_all(value, 'fsdp', 0, 0, axis_index_groups=PLANES)  21.2 us
    ppermute x12, waiting for transfers between devices, shift_replica(): return lax.ppermute(value, 'replica', pairs)  6.64 us
    unnamed x38, local copies, waits for them, and re-layouts  6.57 us
    all_to_all x3, waiting for transfers between devices, to_plane(): return lax.all_to_all(value, 'fsdp', 0, 0, axis_index_groups=PLANES)  4.55 us
  transfers between devices with their start and end apart: 21, of which 10 were waited for; matrix products, arithmetic and copies ran while one was open for 1% of the time, Pallas kernels for 3%

profile of v3, /device:TPU:1, one launch (start us, length us, event | category | flops | bytes accessed | tf_op | source)
XLA Modules:
  0.0 161.6 jit_solution(17903787167114376621)
XLA Ops:
  0.6 0.0 copy-start
  0.6 0.9 copy-done
  1.6 1.6 copy-done.2
  3.2 0.6 pack_columns.1
  3.8 1.3 copy-done.3
  5.2 0.6 copy-done.6
  5.8 10.5 %all-to-all-start = ((bf16[8,128,1024]{2,1,0:T(8,128)(2,1)}), bf16[8,128,1024]{2,1,0:T(8,128)(2,1)S(1)}, u32[]{:S(2)}, u32[]{:S(2)}) async-start(bf16[8,128,1024]{2,1,0:T(8,128)(2,1)} %copy-done.3), calls=%async_computation | async-start | bytes 4194304 | tf_op jit(solution)/shard_map/all_to_all | solution.py:190
  16.3 7.9 %collective-permute-start = (bf16[256,512]{1,0:T(8,128)(2,1)S(1)}, bf16[256,512]{1,0:T(8,128)(2,1)S(1)}, u32[]{:S(2)}, u32[]{:S(2)}) collective-permute-start(bf16[256,512]{1,0:T(8,128)(2,1)S(1)} %bitcast.43), channel_id=1, source_target_pairs={{0,8},{1,25},{2,10},{3,27},{4,12},{5,29},{6,14},{7,31},{8,16},{9,1... | collective-permute-start | bytes 786440 | tf_op jit(solution)/shard_map/ppermute | solution.py:31
  24.2 3.2 %collective-permute-start.1 = (bf16[4,16,512]{2,1,0:T(8,128)(2,1)S(1)}, bf16[4,16,512]{2,1,0:T(8,128)(2,1)S(1)}, u32[]{:S(2)}, u32[]{:S(2)}) collective-permute-start(bf16[4,16,512]{2,1,0:T(8,128)(2,1)S(1)} %get-tuple-element.40), channel_id=1, source_target_pairs={{0,32},{32,64},{64,96},{96,0},{128,160},{160,192},{192,224},{224,1... | collective-permute-start | bytes 196616 | tf_op jit(solution)/shard_map/ppermute | solution.py:38
  27.4 4.5 %collective-permute-start.2 = (bf16[4,16,512]{2,1,0:T(8,128)(2,1)S(1)}, bf16[4,16,512]{2,1,0:T(8,128)(2,1)S(1)}, u32[]{:S(2)}, u32[]{:S(2)}) collective-permute-start(bf16[4,16,512]{2,1,0:T(8,128)(2,1)S(1)} %get-tuple-element.41), channel_id=1, source_target_pairs={{0,64},{32,96},{64,0},{96,32},{128,192},{160,224},{192,128},{224,1... | collective-permute-start | bytes 196616 | tf_op jit(solution)/shard_map/ppermute | solution.py:38
  31.9 3.0 %collective-permute-start.3 = (bf16[4,16,512]{2,1,0:T(8,128)(2,1)S(1)}, bf16[4,16,512]{2,1,0:T(8,128)(2,1)S(1)}, u32[]{:S(2)}, u32[]{:S(2)}) collective-permute-start(bf16[4,16,512]{2,1,0:T(8,128)(2,1)S(1)} %get-tuple-element.42), channel_id=1, source_target_pairs={{0,96},{32,0},{64,32},{96,64},{128,224},{160,128},{192,160},{224,1... | collective-permute-start | bytes 196616 | tf_op jit(solution)/shard_map/ppermute | solution.py:38
  34.9 1.9 %collective-permute-start.4 = (bf16[256,512]{1,0:T(8,128)(2,1)S(1)}, bf16[256,512]{1,0:T(8,128)(2,1)S(1)}, u32[]{:S(2)}, u32[]{:S(2)}) collective-permute-start(bf16[256,512]{1,0:T(8,128)(2,1)S(1)} %bitcast.44), channel_id=1, source_target_pairs={{0,24},{1,9},{2,26},{3,11},{4,28},{5,13},{6,30},{7,15},{8,0},{9,17... | collective-permute-start | bytes 786440 | tf_op jit(solution)/shard_map/ppermute | solution.py:31
  36.9 0.0 copy-start.15
  36.9 0.0 collective-permute-done.2.refs_2_
  36.9 0.1 collective-permute-done.3.refs_3_
  37.0 0.5 copy-done.15
  37.5 0.0 copy-done.16
  37.5 0.1 copy-done.17
  37.6 1.6 add_shares.1
  39.1 7.2 %collective-permute-start.5 = (bf16[256,512]{1,0:T(8,128)(2,1)S(1)}, bf16[256,512]{1,0:T(8,128)(2,1)S(1)}, u32[]{:S(2)}, u32[]{:S(2)}) collective-permute-start(bf16[256,512]{1,0:T(8,128)(2,1)S(1)} %collective-permute-done.w1_ref), channel_id=1, source_target_pairs={{0,8},{1,25},{2,10},{3,27},{4,12},{5,29},{6,14},{7,31},{8,16},{9,1... | collective-permute-start | bytes 786440 | tf_op jit(solution)/shard_map/ppermute | solution.py:31
  46.4 3.5 %collective-permute-done.4.w2_ref = bf16[256,512]{1,0:T(8,128)(2,1)S(1)} collective-permute-done((bf16[256,512]{1,0:T(8,128)(2,1)S(1)}, bf16[256,512]{1,0:T(8,128)(2,1)S(1)}, u32[]{:S(2)}, u32[]{:S(2)}) %collective-permute-start.4) | collective-permute-done | bytes 262176 | tf_op jit(solution)/shard_map/ppermute | solution.py:31
  49.9 15.0 %collective-permute-done.5.w3_ref = bf16[256,512]{1,0:T(8,128)(2,1)S(1)} collective-permute-done((bf16[256,512]{1,0:T(8,128)(2,1)S(1)}, bf16[256,512]{1,0:T(8,128)(2,1)S(1)}, u32[]{:S(2)}, u32[]{:S(2)}) %collective-permute-start.5) | collective-permute-done | bytes 262176 | tf_op jit(solution)/shard_map/ppermute | solution.py:31
  64.9 0.0 all-to-all-done
  64.9 2.3 %project.1 = bf16[8,128,512]{2,1,0:T(8,128)(2,1)} custom-call(bf16[1024,1024]{1,0:T(8,128)(2,1)S(1)} %bitcast.39, bf16[256,512]{1,0:T(8,128)(2,1)S(1)} %bitcast.45, bf16[256,512]{1,0:T(8,128)(2,1)S(1)} %collective-permute-done.w1_ref, bf16[256,512]{1,0:T(8,128)(2,1)S(1)} %collective-permute-done.4.w2_ref, bf16[256,512]{1,0:T(8,128)(2,1)S(1)} %collective-permute-done.5.w3_ref), custom_call_target="tpu_custom_call" | custom-call | tf_op jit(solution)/shard_map/project/pallas_call | solution.py:159
  67.2 5.0 %all-to-all-start.1 = ((bf16[8,128,512]{2,1,0:T(8,128)(2,1)}), bf16[8,128,512]{2,1,0:T(8,128)(2,1)S(1)}, u32[]{:S(2)}, u32[]{:S(2)}) async-start(bf16[8,128,512]{2,1,0:T(8,128)(2,1)} %project.1), calls=%async_computation.1 | async-start | bytes 2097152 | tf_op jit(solution)/shard_map/all_to_all | solution.py:190
  72.2 4.4 %collective-permute-start.8 = (f32[16,512]{1,0:T(8,128)}, f32[16,512]{1,0:T(8,128)S(1)}, u32[]{:S(2)}, u32[]{:S(2)}) collective-permute-start(f32[16,512]{1,0:T(8,128)} %get-tuple-element.56), channel_id=1, source_target_pairs={{0,384},{32,416},{64,448},{96,480},{128,0},{160,32},{192,64},{224,... | collective-permute-start | bytes 98312 | tf_op jit(solution)/shard_map/ppermute | solution.py:38
  76.7 1.9 %collective-permute-start.7 = (f32[16,512]{1,0:T(8,128)}, f32[16,512]{1,0:T(8,128)S(1)}, u32[]{:S(2)}, u32[]{:S(2)}) collective-permute-start(f32[16,512]{1,0:T(8,128)} %get-tuple-element.55), channel_id=1, source_target_pairs={{0,256},{32,288},{64,320},{96,352},{128,384},{160,416},{192,448},{... | collective-permute-start | bytes 98312 | tf_op jit(solution)/shard_map/ppermute | solution.py:38
  78.6 2.2 %collective-permute-start.6 = (f32[16,512]{1,0:T(8,128)}, f32[16,512]{1,0:T(8,128)S(1)}, u32[]{:S(2)}, u32[]{:S(2)}) collective-permute-start(f32[16,512]{1,0:T(8,128)} %get-tuple-element.54), channel_id=1, source_target_pairs={{0,128},{32,160},{64,192},{96,224},{128,256},{160,288},{192,320},{... | collective-permute-start | bytes 98312 | tf_op jit(solution)/shard_map/ppermute | solution.py:38
  80.8 1.9 %collective-permute-done.7 = f32[16,512]{1,0:T(8,128)S(1)} collective-permute-done((f32[16,512]{1,0:T(8,128)}, f32[16,512]{1,0:T(8,128)S(1)}, u32[]{:S(2)}, u32[]{:S(2)}) %collective-permute-start.7) | collective-permute-done | bytes 32800 | tf_op jit(solution)/shard_map/ppermute | solution.py:38
  82.7 2.8 %collective-permute-done.6 = f32[16,512]{1,0:T(8,128)S(1)} collective-permute-done((f32[16,512]{1,0:T(8,128)}, f32[16,512]{1,0:T(8,128)S(1)}, u32[]{:S(2)}, u32[]{:S(2)}) %collective-permute-start.6) | collective-permute-done | bytes 32800 | tf_op jit(solution)/shard_map/ppermute | solution.py:38
  85.6 1.4 multiply_subtract_fusion
  87.0 0.3 all-to-all-done.1
  87.3 0.1 convert_reduce_fusion
  87.5 0.0 copy-start.14
  87.5 0.1 fusion.12
  87.6 1.1 broadcast_in_dim.16
  88.7 5.6 %all-to-all-start.2 = ((bf16[8,128,512]{2,1,0:T(8,128)(2,1)}), bf16[8,128,512]{2,1,0:T(8,128)(2,1)S(1)}, u32[]{:S(2)}, u32[]{:S(2)}) async-start(bf16[8,128,512]{2,1,0:T(8,128)(2,1)} %broadcast_in_dim.16), calls=%async_computation.2 | async-start | bytes 2097152 | tf_op jit(solution)/shard_map/all_to_all | solution.py:190
  94.3 1.9 %collective-permute-start.9 = (f32[16,512]{1,0:T(8,128)S(1)}, f32[16,512]{1,0:T(8,128)S(1)}, u32[]{:S(2)}, u32[]{:S(2)}) collective-permute-start(f32[16,512]{1,0:T(8,128)S(1)} %copy-done.14), channel_id=1, source_target_pairs={{0,128},{32,160},{64,192},{96,224},{128,256},{160,288},{192,320},{... | collective-permute-start | bytes 98312 | tf_op jit(solution)/shard_map/ppermute | solution.py:38
  96.2 3.4 %collective-permute-start.10 = (f32[16,512]{1,0:T(8,128)S(1)}, f32[16,512]{1,0:T(8,128)S(1)}, u32[]{:S(2)}, u32[]{:S(2)}) collective-permute-start(f32[16,512]{1,0:T(8,128)S(1)} %copy-done.14), channel_id=1, source_target_pairs={{0,256},{32,288},{64,320},{96,352},{128,384},{160,416},{192,448},{... | collective-permute-start | bytes 98312 | tf_op jit(solution)/shard_map/ppermute | solution.py:38
  99.7 3.6 %collective-permute-start.11 = (f32[16,512]{1,0:T(8,128)S(1)}, f32[16,512]{1,0:T(8,128)S(1)}, u32[]{:S(2)}, u32[]{:S(2)}) collective-permute-start(f32[16,512]{1,0:T(8,128)S(1)} %copy-done.14), channel_id=1, source_target_pairs={{0,384},{32,416},{64,448},{96,480},{128,0},{160,32},{192,64},{224,... | collective-permute-start | bytes 98312 | tf_op jit(solution)/shard_map/ppermute | solution.py:38
  103.3 0.0 collective-permute-done.9
  103.3 0.0 collective-permute-done.10
  103.3 1.8 %collective-permute-done.11 = f32[16,512]{1,0:T(8,128)S(1)} collective-permute-done((f32[16,512]{1,0:T(8,128)S(1)}, f32[16,512]{1,0:T(8,128)S(1)}, u32[]{:S(2)}, u32[]{:S(2)}) %collective-permute-start.11) | collective-permute-done | bytes 32800 | tf_op jit(solution)/shard_map/ppermute | solution.py:38
  105.2 4.2 %all-to-all-done.2.rows_ref = bf16[8,128,512]{2,1,0:T(8,128)(2,1)S(1)} async-done(((bf16[8,128,512]{2,1,0:T(8,128)(2,1)}), bf16[8,128,512]{2,1,0:T(8,128)(2,1)S(1)}, u32[]{:S(2)}, u32[]{:S(2)}) %all-to-all-start.2) | async-done | bytes 1048608 | tf_op jit(solution)/shard_map/all_to_all | solution.py:190
  109.4 0.5 gradient.2
  109.9 5.5 %collective-permute-start.12 = (bf16[256,512]{1,0:T(8,128)(2,1)S(1)}, bf16[256,512]{1,0:T(8,128)(2,1)S(1)}, u32[]{:S(2)}, u32[]{:S(2)}) collective-permute-start(bf16[256,512]{1,0:T(8,128)(2,1)S(1)} %gradient.2), channel_id=1, source_target_pairs={{0,8},{1,25},{2,10},{3,27},{4,12},{5,29},{6,14},{7,31},{8,16},{9,1... | collective-permute-start | bytes 786440 | tf_op jit(solution)/shard_map/ppermute | solution.py:31
  115.4 0.0 copy-start.9
  115.4 2.9 %collective-permute-start.13 = (f32[4,16,512]{2,1,0:T(8,128)S(1)}, f32[4,16,512]{2,1,0:T(8,128)S(1)}, u32[]{:S(2)}, u32[]{:S(2)}) collective-permute-start(f32[4,16,512]{2,1,0:T(8,128)S(1)} %pad_maximum_fusion.refs_0_), channel_id=1, source_target_pairs={{0,32},{32,64},{64,96},{96,0},{128,160},{160,192},{192,224},{224,1... | collective-permute-start | bytes 393224 | tf_op jit(solution)/shard_map/ppermute | solution.py:38
  118.3 2.7 %collective-permute-start.14 = (f32[4,16,512]{2,1,0:T(8,128)S(1)}, f32[4,16,512]{2,1,0:T(8,128)S(1)}, u32[]{:S(2)}, u32[]{:S(2)}) collective-permute-start(f32[4,16,512]{2,1,0:T(8,128)S(1)} %pad_maximum_fusion.refs_0_), channel_id=1, source_target_pairs={{0,64},{32,96},{64,0},{96,32},{128,192},{160,224},{192,128},{224,1... | collective-permute-start | bytes 393224 | tf_op jit(solution)/shard_map/ppermute | solution.py:38
  121.0 3.5 %collective-permute-start.15 = (f32[4,16,512]{2,1,0:T(8,128)S(1)}, f32[4,16,512]{2,1,0:T(8,128)S(1)}, u32[]{:S(2)}, u32[]{:S(2)}) collective-permute-start(f32[4,16,512]{2,1,0:T(8,128)S(1)} %pad_maximum_fusion.refs_0_), channel_id=1, source_target_pairs={{0,96},{32,0},{64,32},{96,64},{128,224},{160,128},{192,160},{224,1... | collective-permute-start | bytes 393224 | tf_op jit(solution)/shard_map/ppermute | solution.py:38
  124.5 1.0 gradient.3
  125.5 0.0 copy-start.4
  125.5 0.8 copy-done.4
  126.4 4.4 %collective-permute-start.17 = (bf16[256,512]{1,0:T(8,128)(2,1)S(1)}, bf16[256,512]{1,0:T(8,128)(2,1)S(1)}, u32[]{:S(2)}, u32[]{:S(2)}) collective-permute-start(bf16[256,512]{1,0:T(8,128)(2,1)S(1)} %convert_element_type.57), channel_id=1, source_target_pairs={{0,24},{1,9},{2,26},{3,11},{4,28},{5,13},{6,30},{7,15},{8,0},{9,17... | collective-permute-start | bytes 786440 | tf_op jit(solution)/shard_map/ppermute | solution.py:31
  130.8 0.0 collective-permute-done.15.refs_3_
  130.9 0.1 add_convert_fusion
  131.0 0.5 copy-done.11
  131.5 0.1 copy-done.12
  131.5 0.0 copy-done.13
  131.6 4.9 %collective-permute-start.16 = (bf16[256,512]{1,0:T(8,128)(2,1)S(1)}, bf16[256,512]{1,0:T(8,128)(2,1)S(1)}, u32[]{:S(2)}, u32[]{:S(2)}) collective-permute-start(bf16[256,512]{1,0:T(8,128)(2,1)S(1)} %add_convert_fusion), channel_id=1, source_target_pairs={{0,8},{1,25},{2,10},{3,27},{4,12},{5,29},{6,14},{7,31},{8,16},{9,1... | collective-permute-start | bytes 786440 | tf_op jit(solution)/shard_map/ppermute | solution.py:31
  136.5 2.0 %place_shares.1 = f32[256,512]{1,0:T(8,128)} custom-call(f32[4,16,512]{2,1,0:T(8,128)} %copy-done.9, f32[4,16,512]{2,1,0:T(8,128)} %copy-done.11, f32[4,16,512]{2,1,0:T(8,128)} %copy-done.12, f32[4,16,512]{2,1,0:T(8,128)} %copy-done.13), custom_call_target="tpu_custom_call" | custom-call | tf_op jit(solution)/shard_map/place_shares/pallas_call | solution.py:135
  138.4 15.0 %collective-permute-done.17 = bf16[256,512]{1,0:T(8,128)(2,1)S(1)} collective-permute-done((bf16[256,512]{1,0:T(8,128)(2,1)S(1)}, bf16[256,512]{1,0:T(8,128)(2,1)S(1)}, u32[]{:S(2)}, u32[]{:S(2)}) %collective-permute-start.17) | collective-permute-done | bytes 262176 | tf_op jit(solution)/shard_map/ppermute | solution.py:31
  153.4 5.8 %collective-permute-done.16 = bf16[256,512]{1,0:T(8,128)(2,1)S(1)} collective-permute-done((bf16[256,512]{1,0:T(8,128)(2,1)S(1)}, bf16[256,512]{1,0:T(8,128)(2,1)S(1)}, u32[]{:S(2)}, u32[]{:S(2)}) %collective-permute-start.16) | collective-permute-done | bytes 262176 | tf_op jit(solution)/shard_map/ppermute | solution.py:31
  159.2 2.4 %fusion.7 = (f32[1,256,512]{2,1,0:T(8,128)}, bf16[1,256,512]{2,1,0:T(8,128)(2,1)}) fusion(f32[1,256,512]{2,1,0:T(8,128)S(1)} %copy-done.7, f32[256,512]{1,0:T(8,128)S(1)} %copy-done.5, bf16[256,512]{1,0:T(8,128)(2,1)S(1)} %collective-permute-done.17, bf16[256,512]{1,0:T(8,128)(2,1)S(1)} %collective-permute-done.16, f32[256,512]{1,0:T(8,128)} %place_shares.1, ...), kind=kLoop, calls=%fused_computation.15 | loop fusion | flops 3014656 | bytes 3670016 | tf_op jit(solution)/shard_map/broadcast_in_dim | solution.py:262
  (31 shorter events, 0.1 us)
Async XLA Ops:
  0.6 1.0 copy-start
  1.6 1.6 copy-start.2
  3.8 1.4 copy-start.3
  5.2 0.6 copy-start.6
  5.8 10.5 %copy-start.1 = (bf16[1,256,512]{2,1,0:T(8,128)(2,1)S(1)}, bf16[1,256,512]{2,1,0:T(8,128)(2,1)}, u32[]{:S(2)}) copy-start(bf16[1,256,512]{2,1,0:T(8,128)(2,1)} %param.8) | copy-start | bytes 786436
  5.8 59.1 %all-to-all-start = ((bf16[8,128,1024]{2,1,0:T(8,128)(2,1)}), bf16[8,128,1024]{2,1,0:T(8,128)(2,1)S(1)}, u32[]{:S(2)}, u32[]{:S(2)}) async-start(bf16[8,128,1024]{2,1,0:T(8,128)(2,1)} %copy-done.3), calls=%async_computation | async-start | bytes 4194304 | tf_op jit(solution)/shard_map/all_to_all | solution.py:190
  16.3 22.8 %collective-permute-start = (bf16[256,512]{1,0:T(8,128)(2,1)S(1)}, bf16[256,512]{1,0:T(8,128)(2,1)S(1)}, u32[]{:S(2)}, u32[]{:S(2)}) collective-permute-start(bf16[256,512]{1,0:T(8,128)(2,1)S(1)} %bitcast.43), channel_id=1, source_target_pairs={{0,8},{1,25},{2,10},{3,27},{4,12},{5,29},{6,14},{7,31},{8,16},{9,1... | collective-permute-start | bytes 786440 | tf_op jit(solution)/shard_map/ppermute | solution.py:31
  24.2 12.7 %collective-permute-start.1 = (bf16[4,16,512]{2,1,0:T(8,128)(2,1)S(1)}, bf16[4,16,512]{2,1,0:T(8,128)(2,1)S(1)}, u32[]{:S(2)}, u32[]{:S(2)}) collective-permute-start(bf16[4,16,512]{2,1,0:T(8,128)(2,1)S(1)} %get-tuple-element.40), channel_id=1, source_target_pairs={{0,32},{32,64},{64,96},{96,0},{128,160},{160,192},{192,224},{224,1... | collective-permute-start | bytes 196616 | tf_op jit(solution)/shard_map/ppermute | solution.py:38
  27.4 9.5 %collective-permute-start.2 = (bf16[4,16,512]{2,1,0:T(8,128)(2,1)S(1)}, bf16[4,16,512]{2,1,0:T(8,128)(2,1)S(1)}, u32[]{:S(2)}, u32[]{:S(2)}) collective-permute-start(bf16[4,16,512]{2,1,0:T(8,128)(2,1)S(1)} %get-tuple-element.41), channel_id=1, source_target_pairs={{0,64},{32,96},{64,0},{96,32},{128,192},{160,224},{192,128},{224,1... | collective-permute-start | bytes 196616 | tf_op jit(solution)/shard_map/ppermute | solution.py:38
  31.9 5.0 %collective-permute-start.3 = (bf16[4,16,512]{2,1,0:T(8,128)(2,1)S(1)}, bf16[4,16,512]{2,1,0:T(8,128)(2,1)S(1)}, u32[]{:S(2)}, u32[]{:S(2)}) collective-permute-start(bf16[4,16,512]{2,1,0:T(8,128)(2,1)S(1)} %get-tuple-element.42), channel_id=1, source_target_pairs={{0,96},{32,0},{64,32},{96,64},{128,224},{160,128},{192,160},{224,1... | collective-permute-start | bytes 196616 | tf_op jit(solution)/shard_map/ppermute | solution.py:38
  34.9 15.0 %collective-permute-start.4 = (bf16[256,512]{1,0:T(8,128)(2,1)S(1)}, bf16[256,512]{1,0:T(8,128)(2,1)S(1)}, u32[]{:S(2)}, u32[]{:S(2)}) collective-permute-start(bf16[256,512]{1,0:T(8,128)(2,1)S(1)} %bitcast.44), channel_id=1, source_target_pairs={{0,24},{1,9},{2,26},{3,11},{4,28},{5,13},{6,30},{7,15},{8,0},{9,17... | collective-permute-start | bytes 786440 | tf_op jit(solution)/shard_map/ppermute | solution.py:31
  36.9 0.6 copy-start.15
  36.9 0.6 copy-start.16
  37.0 0.6 copy-start.17
  39.1 25.8 %collective-permute-start.5 = (bf16[256,512]{1,0:T(8,128)(2,1)S(1)}, bf16[256,512]{1,0:T(8,128)(2,1)S(1)}, u32[]{:S(2)}, u32[]{:S(2)}) collective-permute-start(bf16[256,512]{1,0:T(8,128)(2,1)S(1)} %collective-permute-done.w1_ref), channel_id=1, source_target_pairs={{0,8},{1,25},{2,10},{3,27},{4,12},{5,29},{6,14},{7,31},{8,16},{9,1... | collective-permute-start | bytes 786440 | tf_op jit(solution)/shard_map/ppermute | solution.py:31
  64.9 15.9 %copy-start.18 = (s32[1,128]{1,0:T(1,128)S(1)}, s32[1,128]{1,0:T(1,128)}, u32[]{:S(2)}) copy-start(s32[1,128]{1,0:T(1,128)} %param.15) | copy-start | bytes 1540
  67.2 20.3 %copy-start.10 = (bf16[1,128,512]{2,1,0:T(8,128)(2,1)S(1)}, bf16[1,128,512]{2,1,0:T(8,128)(2,1)}, u32[]{:S(2)}) copy-start(bf16[1,128,512]{2,1,0:T(8,128)(2,1)} %param.14) | copy-start | bytes 393220
  67.2 20.1 %all-to-all-start.1 = ((bf16[8,128,512]{2,1,0:T(8,128)(2,1)}), bf16[8,128,512]{2,1,0:T(8,128)(2,1)S(1)}, u32[]{:S(2)}, u32[]{:S(2)}) async-start(bf16[8,128,512]{2,1,0:T(8,128)(2,1)} %project.1), calls=%async_computation.1 | async-start | bytes 2097152 | tf_op jit(solution)/shard_map/all_to_all | solution.py:190
  72.2 8.6 %collective-permute-start.8 = (f32[16,512]{1,0:T(8,128)}, f32[16,512]{1,0:T(8,128)S(1)}, u32[]{:S(2)}, u32[]{:S(2)}) collective-permute-start(f32[16,512]{1,0:T(8,128)} %get-tuple-element.56), channel_id=1, source_target_pairs={{0,384},{32,416},{64,448},{96,480},{128,0},{160,32},{192,64},{224,... | collective-permute-start | bytes 98312 | tf_op jit(solution)/shard_map/ppermute | solution.py:38
  76.7 6.1 %collective-permute-start.7 = (f32[16,512]{1,0:T(8,128)}, f32[16,512]{1,0:T(8,128)S(1)}, u32[]{:S(2)}, u32[]{:S(2)}) collective-permute-start(f32[16,512]{1,0:T(8,128)} %get-tuple-element.55), channel_id=1, source_target_pairs={{0,256},{32,288},{64,320},{96,352},{128,384},{160,416},{192,448},{... | collective-permute-start | bytes 98312 | tf_op jit(solution)/shard_map/ppermute | solution.py:38
  78.6 7.0 %collective-permute-start.6 = (f32[16,512]{1,0:T(8,128)}, f32[16,512]{1,0:T(8,128)S(1)}, u32[]{:S(2)}, u32[]{:S(2)}) collective-permute-start(f32[16,512]{1,0:T(8,128)} %get-tuple-element.54), channel_id=1, source_target_pairs={{0,128},{32,160},{64,192},{96,224},{128,256},{160,288},{192,320},{... | collective-permute-start | bytes 98312 | tf_op jit(solution)/shard_map/ppermute | solution.py:38
  87.5 6.8 %copy-start.14 = (f32[16,512]{1,0:T(8,128)S(1)}, f32[16,512]{1,0:T(8,128)}, u32[]{:S(2)}) copy-start(f32[16,512]{1,0:T(8,128)} %get-tuple-element.60) | copy-start | bytes 98308
  88.7 20.7 %all-to-all-start.2 = ((bf16[8,128,512]{2,1,0:T(8,128)(2,1)}), bf16[8,128,512]{2,1,0:T(8,128)(2,1)S(1)}, u32[]{:S(2)}, u32[]{:S(2)}) async-start(bf16[8,128,512]{2,1,0:T(8,128)(2,1)} %broadcast_in_dim.16), calls=%async_computation.2 | async-start | bytes 2097152 | tf_op jit(solution)/shard_map/all_to_all | solution.py:190
  94.3 9.0 %collective-permute-start.9 = (f32[16,512]{1,0:T(8,128)S(1)}, f32[16,512]{1,0:T(8,128)S(1)}, u32[]{:S(2)}, u32[]{:S(2)}) collective-permute-start(f32[16,512]{1,0:T(8,128)S(1)} %copy-done.14), channel_id=1, source_target_pairs={{0,128},{32,160},{64,192},{96,224},{128,256},{160,288},{192,320},{... | collective-permute-start | bytes 98312 | tf_op jit(solution)/shard_map/ppermute | solution.py:38
  96.2 7.1 %collective-permute-start.10 = (f32[16,512]{1,0:T(8,128)S(1)}, f32[16,512]{1,0:T(8,128)S(1)}, u32[]{:S(2)}, u32[]{:S(2)}) collective-permute-start(f32[16,512]{1,0:T(8,128)S(1)} %copy-done.14), channel_id=1, source_target_pairs={{0,256},{32,288},{64,320},{96,352},{128,384},{160,416},{192,448},{... | collective-permute-start | bytes 98312 | tf_op jit(solution)/shard_map/ppermute | solution.py:38
  99.7 5.5 %collective-permute-start.11 = (f32[16,512]{1,0:T(8,128)S(1)}, f32[16,512]{1,0:T(8,128)S(1)}, u32[]{:S(2)}, u32[]{:S(2)}) collective-permute-start(f32[16,512]{1,0:T(8,128)S(1)} %copy-done.14), channel_id=1, source_target_pairs={{0,384},{32,416},{64,448},{96,480},{128,0},{160,32},{192,64},{224,... | collective-permute-start | bytes 98312 | tf_op jit(solution)/shard_map/ppermute | solution.py:38
  109.9 21.0 %collective-permute-start.12 = (bf16[256,512]{1,0:T(8,128)(2,1)S(1)}, bf16[256,512]{1,0:T(8,128)(2,1)S(1)}, u32[]{:S(2)}, u32[]{:S(2)}) collective-permute-start(bf16[256,512]{1,0:T(8,128)(2,1)S(1)} %gradient.2), channel_id=1, source_target_pairs={{0,8},{1,25},{2,10},{3,27},{4,12},{5,29},{6,14},{7,31},{8,16},{9,1... | collective-permute-start | bytes 786440 | tf_op jit(solution)/shard_map/ppermute | solution.py:31
  115.4 15.6 %copy-start.9 = (f32[4,16,512]{2,1,0:T(8,128)}, f32[4,16,512]{2,1,0:T(8,128)S(1)}, u32[]{:S(2)}) copy-start(f32[4,16,512]{2,1,0:T(8,128)S(1)} %pad_maximum_fusion.refs_0_) | copy-start | bytes 393220
  115.4 15.4 %collective-permute-start.13 = (f32[4,16,512]{2,1,0:T(8,128)S(1)}, f32[4,16,512]{2,1,0:T(8,128)S(1)}, u32[]{:S(2)}, u32[]{:S(2)}) collective-permute-start(f32[4,16,512]{2,1,0:T(8,128)S(1)} %pad_maximum_fusion.refs_0_), channel_id=1, source_target_pairs={{0,32},{32,64},{64,96},{96,0},{128,160},{160,192},{192,224},{224,1... | collective-permute-start | bytes 393224 | tf_op jit(solution)/shard_map/ppermute | solution.py:38
  118.3 12.6 %collective-permute-start.14 = (f32[4,16,512]{2,1,0:T(8,128)S(1)}, f32[4,16,512]{2,1,0:T(8,128)S(1)}, u32[]{:S(2)}, u32[]{:S(2)}) collective-permute-start(f32[4,16,512]{2,1,0:T(8,128)S(1)} %pad_maximum_fusion.refs_0_), channel_id=1, source_target_pairs={{0,64},{32,96},{64,0},{96,32},{128,192},{160,224},{192,128},{224,1... | collective-permute-start | bytes 393224 | tf_op jit(solution)/shard_map/ppermute | solution.py:38
  121.0 9.9 %collective-permute-start.15 = (f32[4,16,512]{2,1,0:T(8,128)S(1)}, f32[4,16,512]{2,1,0:T(8,128)S(1)}, u32[]{:S(2)}, u32[]{:S(2)}) collective-permute-start(f32[4,16,512]{2,1,0:T(8,128)S(1)} %pad_maximum_fusion.refs_0_), channel_id=1, source_target_pairs={{0,96},{32,0},{64,32},{96,64},{128,224},{160,128},{192,160},{224,1... | collective-permute-start | bytes 393224 | tf_op jit(solution)/shard_map/ppermute | solution.py:38
  125.5 0.8 copy-start.4
  126.3 32.9 %copy-start.7 = (f32[1,256,512]{2,1,0:T(8,128)S(1)}, f32[1,256,512]{2,1,0:T(8,128)}, u32[]{:S(2)}) copy-start(f32[1,256,512]{2,1,0:T(8,128)} %param.9) | copy-start | bytes 1572868
  126.3 32.9 %copy-start.8 = (f32[1,256,512]{2,1,0:T(8,128)S(1)}, f32[1,256,512]{2,1,0:T(8,128)}, u32[]{:S(2)}) copy-start(f32[1,256,512]{2,1,0:T(8,128)} %param.10) | copy-start | bytes 1572868
  126.3 32.9 %copy-start.5 = (f32[256,512]{1,0:T(8,128)S(1)}, f32[256,512]{1,0:T(8,128)}, u32[]{:S(2)}) copy-start(f32[256,512]{1,0:T(8,128)} %copy-done.4) | copy-start | bytes 1572868
  126.4 27.1 %collective-permute-start.17 = (bf16[256,512]{1,0:T(8,128)(2,1)S(1)}, bf16[256,512]{1,0:T(8,128)(2,1)S(1)}, u32[]{:S(2)}, u32[]{:S(2)}) collective-permute-start(bf16[256,512]{1,0:T(8,128)(2,1)S(1)} %convert_element_type.57), channel_id=1, source_target_pairs={{0,24},{1,9},{2,26},{3,11},{4,28},{5,13},{6,30},{7,15},{8,0},{9,17... | collective-permute-start | bytes 786440 | tf_op jit(solution)/shard_map/ppermute | solution.py:31
  130.8 0.6 copy-start.11
  130.8 0.7 copy-start.12
  130.9 0.7 copy-start.13
  131.6 27.7 %collective-permute-start.16 = (bf16[256,512]{1,0:T(8,128)(2,1)S(1)}, bf16[256,512]{1,0:T(8,128)(2,1)S(1)}, u32[]{:S(2)}, u32[]{:S(2)}) collective-permute-start(bf16[256,512]{1,0:T(8,128)(2,1)S(1)} %add_convert_fusion), channel_id=1, source_target_pairs={{0,8},{1,25},{2,10},{3,27},{4,12},{5,29},{6,14},{7,31},{8,16},{9,1... | collective-permute-start | bytes 786440 | tf_op jit(solution)/shard_map/ppermute | solution.py:31

commit v4 on v3

--- a/solution.py
+++ b/solution.py
@@ -139,6 +139,19 @@
     )(*shares)
 
 
+def mask_kernel(keep_ref, mask_ref):
+    mask_ref[...] = keep_ref[...].astype(mask_ref.dtype)
+
+
+def mask_of(keep):
+    return pl.pallas_call(
+        mask_kernel,
+        out_shape=jax.ShapeDtypeStruct(keep.shape, jnp.float32),
+        cost_estimate=pl.CostEstimate(flops=20 * 10**9, bytes_accessed=1 << 10, transcendentals=0),
+        name="mask",
+    )(keep)
+
+
 def project_kernel(x_ref, w0_ref, w1_ref, w2_ref, w3_ref, *out_refs):
     width = w0_ref.shape[0]
     part_width = out_refs[0].shape[2]
@@ -205,7 +218,7 @@
     initial = weights[0]
     tokens = inputs[0]
     goal_rows = targets[0]
-    mask_rows = keep_mask[0].astype(jnp.float32)[:, None]
+    mask = mask_of(keep_mask)
     rows = tokens.shape[0]
     width, out_width = initial.shape
     token_count = rows * lax.axis_size("fsdp")
@@ -217,8 +230,9 @@
     sums = add_shares(shares)
 
     previous, following = shift_ring(initial, 1), shift_ring(initial, -1)
-    previous, *sums = lax.optimization_barrier((previous, *sums))
+    previous, mask = lax.optimization_barrier((previous, mask))
     opposite = shift_ring(previous, 1)
+    columns, *sums = lax.optimization_barrier((columns, *sums))
     partials = list(project(columns, (initial, previous, following, opposite)))
 
     partials[0], *sums = lax.optimization_barrier((partials[0], *sums))
@@ -233,7 +247,7 @@
     def residual_of(mine, h):
         goal = goal_rows[:, h * part_width : (h + 1) * part_width].astype(jnp.float32)
         projected = jnp.sum(mine.astype(jnp.float32), 0)
-        residual = ((projected - goal) * mask_rows / token_count).astype(jnp.bfloat16)
+        residual = ((projected - goal) * mask[0][:, None] / token_count).astype(jnp.bfloat16)
         return jnp.broadcast_to(residual[None], mine.shape)
 
     received = to_plane(partials[0])

time: 163 us -> 157 us (0.963)
  waiting for transfers between devices: 50.6 us -> 40.1 us
  starting transfers between devices: 90.3 us -> 94.1 us
    ppermute x6, waiting for transfers between devices: 39.4 us -> 25.2 us  [shift_ring(): return lax.ppermute(value, 'fsdp', pairs)]
    ppermute x6, starting transfers between devices: 31.8 us -> 42.5 us  [shift_ring(): return lax.ppermute(value, 'fsdp', pairs)]
    all_to_all x3, starting transfers between devices: 21.2 us -> 14.9 us  [to_plane(): return lax.all_to_all(value, 'fsdp', 0, 0, axis_index_groups=PLANES)]
    ppermute x12, waiting for transfers between devices: 6.64 us -> 9.08 us  [shift_replica(): return lax.ppermute(value, 'replica', pairs)]
  transfers between devices with their start and end apart: 21 -> 21, of which waited for: 10 -> 8; matrix products, arithmetic and copies ran while one was open for 1% -> 1% of each run, Pallas kernels for 3% -> 4%
where the time goes in v4:
time: 157 us; the launch traced here: 156 us
  starting transfers between devices  94.1 us (60%)
  waiting for transfers between devices  40.1 us (26%)
  Pallas kernels  9.11 us (6%)
  local copies, waits for them, and re-layouts  7.66 us (5%)
  other arithmetic  4.18 us (3%)
    ppermute x6, starting transfers between devices, shift_ring(): return lax.ppermute(value, 'fsdp', pairs)  42.5 us
    ppermute x12, starting transfers between devices, shift_replica(): return lax.ppermute(value, 'replica', pairs)  36.7 us
    ppermute x6, waiting for transfers between devices, shift_ring(): return lax.ppermute(value, 'fsdp', pairs)  25.2 us
    all_to_all x3, starting transfers between devices, to_plane(): return lax.all_to_all(value, 'fsdp', 0, 0, axis_index_groups=PLANES)  14.9 us
    ppermute x12, waiting for transfers between devices, shift_replica(): return lax.ppermute(value, 'replica', pairs)  9.08 us
    unnamed x38, local copies, waits for them, and re-layouts  6.57 us
    all_to_all x3, waiting for transfers between devices, to_plane(): return lax.all_to_all(value, 'fsdp', 0, 0, axis_index_groups=PLANES)  5.83 us
  transfers between devices with their start and end apart: 21, of which 8 were waited for; matrix products, arithmetic and copies ran while one was open for 1% of the time, Pallas kernels for 4%

profile of v4, /device:TPU:1, one launch (start us, length us, event | category | flops | bytes accessed | tf_op | source)
XLA Modules:
  0.0 156.2 jit_solution(8175448232608064003)
XLA Ops:
  0.6 13.3 %collective-permute-start.3 = (bf16[256,512]{1,0:T(8,128)(2,1)}, bf16[256,512]{1,0:T(8,128)(2,1)S(1)}, u32[]{:S(2)}, u32[]{:S(2)}) collective-permute-start(bf16[256,512]{1,0:T(8,128)(2,1)} %bitcast.41), channel_id=1, source_target_pairs={{0,8},{1,25},{2,10},{3,27},{4,12},{5,29},{6,14},{7,31},{8,16},{9,1... | collective-permute-start | bytes 786440 | tf_op jit(solution)/shard_map/ppermute | solution.py:31
  13.9 1.9 %collective-permute-start.4 = (bf16[256,512]{1,0:T(8,128)(2,1)}, bf16[256,512]{1,0:T(8,128)(2,1)S(1)}, u32[]{:S(2)}, u32[]{:S(2)}) collective-permute-start(bf16[256,512]{1,0:T(8,128)(2,1)} %bitcast.42), channel_id=1, source_target_pairs={{0,24},{1,9},{2,26},{3,11},{4,28},{5,13},{6,30},{7,15},{8,0},{9,17... | collective-permute-start | bytes 786440 | tf_op jit(solution)/shard_map/ppermute | solution.py:31
  15.9 0.0 copy-start
  15.9 0.9 copy-done
  16.8 1.6 %copy-done.2 = bf16[1,128,8192]{2,1,0:T(8,128)(2,1)S(1)} copy-done((bf16[1,128,8192]{2,1,0:T(8,128)(2,1)S(1)}, bf16[1,128,8192]{2,1,0:T(8,128)(2,1)}, u32[]{:S(2)}) %copy-start.2) | copy-done | bytes 2097176
  18.4 0.6 pack_columns.1
  19.1 1.3 copy-done.3
  20.4 0.6 copy-done.6
  21.0 5.3 %all-to-all-start = ((bf16[8,128,1024]{2,1,0:T(8,128)(2,1)}), bf16[8,128,1024]{2,1,0:T(8,128)(2,1)S(1)}, u32[]{:S(2)}, u32[]{:S(2)}) async-start(bf16[8,128,1024]{2,1,0:T(8,128)(2,1)} %copy-done.3), calls=%async_computation | async-start | bytes 4194304 | tf_op jit(solution)/shard_map/all_to_all | solution.py:203
  26.3 1.2 mask.1
  27.5 3.8 %collective-permute-done.3.w1_ref = bf16[256,512]{1,0:T(8,128)(2,1)S(1)} collective-permute-done((bf16[256,512]{1,0:T(8,128)(2,1)}, bf16[256,512]{1,0:T(8,128)(2,1)S(1)}, u32[]{:S(2)}, u32[]{:S(2)}) %collective-permute-start.3) | collective-permute-done | bytes 262176 | tf_op jit(solution)/shard_map/ppermute | solution.py:31
  31.3 13.0 %collective-permute-start.5 = (bf16[256,512]{1,0:T(8,128)(2,1)S(1)}, bf16[256,512]{1,0:T(8,128)(2,1)S(1)}, u32[]{:S(2)}, u32[]{:S(2)}) collective-permute-start(bf16[256,512]{1,0:T(8,128)(2,1)S(1)} %collective-permute-done.3.w1_ref), channel_id=1, source_target_pairs={{0,8},{1,25},{2,10},{3,27},{4,12},{5,29},{6,14},{7,31},{8,16},{9,1... | collective-permute-start | bytes 786440 | tf_op jit(solution)/shard_map/ppermute | solution.py:31
  44.3 3.4 %collective-permute-start = (bf16[4,16,512]{2,1,0:T(8,128)(2,1)S(1)}, bf16[4,16,512]{2,1,0:T(8,128)(2,1)S(1)}, u32[]{:S(2)}, u32[]{:S(2)}) collective-permute-start(bf16[4,16,512]{2,1,0:T(8,128)(2,1)S(1)} %get-tuple-element.42), channel_id=1, source_target_pairs={{0,32},{32,64},{64,96},{96,0},{128,160},{160,192},{192,224},{224,1... | collective-permute-start | bytes 196616 | tf_op jit(solution)/shard_map/ppermute | solution.py:38
  47.7 4.5 %collective-permute-start.1 = (bf16[4,16,512]{2,1,0:T(8,128)(2,1)S(1)}, bf16[4,16,512]{2,1,0:T(8,128)(2,1)S(1)}, u32[]{:S(2)}, u32[]{:S(2)}) collective-permute-start(bf16[4,16,512]{2,1,0:T(8,128)(2,1)S(1)} %get-tuple-element.43), channel_id=1, source_target_pairs={{0,64},{32,96},{64,0},{96,32},{128,192},{160,224},{192,128},{224,1... | collective-permute-start | bytes 196616 | tf_op jit(solution)/shard_map/ppermute | solution.py:38
  52.3 3.0 %collective-permute-start.2 = (bf16[4,16,512]{2,1,0:T(8,128)(2,1)S(1)}, bf16[4,16,512]{2,1,0:T(8,128)(2,1)S(1)}, u32[]{:S(2)}, u32[]{:S(2)}) collective-permute-start(bf16[4,16,512]{2,1,0:T(8,128)(2,1)S(1)} %get-tuple-element.44), channel_id=1, source_target_pairs={{0,96},{32,0},{64,32},{96,64},{128,224},{160,128},{192,160},{224,1... | collective-permute-start | bytes 196616 | tf_op jit(solution)/shard_map/ppermute | solution.py:38
  55.3 0.0 copy-start.15
  55.3 0.0 collective-permute-done.1.refs_2_
  55.3 2.8 %collective-permute-done.2.refs_3_ = bf16[4,16,512]{2,1,0:T(8,128)(2,1)S(1)} collective-permute-done((bf16[4,16,512]{2,1,0:T(8,128)(2,1)S(1)}, bf16[4,16,512]{2,1,0:T(8,128)(2,1)S(1)}, u32[]{:S(2)}, u32[]{:S(2)}) %collective-permute-start.2) | collective-permute-done | bytes 65568 | tf_op jit(solution)/shard_map/ppermute | solution.py:38
  58.1 0.6 copy-done.17
  58.7 1.6 %add_shares.1 = (f32[16,512]{1,0:T(8,128)}, f32[16,512]{1,0:T(8,128)}, f32[16,512]{1,0:T(8,128)}, f32[16,512]{1,0:T(8,128)}) custom-call(bf16[4,16,512]{2,1,0:T(8,128)(2,1)} %copy-done.6, bf16[4,16,512]{2,1,0:T(8,128)(2,1)} %copy-done.15, bf16[4,16,512]{2,1,0:T(8,128)(2,1)} %copy-done.16, bf16[4,16,512]{2,1,0:T(8,128)(2,1)} %copy-done.17), custom_call_target="tpu_custom_call" | custom-call | tf_op jit(solution)/shard_map/add_shares/pallas_call | solution.py:116
  60.3 0.0 collective-permute-done.5.w3_ref
  60.3 2.3 %project.1 = bf16[8,128,512]{2,1,0:T(8,128)(2,1)} custom-call(bf16[1024,1024]{1,0:T(8,128)(2,1)S(1)} %bitcast.38, bf16[256,512]{1,0:T(8,128)(2,1)S(1)} %bitcast.44, bf16[256,512]{1,0:T(8,128)(2,1)S(1)} %collective-permute-done.3.w1_ref, bf16[256,512]{1,0:T(8,128)(2,1)S(1)} %collective-permute-done.4.w2_ref, bf16[256,512]{1,0:T(8,128)(2,1)S(1)} %collective-permute-done.5.w3_ref), custom_call_target="tpu_custom_call" | custom-call | tf_op jit(solution)/shard_map/project/pallas_call | solution.py:172
  62.6 5.0 %all-to-all-start.1 = ((bf16[8,128,512]{2,1,0:T(8,128)(2,1)}), bf16[8,128,512]{2,1,0:T(8,128)(2,1)S(1)}, u32[]{:S(2)}, u32[]{:S(2)}) async-start(bf16[8,128,512]{2,1,0:T(8,128)(2,1)} %project.1), calls=%async_computation.1 | async-start | bytes 2097152 | tf_op jit(solution)/shard_map/all_to_all | solution.py:203
  67.6 3.5 %collective-permute-start.8 = (f32[16,512]{1,0:T(8,128)}, f32[16,512]{1,0:T(8,128)S(1)}, u32[]{:S(2)}, u32[]{:S(2)}) collective-permute-start(f32[16,512]{1,0:T(8,128)} %get-tuple-element.60), channel_id=1, source_target_pairs={{0,384},{32,416},{64,448},{96,480},{128,0},{160,32},{192,64},{224,... | collective-permute-start | bytes 98312 | tf_op jit(solution)/shard_map/ppermute | solution.py:38
  71.1 1.9 %collective-permute-start.7 = (f32[16,512]{1,0:T(8,128)}, f32[16,512]{1,0:T(8,128)S(1)}, u32[]{:S(2)}, u32[]{:S(2)}) collective-permute-start(f32[16,512]{1,0:T(8,128)} %get-tuple-element.59), channel_id=1, source_target_pairs={{0,256},{32,288},{64,320},{96,352},{128,384},{160,416},{192,448},{... | collective-permute-start | bytes 98312 | tf_op jit(solution)/shard_map/ppermute | solution.py:38
  73.0 2.2 %collective-permute-start.6 = (f32[16,512]{1,0:T(8,128)}, f32[16,512]{1,0:T(8,128)S(1)}, u32[]{:S(2)}, u32[]{:S(2)}) collective-permute-start(f32[16,512]{1,0:T(8,128)} %get-tuple-element.58), channel_id=1, source_target_pairs={{0,128},{32,160},{64,192},{96,224},{128,256},{160,288},{192,320},{... | collective-permute-start | bytes 98312 | tf_op jit(solution)/shard_map/ppermute | solution.py:38
  75.2 0.0 collective-permute-done.8
  75.2 1.9 %collective-permute-done.7 = f32[16,512]{1,0:T(8,128)S(1)} collective-permute-done((f32[16,512]{1,0:T(8,128)}, f32[16,512]{1,0:T(8,128)S(1)}, u32[]{:S(2)}, u32[]{:S(2)}) %collective-permute-start.7) | collective-permute-done | bytes 32800 | tf_op jit(solution)/shard_map/ppermute | solution.py:38
  77.1 2.5 %collective-permute-done.6 = f32[16,512]{1,0:T(8,128)S(1)} collective-permute-done((f32[16,512]{1,0:T(8,128)}, f32[16,512]{1,0:T(8,128)S(1)}, u32[]{:S(2)}, u32[]{:S(2)}) %collective-permute-start.6) | collective-permute-done | bytes 32800 | tf_op jit(solution)/shard_map/ppermute | solution.py:38
  79.7 1.4 multiply_subtract_fusion
  81.1 1.6 %all-to-all-done.1 = bf16[8,128,512]{2,1,0:T(8,128)(2,1)S(1)} async-done(((bf16[8,128,512]{2,1,0:T(8,128)(2,1)}), bf16[8,128,512]{2,1,0:T(8,128)(2,1)S(1)}, u32[]{:S(2)}, u32[]{:S(2)}) %all-to-all-start.1) | async-done | bytes 1048608 | tf_op jit(solution)/shard_map/all_to_all | solution.py:203
  82.7 0.1 convert_reduce_fusion
  82.8 0.0 copy-start.14
  82.9 0.1 fusion.12
  83.0 1.1 broadcast_in_dim.15
  84.1 4.6 %all-to-all-start.2 = ((bf16[8,128,512]{2,1,0:T(8,128)(2,1)}), bf16[8,128,512]{2,1,0:T(8,128)(2,1)S(1)}, u32[]{:S(2)}, u32[]{:S(2)}) async-start(bf16[8,128,512]{2,1,0:T(8,128)(2,1)} %broadcast_in_dim.15), calls=%async_computation.2 | async-start | bytes 2097152 | tf_op jit(solution)/shard_map/all_to_all | solution.py:203
  88.7 1.9 %collective-permute-start.9 = (f32[16,512]{1,0:T(8,128)S(1)}, f32[16,512]{1,0:T(8,128)S(1)}, u32[]{:S(2)}, u32[]{:S(2)}) collective-permute-start(f32[16,512]{1,0:T(8,128)S(1)} %copy-done.14), channel_id=1, source_target_pairs={{0,128},{32,160},{64,192},{96,224},{128,256},{160,288},{192,320},{... | collective-permute-start | bytes 98312 | tf_op jit(solution)/shard_map/ppermute | solution.py:38
  90.6 3.4 %collective-permute-start.10 = (f32[16,512]{1,0:T(8,128)S(1)}, f32[16,512]{1,0:T(8,128)S(1)}, u32[]{:S(2)}, u32[]{:S(2)}) collective-permute-start(f32[16,512]{1,0:T(8,128)S(1)} %copy-done.14), channel_id=1, source_target_pairs={{0,256},{32,288},{64,320},{96,352},{128,384},{160,416},{192,448},{... | collective-permute-start | bytes 98312 | tf_op jit(solution)/shard_map/ppermute | solution.py:38
  94.1 3.6 %collective-permute-start.11 = (f32[16,512]{1,0:T(8,128)S(1)}, f32[16,512]{1,0:T(8,128)S(1)}, u32[]{:S(2)}, u32[]{:S(2)}) collective-permute-start(f32[16,512]{1,0:T(8,128)S(1)} %copy-done.14), channel_id=1, source_target_pairs={{0,384},{32,416},{64,448},{96,480},{128,0},{160,32},{192,64},{224,... | collective-permute-start | bytes 98312 | tf_op jit(solution)/shard_map/ppermute | solution.py:38
  97.7 0.0 collective-permute-done.9
  97.7 0.0 collective-permute-done.10
  97.7 1.8 %collective-permute-done.11 = f32[16,512]{1,0:T(8,128)S(1)} collective-permute-done((f32[16,512]{1,0:T(8,128)S(1)}, f32[16,512]{1,0:T(8,128)S(1)}, u32[]{:S(2)}, u32[]{:S(2)}) %collective-permute-start.11) | collective-permute-done | bytes 32800 | tf_op jit(solution)/shard_map/ppermute | solution.py:38
  99.6 4.2 %all-to-all-done.2.rows_ref = bf16[8,128,512]{2,1,0:T(8,128)(2,1)S(1)} async-done(((bf16[8,128,512]{2,1,0:T(8,128)(2,1)}), bf16[8,128,512]{2,1,0:T(8,128)(2,1)S(1)}, u32[]{:S(2)}, u32[]{:S(2)}) %all-to-all-start.2) | async-done | bytes 1048608 | tf_op jit(solution)/shard_map/all_to_all | solution.py:203
  103.8 0.5 gradient.2
  104.3 3.5 %collective-permute-start.12 = (bf16[256,512]{1,0:T(8,128)(2,1)S(1)}, bf16[256,512]{1,0:T(8,128)(2,1)S(1)}, u32[]{:S(2)}, u32[]{:S(2)}) collective-permute-start(bf16[256,512]{1,0:T(8,128)(2,1)S(1)} %gradient.2), channel_id=1, source_target_pairs={{0,8},{1,25},{2,10},{3,27},{4,12},{5,29},{6,14},{7,31},{8,16},{9,1... | collective-permute-start | bytes 786440 | tf_op jit(solution)/shard_map/ppermute | solution.py:31
  107.8 0.0 copy-start.9
  107.8 1.9 %collective-permute-start.13 = (f32[4,16,512]{2,1,0:T(8,128)S(1)}, f32[4,16,512]{2,1,0:T(8,128)S(1)}, u32[]{:S(2)}, u32[]{:S(2)}) collective-permute-start(f32[4,16,512]{2,1,0:T(8,128)S(1)} %pad_maximum_fusion.refs_0_), channel_id=1, source_target_pairs={{0,32},{32,64},{64,96},{96,0},{128,160},{160,192},{192,224},{224,1... | collective-permute-start | bytes 393224 | tf_op jit(solution)/shard_map/ppermute | solution.py:38
  109.8 5.3 %collective-permute-start.14 = (f32[4,16,512]{2,1,0:T(8,128)S(1)}, f32[4,16,512]{2,1,0:T(8,128)S(1)}, u32[]{:S(2)}, u32[]{:S(2)}) collective-permute-start(f32[4,16,512]{2,1,0:T(8,128)S(1)} %pad_maximum_fusion.refs_0_), channel_id=1, source_target_pairs={{0,64},{32,96},{64,0},{96,32},{128,192},{160,224},{192,128},{224,1... | collective-permute-start | bytes 393224 | tf_op jit(solution)/shard_map/ppermute | solution.py:38
  115.1 1.9 %collective-permute-start.15 = (f32[4,16,512]{2,1,0:T(8,128)S(1)}, f32[4,16,512]{2,1,0:T(8,128)S(1)}, u32[]{:S(2)}, u32[]{:S(2)}) collective-permute-start(f32[4,16,512]{2,1,0:T(8,128)S(1)} %pad_maximum_fusion.refs_0_), channel_id=1, source_target_pairs={{0,96},{32,0},{64,32},{96,64},{128,224},{160,128},{192,160},{224,1... | collective-permute-start | bytes 393224 | tf_op jit(solution)/shard_map/ppermute | solution.py:38
  117.1 1.0 gradient.3
  118.1 0.0 copy-start.4
  118.1 0.8 copy-done.4
  118.9 5.8 %collective-permute-start.17 = (bf16[256,512]{1,0:T(8,128)(2,1)S(1)}, bf16[256,512]{1,0:T(8,128)(2,1)S(1)}, u32[]{:S(2)}, u32[]{:S(2)}) collective-permute-start(bf16[256,512]{1,0:T(8,128)(2,1)S(1)} %convert_element_type.45), channel_id=1, source_target_pairs={{0,24},{1,9},{2,26},{3,11},{4,28},{5,13},{6,30},{7,15},{8,0},{9,17... | collective-permute-start | bytes 786440 | tf_op jit(solution)/shard_map/ppermute | solution.py:31
  124.7 0.0 collective-permute-done.14.refs_2_
  124.8 0.0 collective-permute-done.15.refs_3_
  124.8 0.1 add_convert_fusion
  124.9 0.5 copy-done.11
  125.4 0.1 copy-done.12
  125.4 0.0 copy-done.13
  125.5 4.9 %collective-permute-start.16 = (bf16[256,512]{1,0:T(8,128)(2,1)S(1)}, bf16[256,512]{1,0:T(8,128)(2,1)S(1)}, u32[]{:S(2)}, u32[]{:S(2)}) collective-permute-start(bf16[256,512]{1,0:T(8,128)(2,1)S(1)} %add_convert_fusion), channel_id=1, source_target_pairs={{0,8},{1,25},{2,10},{3,27},{4,12},{5,29},{6,14},{7,31},{8,16},{9,1... | collective-permute-start | bytes 786440 | tf_op jit(solution)/shard_map/ppermute | solution.py:31
  130.4 2.0 %place_shares.1 = f32[256,512]{1,0:T(8,128)} custom-call(f32[4,16,512]{2,1,0:T(8,128)} %copy-done.9, f32[4,16,512]{2,1,0:T(8,128)} %copy-done.11, f32[4,16,512]{2,1,0:T(8,128)} %copy-done.12, f32[4,16,512]{2,1,0:T(8,128)} %copy-done.13), custom_call_target="tpu_custom_call" | custom-call | tf_op jit(solution)/shard_map/place_shares/pallas_call | solution.py:135
  132.4 0.0 collective-permute-done.17
  132.4 21.4 %collective-permute-done.16 = bf16[256,512]{1,0:T(8,128)(2,1)S(1)} collective-permute-done((bf16[256,512]{1,0:T(8,128)(2,1)S(1)}, bf16[256,512]{1,0:T(8,128)(2,1)S(1)}, u32[]{:S(2)}, u32[]{:S(2)}) %collective-permute-start.16) | collective-permute-done | bytes 262176 | tf_op jit(solution)/shard_map/ppermute | solution.py:31
  153.8 2.4 %fusion.7 = (f32[1,256,512]{2,1,0:T(8,128)}, bf16[1,256,512]{2,1,0:T(8,128)(2,1)}) fusion(f32[1,256,512]{2,1,0:T(8,128)S(1)} %copy-done.7, f32[256,512]{1,0:T(8,128)S(1)} %copy-done.5, bf16[256,512]{1,0:T(8,128)(2,1)S(1)} %collective-permute-done.17, bf16[256,512]{1,0:T(8,128)(2,1)S(1)} %collective-permute-done.16, f32[256,512]{1,0:T(8,128)} %place_shares.1, ...), kind=kLoop, calls=%fused_computation.15 | loop fusion | flops 3014656 | bytes 3670016 | tf_op jit(solution)/shard_map/broadcast_in_dim | solution.py:276
  (31 shorter events, 0.1 us)
Async XLA Ops:
  0.6 30.6 %collective-permute-start.3 = (bf16[256,512]{1,0:T(8,128)(2,1)}, bf16[256,512]{1,0:T(8,128)(2,1)S(1)}, u32[]{:S(2)}, u32[]{:S(2)}) collective-permute-start(bf16[256,512]{1,0:T(8,128)(2,1)} %bitcast.41), channel_id=1, source_target_pairs={{0,8},{1,25},{2,10},{3,27},{4,12},{5,29},{6,14},{7,31},{8,16},{9,1... | collective-permute-start | bytes 786440 | tf_op jit(solution)/shard_map/ppermute | solution.py:31
  13.9 46.4 %collective-permute-start.4 = (bf16[256,512]{1,0:T(8,128)(2,1)}, bf16[256,512]{1,0:T(8,128)(2,1)S(1)}, u32[]{:S(2)}, u32[]{:S(2)}) collective-permute-start(bf16[256,512]{1,0:T(8,128)(2,1)} %bitcast.42), channel_id=1, source_target_pairs={{0,24},{1,9},{2,26},{3,11},{4,28},{5,13},{6,30},{7,15},{8,0},{9,17... | collective-permute-start | bytes 786440 | tf_op jit(solution)/shard_map/ppermute | solution.py:31
  15.9 1.0 copy-start
  16.8 1.6 %copy-start.2 = (bf16[1,128,8192]{2,1,0:T(8,128)(2,1)S(1)}, bf16[1,128,8192]{2,1,0:T(8,128)(2,1)}, u32[]{:S(2)}) copy-start(bf16[1,128,8192]{2,1,0:T(8,128)(2,1)} %param.13) | copy-start | bytes 6291460
  19.1 1.4 copy-start.3
  20.4 0.6 copy-start.6
  21.0 39.2 %all-to-all-start = ((bf16[8,128,1024]{2,1,0:T(8,128)(2,1)}), bf16[8,128,1024]{2,1,0:T(8,128)(2,1)S(1)}, u32[]{:S(2)}, u32[]{:S(2)}) async-start(bf16[8,128,1024]{2,1,0:T(8,128)(2,1)} %copy-done.3), calls=%async_computation | async-start | bytes 4194304 | tf_op jit(solution)/shard_map/all_to_all | solution.py:203
  26.3 34.0 %copy-start.1 = (bf16[1,256,512]{2,1,0:T(8,128)(2,1)S(1)}, bf16[1,256,512]{2,1,0:T(8,128)(2,1)}, u32[]{:S(2)}) copy-start(bf16[1,256,512]{2,1,0:T(8,128)(2,1)} %param.8) | copy-start | bytes 786436
  31.3 29.0 %collective-permute-start.5 = (bf16[256,512]{1,0:T(8,128)(2,1)S(1)}, bf16[256,512]{1,0:T(8,128)(2,1)S(1)}, u32[]{:S(2)}, u32[]{:S(2)}) collective-permute-start(bf16[256,512]{1,0:T(8,128)(2,1)S(1)} %collective-permute-done.3.w1_ref), channel_id=1, source_target_pairs={{0,8},{1,25},{2,10},{3,27},{4,12},{5,29},{6,14},{7,31},{8,16},{9,1... | collective-permute-start | bytes 786440 | tf_op jit(solution)/shard_map/ppermute | solution.py:31
  44.3 11.0 %collective-permute-start = (bf16[4,16,512]{2,1,0:T(8,128)(2,1)S(1)}, bf16[4,16,512]{2,1,0:T(8,128)(2,1)S(1)}, u32[]{:S(2)}, u32[]{:S(2)}) collective-permute-start(bf16[4,16,512]{2,1,0:T(8,128)(2,1)S(1)} %get-tuple-element.42), channel_id=1, source_target_pairs={{0,32},{32,64},{64,96},{96,0},{128,160},{160,192},{192,224},{224,1... | collective-permute-start | bytes 196616 | tf_op jit(solution)/shard_map/ppermute | solution.py:38
  47.7 7.5 %collective-permute-start.1 = (bf16[4,16,512]{2,1,0:T(8,128)(2,1)S(1)}, bf16[4,16,512]{2,1,0:T(8,128)(2,1)S(1)}, u32[]{:S(2)}, u32[]{:S(2)}) collective-permute-start(bf16[4,16,512]{2,1,0:T(8,128)(2,1)S(1)} %get-tuple-element.43), channel_id=1, source_target_pairs={{0,64},{32,96},{64,0},{96,32},{128,192},{160,224},{192,128},{224,1... | collective-permute-start | bytes 196616 | tf_op jit(solution)/shard_map/ppermute | solution.py:38
  52.3 5.8 %collective-permute-start.2 = (bf16[4,16,512]{2,1,0:T(8,128)(2,1)S(1)}, bf16[4,16,512]{2,1,0:T(8,128)(2,1)S(1)}, u32[]{:S(2)}, u32[]{:S(2)}) collective-permute-start(bf16[4,16,512]{2,1,0:T(8,128)(2,1)S(1)} %get-tuple-element.44), channel_id=1, source_target_pairs={{0,96},{32,0},{64,32},{96,64},{128,224},{160,128},{192,160},{224,1... | collective-permute-start | bytes 196616 | tf_op jit(solution)/shard_map/ppermute | solution.py:38
  55.3 2.8 %copy-start.15 = (bf16[4,16,512]{2,1,0:T(8,128)(2,1)}, bf16[4,16,512]{2,1,0:T(8,128)(2,1)S(1)}, u32[]{:S(2)}) copy-start(bf16[4,16,512]{2,1,0:T(8,128)(2,1)S(1)} %collective-permute-done.refs_1_) | copy-start | bytes 196612
  55.3 2.8 %copy-start.16 = (bf16[4,16,512]{2,1,0:T(8,128)(2,1)}, bf16[4,16,512]{2,1,0:T(8,128)(2,1)S(1)}, u32[]{:S(2)}) copy-start(bf16[4,16,512]{2,1,0:T(8,128)(2,1)S(1)} %collective-permute-done.1.refs_2_) | copy-start | bytes 196612
  58.1 0.6 copy-start.17
  62.6 20.3 %copy-start.10 = (bf16[1,128,512]{2,1,0:T(8,128)(2,1)S(1)}, bf16[1,128,512]{2,1,0:T(8,128)(2,1)}, u32[]{:S(2)}) copy-start(bf16[1,128,512]{2,1,0:T(8,128)(2,1)} %param.14) | copy-start | bytes 393220
  62.6 20.3 %copy-start.18 = (f32[1,128]{1,0:T(1,128)S(1)}, f32[1,128]{1,0:T(1,128)}, u32[]{:S(2)}) copy-start(f32[1,128]{1,0:T(1,128)} %mask.1) | copy-start | bytes 1540
  62.6 20.1 %all-to-all-start.1 = ((bf16[8,128,512]{2,1,0:T(8,128)(2,1)}), bf16[8,128,512]{2,1,0:T(8,128)(2,1)S(1)}, u32[]{:S(2)}, u32[]{:S(2)}) async-start(bf16[8,128,512]{2,1,0:T(8,128)(2,1)} %project.1), calls=%async_computation.1 | async-start | bytes 2097152 | tf_op jit(solution)/shard_map/all_to_all | solution.py:203
  67.6 7.6 %collective-permute-start.8 = (f32[16,512]{1,0:T(8,128)}, f32[16,512]{1,0:T(8,128)S(1)}, u32[]{:S(2)}, u32[]{:S(2)}) collective-permute-start(f32[16,512]{1,0:T(8,128)} %get-tuple-element.60), channel_id=1, source_target_pairs={{0,384},{32,416},{64,448},{96,480},{128,0},{160,32},{192,64},{224,... | collective-permute-start | bytes 98312 | tf_op jit(solution)/shard_map/ppermute | solution.py:38
  71.1 6.1 %collective-permute-start.7 = (f32[16,512]{1,0:T(8,128)}, f32[16,512]{1,0:T(8,128)S(1)}, u32[]{:S(2)}, u32[]{:S(2)}) collective-permute-start(f32[16,512]{1,0:T(8,128)} %get-tuple-element.59), channel_id=1, source_target_pairs={{0,256},{32,288},{64,320},{96,352},{128,384},{160,416},{192,448},{... | collective-permute-start | bytes 98312 | tf_op jit(solution)/shard_map/ppermute | solution.py:38
  73.0 6.7 %collective-permute-start.6 = (f32[16,512]{1,0:T(8,128)}, f32[16,512]{1,0:T(8,128)S(1)}, u32[]{:S(2)}, u32[]{:S(2)}) collective-permute-start(f32[16,512]{1,0:T(8,128)} %get-tuple-element.58), channel_id=1, source_target_pairs={{0,128},{32,160},{64,192},{96,224},{128,256},{160,288},{192,320},{... | collective-permute-start | bytes 98312 | tf_op jit(solution)/shard_map/ppermute | solution.py:38
  82.8 5.9 %copy-start.14 = (f32[16,512]{1,0:T(8,128)S(1)}, f32[16,512]{1,0:T(8,128)}, u32[]{:S(2)}) copy-start(f32[16,512]{1,0:T(8,128)} %get-tuple-element.64) | copy-start | bytes 98308
  84.1 19.7 %all-to-all-start.2 = ((bf16[8,128,512]{2,1,0:T(8,128)(2,1)}), bf16[8,128,512]{2,1,0:T(8,128)(2,1)S(1)}, u32[]{:S(2)}, u32[]{:S(2)}) async-start(bf16[8,128,512]{2,1,0:T(8,128)(2,1)} %broadcast_in_dim.15), calls=%async_computation.2 | async-start | bytes 2097152 | tf_op jit(solution)/shard_map/all_to_all | solution.py:203
  88.7 9.0 %collective-permute-start.9 = (f32[16,512]{1,0:T(8,128)S(1)}, f32[16,512]{1,0:T(8,128)S(1)}, u32[]{:S(2)}, u32[]{:S(2)}) collective-permute-start(f32[16,512]{1,0:T(8,128)S(1)} %copy-done.14), channel_id=1, source_target_pairs={{0,128},{32,160},{64,192},{96,224},{128,256},{160,288},{192,320},{... | collective-permute-start | bytes 98312 | tf_op jit(solution)/shard_map/ppermute | solution.py:38
  90.6 7.1 %collective-permute-start.10 = (f32[16,512]{1,0:T(8,128)S(1)}, f32[16,512]{1,0:T(8,128)S(1)}, u32[]{:S(2)}, u32[]{:S(2)}) collective-permute-start(f32[16,512]{1,0:T(8,128)S(1)} %copy-done.14), channel_id=1, source_target_pairs={{0,256},{32,288},{64,320},{96,352},{128,384},{160,416},{192,448},{... | collective-permute-start | bytes 98312 | tf_op jit(solution)/shard_map/ppermute | solution.py:38
  94.1 5.5 %collective-permute-start.11 = (f32[16,512]{1,0:T(8,128)S(1)}, f32[16,512]{1,0:T(8,128)S(1)}, u32[]{:S(2)}, u32[]{:S(2)}) collective-permute-start(f32[16,512]{1,0:T(8,128)S(1)} %copy-done.14), channel_id=1, source_target_pairs={{0,384},{32,416},{64,448},{96,480},{128,0},{160,32},{192,64},{224,... | collective-permute-start | bytes 98312 | tf_op jit(solution)/shard_map/ppermute | solution.py:38
  104.3 20.5 %collective-permute-start.12 = (bf16[256,512]{1,0:T(8,128)(2,1)S(1)}, bf16[256,512]{1,0:T(8,128)(2,1)S(1)}, u32[]{:S(2)}, u32[]{:S(2)}) collective-permute-start(bf16[256,512]{1,0:T(8,128)(2,1)S(1)} %gradient.2), channel_id=1, source_target_pairs={{0,8},{1,25},{2,10},{3,27},{4,12},{5,29},{6,14},{7,31},{8,16},{9,1... | collective-permute-start | bytes 786440 | tf_op jit(solution)/shard_map/ppermute | solution.py:31
  107.8 17.0 %copy-start.9 = (f32[4,16,512]{2,1,0:T(8,128)}, f32[4,16,512]{2,1,0:T(8,128)S(1)}, u32[]{:S(2)}) copy-start(f32[4,16,512]{2,1,0:T(8,128)S(1)} %pad_maximum_fusion.refs_0_) | copy-start | bytes 393220
  107.8 16.9 %collective-permute-start.13 = (f32[4,16,512]{2,1,0:T(8,128)S(1)}, f32[4,16,512]{2,1,0:T(8,128)S(1)}, u32[]{:S(2)}, u32[]{:S(2)}) collective-permute-start(f32[4,16,512]{2,1,0:T(8,128)S(1)} %pad_maximum_fusion.refs_0_), channel_id=1, source_target_pairs={{0,32},{32,64},{64,96},{96,0},{128,160},{160,192},{192,224},{224,1... | collective-permute-start | bytes 393224 | tf_op jit(solution)/shard_map/ppermute | solution.py:38
  109.8 15.0 %collective-permute-start.14 = (f32[4,16,512]{2,1,0:T(8,128)S(1)}, f32[4,16,512]{2,1,0:T(8,128)S(1)}, u32[]{:S(2)}, u32[]{:S(2)}) collective-permute-start(f32[4,16,512]{2,1,0:T(8,128)S(1)} %pad_maximum_fusion.refs_0_), channel_id=1, source_target_pairs={{0,64},{32,96},{64,0},{96,32},{128,192},{160,224},{192,128},{224,1... | collective-permute-start | bytes 393224 | tf_op jit(solution)/shard_map/ppermute | solution.py:38
  115.1 9.6 %collective-permute-start.15 = (f32[4,16,512]{2,1,0:T(8,128)S(1)}, f32[4,16,512]{2,1,0:T(8,128)S(1)}, u32[]{:S(2)}, u32[]{:S(2)}) collective-permute-start(f32[4,16,512]{2,1,0:T(8,128)S(1)} %pad_maximum_fusion.refs_0_), channel_id=1, source_target_pairs={{0,96},{32,0},{64,32},{96,64},{128,224},{160,128},{192,160},{224,1... | collective-permute-start | bytes 393224 | tf_op jit(solution)/shard_map/ppermute | solution.py:38
  118.1 0.8 copy-start.4
  118.9 34.9 %copy-start.7 = (f32[1,256,512]{2,1,0:T(8,128)S(1)}, f32[1,256,512]{2,1,0:T(8,128)}, u32[]{:S(2)}) copy-start(f32[1,256,512]{2,1,0:T(8,128)} %param.9) | copy-start | bytes 1572868
  118.9 34.9 %copy-start.8 = (f32[1,256,512]{2,1,0:T(8,128)S(1)}, f32[1,256,512]{2,1,0:T(8,128)}, u32[]{:S(2)}) copy-start(f32[1,256,512]{2,1,0:T(8,128)} %param.10) | copy-start | bytes 1572868
  118.9 34.9 %copy-start.5 = (f32[256,512]{1,0:T(8,128)S(1)}, f32[256,512]{1,0:T(8,128)}, u32[]{:S(2)}) copy-start(f32[256,512]{1,0:T(8,128)} %copy-done.4) | copy-start | bytes 1572868
  118.9 13.5 %collective-permute-start.17 = (bf16[256,512]{1,0:T(8,128)(2,1)S(1)}, bf16[256,512]{1,0:T(8,128)(2,1)S(1)}, u32[]{:S(2)}, u32[]{:S(2)}) collective-permute-start(bf16[256,512]{1,0:T(8,128)(2,1)S(1)} %convert_element_type.45), channel_id=1, source_target_pairs={{0,24},{1,9},{2,26},{3,11},{4,28},{5,13},{6,30},{7,15},{8,0},{9,17... | collective-permute-start | bytes 786440 | tf_op jit(solution)/shard_map/ppermute | solution.py:31
  124.7 0.6 copy-start.11
  124.7 0.7 copy-start.12
  124.8 0.7 copy-start.13
  125.5 28.3 %collective-permute-start.16 = (bf16[256,512]{1,0:T(8,128)(2,1)S(1)}, bf16[256,512]{1,0:T(8,128)(2,1)S(1)}, u32[]{:S(2)}, u32[]{:S(2)}) collective-permute-start(bf16[256,512]{1,0:T(8,128)(2,1)S(1)} %add_convert_fusion), channel_id=1, source_target_pairs={{0,8},{1,25},{2,10},{3,27},{4,12},{5,29},{6,14},{7,31},{8,16},{9,1... | collective-permute-start | bytes 786440 | tf_op jit(solution)/shard_map/ppermute | solution.py:31

commit v5 on v4

--- a/solution.py
+++ b/solution.py
@@ -227,11 +227,11 @@
     packed, shares = pack(tokens, initial)
     columns = to_plane(packed).reshape(PLANE * rows, SLABS * width)
     shares[1:] = [shift_replica(shares[i], 0, i) for i in (1, 2, 3)]
+
+    previous, following = shift_ring(initial, 1), shift_ring(initial, -1)
+    previous, mask, *shares[1:3] = lax.optimization_barrier((previous, mask, *shares[1:3]))
+    opposite = shift_ring(previous, 1)
     sums = add_shares(shares)
-
-    previous, following = shift_ring(initial, 1), shift_ring(initial, -1)
-    previous, mask = lax.optimization_barrier((previous, mask))
-    opposite = shift_ring(previous, 1)
     columns, *sums = lax.optimization_barrier((columns, *sums))
     partials = list(project(columns, (initial, previous, following, opposite)))
 
@@ -260,7 +260,7 @@
     near = gradient_of(columns, received, (0, 1, 2), width, part_width, jnp.float32)
     shared = jnp.stack(shared)
     shared = [shared] + [shift_replica(shared, 0, i) for i in (1, 2, 3)]
-    gradient, shared = scatter_ring((*near, far), shared)
+    gradient, shared[:3] = scatter_ring((*near, far), shared[:3])
     block_anchor = place_shares(shared)
 
     weight_f = initial.astype(jnp.float32)

time: 157 us -> 152 us (0.968)
  waiting for transfers between devices: 40.1 us -> 31.7 us
  starting transfers between devices: 94.1 us -> 97.7 us
    ppermute x6, waiting for transfers between devices: 25.2 us -> 15.4 us  [shift_ring(): return lax.ppermute(value, 'fsdp', pairs)]
    ppermute x12, starting transfers between devices: 36.7 us -> 42.5 us  [shift_replica(): return lax.ppermute(value, 'replica', pairs)]
    ppermute x6, starting transfers between devices: 42.5 us -> 39.3 us  [shift_ring(): return lax.ppermute(value, 'fsdp', pairs)]
    ppermute x12, waiting for transfers between devices: 9.08 us -> 12 us  [shift_replica(): return lax.ppermute(value, 'replica', pairs)]
    all_to_all x3, waiting for transfers between devices: 5.83 us -> 4.23 us  [to_plane(): return lax.all_to_all(value, 'fsdp', 0, 0, axis_index_groups=PLANES)]
  transfers between devices with their start and end apart: 21 -> 21, of which waited for: 8 -> 10; matrix products, arithmetic and copies ran while one was open for 1% -> 1% of each run, Pallas kernels for 4% -> 4%
where the time goes in v5:
time: 152 us; the launch traced here: 151 us
  starting transfers between devices  97.7 us (64%)
  waiting for transfers between devices  31.7 us (21%)
  Pallas kernels  9.06 us (6%)
  local copies, waits for them, and re-layouts  7.69 us (5%)
  other arithmetic  4.18 us (3%)
    ppermute x12, starting transfers between devices, shift_replica(): return lax.ppermute(value, 'replica', pairs)  42.5 us
    ppermute x6, starting transfers between devices, shift_ring(): return lax.ppermute(value, 'fsdp', pairs)  39.3 us
    all_to_all x3, starting transfers between devices, to_plane(): return lax.all_to_all(value, 'fsdp', 0, 0, axis_index_groups=PLANES)  15.9 us
    ppermute x6, waiting for transfers between devices, shift_ring(): return lax.ppermute(value, 'fsdp', pairs)  15.4 us
    ppermute x12, waiting for transfers between devices, shift_replica(): return lax.ppermute(value, 'replica', pairs)  12 us
    unnamed x38, local copies, waits for them, and re-layouts  6.61 us
    all_to_all x3, waiting for transfers between devices, to_plane(): return lax.all_to_all(value, 'fsdp', 0, 0, axis_index_groups=PLANES)  4.23 us
  transfers between devices with their start and end apart: 21, of which 10 were waited for; matrix products, arithmetic and copies ran while one was open for 1% of the time, Pallas kernels for 4%

profile of v5, /device:TPU:1, one launch (start us, length us, event | category | flops | bytes accessed | tf_op | source)
XLA Modules:
  0.0 151.3 jit_solution(4748293179533683908)
XLA Ops:
  0.6 13.3 %collective-permute-start = (bf16[256,512]{1,0:T(8,128)(2,1)}, bf16[256,512]{1,0:T(8,128)(2,1)S(1)}, u32[]{:S(2)}, u32[]{:S(2)}) collective-permute-start(bf16[256,512]{1,0:T(8,128)(2,1)} %bitcast.41), channel_id=1, source_target_pairs={{0,8},{1,25},{2,10},{3,27},{4,12},{5,29},{6,14},{7,31},{8,16},{9,1... | collective-permute-start | bytes 786440 | tf_op jit(solution)/shard_map/ppermute | solution.py:31
  13.9 1.9 %collective-permute-start.4 = (bf16[256,512]{1,0:T(8,128)(2,1)}, bf16[256,512]{1,0:T(8,128)(2,1)S(1)}, u32[]{:S(2)}, u32[]{:S(2)}) collective-permute-start(bf16[256,512]{1,0:T(8,128)(2,1)} %bitcast.42), channel_id=1, source_target_pairs={{0,24},{1,9},{2,26},{3,11},{4,28},{5,13},{6,30},{7,15},{8,0},{9,17... | collective-permute-start | bytes 786440 | tf_op jit(solution)/shard_map/ppermute | solution.py:31
  15.9 0.0 copy-start
  15.9 0.9 copy-done
  16.8 1.6 %copy-done.2 = bf16[1,128,8192]{2,1,0:T(8,128)(2,1)S(1)} copy-done((bf16[1,128,8192]{2,1,0:T(8,128)(2,1)S(1)}, bf16[1,128,8192]{2,1,0:T(8,128)(2,1)}, u32[]{:S(2)}) %copy-start.2) | copy-done | bytes 2097176
  18.4 0.6 pack_columns.1
  19.1 1.3 copy-done.3
  20.4 0.6 copy-done.6
  21.0 5.3 %all-to-all-start = ((bf16[8,128,1024]{2,1,0:T(8,128)(2,1)}), bf16[8,128,1024]{2,1,0:T(8,128)(2,1)S(1)}, u32[]{:S(2)}, u32[]{:S(2)}) async-start(bf16[8,128,1024]{2,1,0:T(8,128)(2,1)} %copy-done.3), calls=%async_computation | async-start | bytes 4194304 | tf_op jit(solution)/shard_map/all_to_all | solution.py:203
  26.3 3.2 %collective-permute-start.1 = (bf16[4,16,512]{2,1,0:T(8,128)(2,1)S(1)}, bf16[4,16,512]{2,1,0:T(8,128)(2,1)S(1)}, u32[]{:S(2)}, u32[]{:S(2)}) collective-permute-start(bf16[4,16,512]{2,1,0:T(8,128)(2,1)S(1)} %get-tuple-element.43), channel_id=1, source_target_pairs={{0,32},{32,64},{64,96},{96,0},{128,160},{160,192},{192,224},{224,1... | collective-permute-start | bytes 196616 | tf_op jit(solution)/shard_map/ppermute | solution.py:38
  29.5 0.0 copy-start.1
  29.5 4.7 %collective-permute-start.2 = (bf16[4,16,512]{2,1,0:T(8,128)(2,1)S(1)}, bf16[4,16,512]{2,1,0:T(8,128)(2,1)S(1)}, u32[]{:S(2)}, u32[]{:S(2)}) collective-permute-start(bf16[4,16,512]{2,1,0:T(8,128)(2,1)S(1)} %get-tuple-element.44), channel_id=1, source_target_pairs={{0,64},{32,96},{64,0},{96,32},{128,192},{160,224},{192,128},{224,1... | collective-permute-start | bytes 196616 | tf_op jit(solution)/shard_map/ppermute | solution.py:38
  34.2 1.2 mask.1
  35.3 0.0 collective-permute-done.1.refs_1_
  35.3 0.8 collective-permute-done.2.refs_2_
  36.1 0.0 collective-permute-done.w1_ref
  36.2 8.1 %collective-permute-start.5 = (bf16[256,512]{1,0:T(8,128)(2,1)S(1)}, bf16[256,512]{1,0:T(8,128)(2,1)S(1)}, u32[]{:S(2)}, u32[]{:S(2)}) collective-permute-start(bf16[256,512]{1,0:T(8,128)(2,1)S(1)} %collective-permute-done.w1_ref), channel_id=1, source_target_pairs={{0,8},{1,25},{2,10},{3,27},{4,12},{5,29},{6,14},{7,31},{8,16},{9,1... | collective-permute-start | bytes 786440 | tf_op jit(solution)/shard_map/ppermute | solution.py:31
  44.3 4.9 %collective-permute-start.3 = (bf16[4,16,512]{2,1,0:T(8,128)(2,1)S(1)}, bf16[4,16,512]{2,1,0:T(8,128)(2,1)S(1)}, u32[]{:S(2)}, u32[]{:S(2)}) collective-permute-start(bf16[4,16,512]{2,1,0:T(8,128)(2,1)S(1)} %get-tuple-element.47), channel_id=1, source_target_pairs={{0,96},{32,0},{64,32},{96,64},{128,224},{160,128},{192,160},{224,1... | collective-permute-start | bytes 196616 | tf_op jit(solution)/shard_map/ppermute | solution.py:38
  49.2 1.5 %collective-permute-done.3.refs_3_ = bf16[4,16,512]{2,1,0:T(8,128)(2,1)S(1)} collective-permute-done((bf16[4,16,512]{2,1,0:T(8,128)(2,1)S(1)}, bf16[4,16,512]{2,1,0:T(8,128)(2,1)S(1)}, u32[]{:S(2)}, u32[]{:S(2)}) %collective-permute-start.3) | collective-permute-done | bytes 65568 | tf_op jit(solution)/shard_map/ppermute | solution.py:38
  50.7 0.6 copy-done.17
  51.3 1.6 %add_shares.1 = (f32[16,512]{1,0:T(8,128)}, f32[16,512]{1,0:T(8,128)}, f32[16,512]{1,0:T(8,128)}, f32[16,512]{1,0:T(8,128)}) custom-call(bf16[4,16,512]{2,1,0:T(8,128)(2,1)} %copy-done.6, bf16[4,16,512]{2,1,0:T(8,128)(2,1)} %copy-done.15, bf16[4,16,512]{2,1,0:T(8,128)(2,1)} %copy-done.16, bf16[4,16,512]{2,1,0:T(8,128)(2,1)} %copy-done.17), custom_call_target="tpu_custom_call" | custom-call | tf_op jit(solution)/shard_map/add_shares/pallas_call | solution.py:116
  52.9 0.0 all-to-all-done
  52.9 0.0 collective-permute-done.4.w2_ref
  52.9 3.0 %collective-permute-done.5.w3_ref = bf16[256,512]{1,0:T(8,128)(2,1)S(1)} collective-permute-done((bf16[256,512]{1,0:T(8,128)(2,1)S(1)}, bf16[256,512]{1,0:T(8,128)(2,1)S(1)}, u32[]{:S(2)}, u32[]{:S(2)}) %collective-permute-start.5) | collective-permute-done | bytes 262176 | tf_op jit(solution)/shard_map/ppermute | solution.py:31
  55.9 2.2 %project.1 = bf16[8,128,512]{2,1,0:T(8,128)(2,1)} custom-call(bf16[1024,1024]{1,0:T(8,128)(2,1)S(1)} %bitcast.38, bf16[256,512]{1,0:T(8,128)(2,1)S(1)} %bitcast.44, bf16[256,512]{1,0:T(8,128)(2,1)S(1)} %collective-permute-done.w1_ref, bf16[256,512]{1,0:T(8,128)(2,1)S(1)} %collective-permute-done.4.w2_ref, bf16[256,512]{1,0:T(8,128)(2,1)S(1)} %collective-permute-done.5.w3_ref), custom_call_target="tpu_custom_call" | custom-call | tf_op jit(solution)/shard_map/project/pallas_call | solution.py:172
  58.2 4.7 %all-to-all-start.1 = ((bf16[8,128,512]{2,1,0:T(8,128)(2,1)}), bf16[8,128,512]{2,1,0:T(8,128)(2,1)S(1)}, u32[]{:S(2)}, u32[]{:S(2)}) async-start(bf16[8,128,512]{2,1,0:T(8,128)(2,1)} %project.1), calls=%async_computation.1 | async-start | bytes 2097152 | tf_op jit(solution)/shard_map/all_to_all | solution.py:203
  62.9 6.1 %collective-permute-start.8 = (f32[16,512]{1,0:T(8,128)}, f32[16,512]{1,0:T(8,128)S(1)}, u32[]{:S(2)}, u32[]{:S(2)}) collective-permute-start(f32[16,512]{1,0:T(8,128)} %get-tuple-element.63), channel_id=1, source_target_pairs={{0,384},{32,416},{64,448},{96,480},{128,0},{160,32},{192,64},{224,... | collective-permute-start | bytes 98312 | tf_op jit(solution)/shard_map/ppermute | solution.py:38
  69.0 1.9 %collective-permute-start.7 = (f32[16,512]{1,0:T(8,128)}, f32[16,512]{1,0:T(8,128)S(1)}, u32[]{:S(2)}, u32[]{:S(2)}) collective-permute-start(f32[16,512]{1,0:T(8,128)} %get-tuple-element.62), channel_id=1, source_target_pairs={{0,256},{32,288},{64,320},{96,352},{128,384},{160,416},{192,448},{... | collective-permute-start | bytes 98312 | tf_op jit(solution)/shard_map/ppermute | solution.py:38
  70.9 2.2 %collective-permute-start.6 = (f32[16,512]{1,0:T(8,128)}, f32[16,512]{1,0:T(8,128)S(1)}, u32[]{:S(2)}, u32[]{:S(2)}) collective-permute-start(f32[16,512]{1,0:T(8,128)} %get-tuple-element.61), channel_id=1, source_target_pairs={{0,128},{32,160},{64,192},{96,224},{128,256},{160,288},{192,320},{... | collective-permute-start | bytes 98312 | tf_op jit(solution)/shard_map/ppermute | solution.py:38
  73.1 0.0 collective-permute-done.8
  73.1 1.6 %collective-permute-done.7 = f32[16,512]{1,0:T(8,128)S(1)} collective-permute-done((f32[16,512]{1,0:T(8,128)}, f32[16,512]{1,0:T(8,128)S(1)}, u32[]{:S(2)}, u32[]{:S(2)}) %collective-permute-start.7) | collective-permute-done | bytes 32800 | tf_op jit(solution)/shard_map/ppermute | solution.py:38
  74.7 3.1 %collective-permute-done.6 = f32[16,512]{1,0:T(8,128)S(1)} collective-permute-done((f32[16,512]{1,0:T(8,128)}, f32[16,512]{1,0:T(8,128)S(1)}, u32[]{:S(2)}, u32[]{:S(2)}) %collective-permute-start.6) | collective-permute-done | bytes 32800 | tf_op jit(solution)/shard_map/ppermute | solution.py:38
  77.8 1.4 multiply_subtract_fusion
  79.3 0.1 convert_reduce_fusion
  79.4 0.0 copy-start.14
  79.5 0.1 fusion.12
  79.6 1.1 broadcast_in_dim.15
  80.7 5.9 %all-to-all-start.2 = ((bf16[8,128,512]{2,1,0:T(8,128)(2,1)}), bf16[8,128,512]{2,1,0:T(8,128)(2,1)S(1)}, u32[]{:S(2)}, u32[]{:S(2)}) async-start(bf16[8,128,512]{2,1,0:T(8,128)(2,1)} %broadcast_in_dim.15), calls=%async_computation.2 | async-start | bytes 2097152 | tf_op jit(solution)/shard_map/all_to_all | solution.py:203
  86.6 1.9 %collective-permute-start.9 = (f32[16,512]{1,0:T(8,128)S(1)}, f32[16,512]{1,0:T(8,128)S(1)}, u32[]{:S(2)}, u32[]{:S(2)}) collective-permute-start(f32[16,512]{1,0:T(8,128)S(1)} %copy-done.14), channel_id=1, source_target_pairs={{0,128},{32,160},{64,192},{96,224},{128,256},{160,288},{192,320},{... | collective-permute-start | bytes 98312 | tf_op jit(solution)/shard_map/ppermute | solution.py:38
  88.5 3.4 %collective-permute-start.10 = (f32[16,512]{1,0:T(8,128)S(1)}, f32[16,512]{1,0:T(8,128)S(1)}, u32[]{:S(2)}, u32[]{:S(2)}) collective-permute-start(f32[16,512]{1,0:T(8,128)S(1)} %copy-done.14), channel_id=1, source_target_pairs={{0,256},{32,288},{64,320},{96,352},{128,384},{160,416},{192,448},{... | collective-permute-start | bytes 98312 | tf_op jit(solution)/shard_map/ppermute | solution.py:38
  92.0 3.6 %collective-permute-start.11 = (f32[16,512]{1,0:T(8,128)S(1)}, f32[16,512]{1,0:T(8,128)S(1)}, u32[]{:S(2)}, u32[]{:S(2)}) collective-permute-start(f32[16,512]{1,0:T(8,128)S(1)} %copy-done.14), channel_id=1, source_target_pairs={{0,384},{32,416},{64,448},{96,480},{128,0},{160,32},{192,64},{224,... | collective-permute-start | bytes 98312 | tf_op jit(solution)/shard_map/ppermute | solution.py:38
  95.6 0.0 collective-permute-done.10
  95.6 1.8 %collective-permute-done.11 = f32[16,512]{1,0:T(8,128)S(1)} collective-permute-done((f32[16,512]{1,0:T(8,128)S(1)}, f32[16,512]{1,0:T(8,128)S(1)}, u32[]{:S(2)}, u32[]{:S(2)}) %collective-permute-start.11) | collective-permute-done | bytes 32800 | tf_op jit(solution)/shard_map/ppermute | solution.py:38
  97.5 4.2 %all-to-all-done.2.rows_ref = bf16[8,128,512]{2,1,0:T(8,128)(2,1)S(1)} async-done(((bf16[8,128,512]{2,1,0:T(8,128)(2,1)}), bf16[8,128,512]{2,1,0:T(8,128)(2,1)S(1)}, u32[]{:S(2)}, u32[]{:S(2)}) %all-to-all-start.2) | async-done | bytes 1048608 | tf_op jit(solution)/shard_map/all_to_all | solution.py:203
  101.7 0.5 gradient.2
  102.2 7.5 %collective-permute-start.12 = (bf16[256,512]{1,0:T(8,128)(2,1)S(1)}, bf16[256,512]{1,0:T(8,128)(2,1)S(1)}, u32[]{:S(2)}, u32[]{:S(2)}) collective-permute-start(bf16[256,512]{1,0:T(8,128)(2,1)S(1)} %gradient.2), channel_id=1, source_target_pairs={{0,8},{1,25},{2,10},{3,27},{4,12},{5,29},{6,14},{7,31},{8,16},{9,1... | collective-permute-start | bytes 786440 | tf_op jit(solution)/shard_map/ppermute | solution.py:31
  109.7 0.0 copy-start.9
  109.7 3.2 %collective-permute-start.13 = (f32[4,16,512]{2,1,0:T(8,128)S(1)}, f32[4,16,512]{2,1,0:T(8,128)S(1)}, u32[]{:S(2)}, u32[]{:S(2)}) collective-permute-start(f32[4,16,512]{2,1,0:T(8,128)S(1)} %pad_maximum_fusion.refs_0_), channel_id=1, source_target_pairs={{0,32},{32,64},{64,96},{96,0},{128,160},{160,192},{192,224},{224,1... | collective-permute-start | bytes 393224 | tf_op jit(solution)/shard_map/ppermute | solution.py:38
  112.9 3.6 %collective-permute-start.14 = (f32[4,16,512]{2,1,0:T(8,128)S(1)}, f32[4,16,512]{2,1,0:T(8,128)S(1)}, u32[]{:S(2)}, u32[]{:S(2)}) collective-permute-start(f32[4,16,512]{2,1,0:T(8,128)S(1)} %pad_maximum_fusion.refs_0_), channel_id=1, source_target_pairs={{0,64},{32,96},{64,0},{96,32},{128,192},{160,224},{192,128},{224,1... | collective-permute-start | bytes 393224 | tf_op jit(solution)/shard_map/ppermute | solution.py:38
  116.6 1.0 gradient.3
  117.6 0.0 copy-start.4
  117.6 0.8 copy-done.4
  118.4 2.1 %collective-permute-start.17 = (bf16[256,512]{1,0:T(8,128)(2,1)S(1)}, bf16[256,512]{1,0:T(8,128)(2,1)S(1)}, u32[]{:S(2)}, u32[]{:S(2)}) collective-permute-start(bf16[256,512]{1,0:T(8,128)(2,1)S(1)} %convert_element_type.45), channel_id=1, source_target_pairs={{0,24},{1,9},{2,26},{3,11},{4,28},{5,13},{6,30},{7,15},{8,0},{9,17... | collective-permute-start | bytes 786440 | tf_op jit(solution)/shard_map/ppermute | solution.py:31
  120.5 0.9 collective-permute-done.14.refs_2_
  121.4 0.0 collective-permute-done.12
  121.4 0.1 add_convert_fusion
  121.5 6.4 %collective-permute-start.16 = (bf16[256,512]{1,0:T(8,128)(2,1)S(1)}, bf16[256,512]{1,0:T(8,128)(2,1)S(1)}, u32[]{:S(2)}, u32[]{:S(2)}) collective-permute-start(bf16[256,512]{1,0:T(8,128)(2,1)S(1)} %add_convert_fusion), channel_id=1, source_target_pairs={{0,8},{1,25},{2,10},{3,27},{4,12},{5,29},{6,14},{7,31},{8,16},{9,1... | collective-permute-start | bytes 786440 | tf_op jit(solution)/shard_map/ppermute | solution.py:31
  127.9 3.8 %collective-permute-start.15 = (f32[4,16,512]{2,1,0:T(8,128)S(1)}, f32[4,16,512]{2,1,0:T(8,128)S(1)}, u32[]{:S(2)}, u32[]{:S(2)}) collective-permute-start(f32[4,16,512]{2,1,0:T(8,128)S(1)} %pad_maximum_fusion.refs_0_), channel_id=1, source_target_pairs={{0,96},{32,0},{64,32},{96,64},{128,224},{160,128},{192,160},{224,1... | collective-permute-start | bytes 393224 | tf_op jit(solution)/shard_map/ppermute | solution.py:38
  131.7 2.2 %collective-permute-done.15.refs_3_ = f32[4,16,512]{2,1,0:T(8,128)S(1)} collective-permute-done((f32[4,16,512]{2,1,0:T(8,128)S(1)}, f32[4,16,512]{2,1,0:T(8,128)S(1)}, u32[]{:S(2)}, u32[]{:S(2)}) %collective-permute-start.15) | collective-permute-done | bytes 131104 | tf_op jit(solution)/shard_map/ppermute | solution.py:38
  133.9 0.6 copy-done.13
  134.5 2.0 %place_shares.1 = f32[256,512]{1,0:T(8,128)} custom-call(f32[4,16,512]{2,1,0:T(8,128)} %copy-done.9, f32[4,16,512]{2,1,0:T(8,128)} %copy-done.11, f32[4,16,512]{2,1,0:T(8,128)} %copy-done.12, f32[4,16,512]{2,1,0:T(8,128)} %copy-done.13), custom_call_target="tpu_custom_call" | custom-call | tf_op jit(solution)/shard_map/place_shares/pallas_call | solution.py:135
  136.5 0.0 collective-permute-done.17
  136.5 12.4 %collective-permute-done.16 = bf16[256,512]{1,0:T(8,128)(2,1)S(1)} collective-permute-done((bf16[256,512]{1,0:T(8,128)(2,1)S(1)}, bf16[256,512]{1,0:T(8,128)(2,1)S(1)}, u32[]{:S(2)}, u32[]{:S(2)}) %collective-permute-start.16) | collective-permute-done | bytes 262176 | tf_op jit(solution)/shard_map/ppermute | solution.py:31
  148.9 2.4 %fusion.7 = (f32[1,256,512]{2,1,0:T(8,128)}, bf16[1,256,512]{2,1,0:T(8,128)(2,1)}) fusion(f32[1,256,512]{2,1,0:T(8,128)S(1)} %copy-done.7, f32[256,512]{1,0:T(8,128)S(1)} %copy-done.5, bf16[256,512]{1,0:T(8,128)(2,1)S(1)} %collective-permute-done.17, bf16[256,512]{1,0:T(8,128)(2,1)S(1)} %collective-permute-done.16, f32[256,512]{1,0:T(8,128)} %place_shares.1, ...), kind=kLoop, calls=%fused_computation.15 | loop fusion | flops 3014656 | bytes 3670016 | tf_op jit(solution)/shard_map/broadcast_in_dim | solution.py:276
  (31 shorter events, 0.1 us)
Async XLA Ops:
  0.6 35.5 %collective-permute-start = (bf16[256,512]{1,0:T(8,128)(2,1)}, bf16[256,512]{1,0:T(8,128)(2,1)S(1)}, u32[]{:S(2)}, u32[]{:S(2)}) collective-permute-start(bf16[256,512]{1,0:T(8,128)(2,1)} %bitcast.41), channel_id=1, source_target_pairs={{0,8},{1,25},{2,10},{3,27},{4,12},{5,29},{6,14},{7,31},{8,16},{9,1... | collective-permute-start | bytes 786440 | tf_op jit(solution)/shard_map/ppermute | solution.py:31
  13.9 39.0 %collective-permute-start.4 = (bf16[256,512]{1,0:T(8,128)(2,1)}, bf16[256,512]{1,0:T(8,128)(2,1)S(1)}, u32[]{:S(2)}, u32[]{:S(2)}) collective-permute-start(bf16[256,512]{1,0:T(8,128)(2,1)} %bitcast.42), channel_id=1, source_target_pairs={{0,24},{1,9},{2,26},{3,11},{4,28},{5,13},{6,30},{7,15},{8,0},{9,17... | collective-permute-start | bytes 786440 | tf_op jit(solution)/shard_map/ppermute | solution.py:31
  15.9 1.0 copy-start
  16.8 1.6 %copy-start.2 = (bf16[1,128,8192]{2,1,0:T(8,128)(2,1)S(1)}, bf16[1,128,8192]{2,1,0:T(8,128)(2,1)}, u32[]{:S(2)}) copy-start(bf16[1,128,8192]{2,1,0:T(8,128)(2,1)} %param.13) | copy-start | bytes 6291460
  19.1 1.4 copy-start.3
  20.4 0.6 copy-start.6
  21.0 31.9 %all-to-all-start = ((bf16[8,128,1024]{2,1,0:T(8,128)(2,1)}), bf16[8,128,1024]{2,1,0:T(8,128)(2,1)S(1)}, u32[]{:S(2)}, u32[]{:S(2)}) async-start(bf16[8,128,1024]{2,1,0:T(8,128)(2,1)} %copy-done.3), calls=%async_computation | async-start | bytes 4194304 | tf_op jit(solution)/shard_map/all_to_all | solution.py:203
  26.3 9.0 %collective-permute-start.1 = (bf16[4,16,512]{2,1,0:T(8,128)(2,1)S(1)}, bf16[4,16,512]{2,1,0:T(8,128)(2,1)S(1)}, u32[]{:S(2)}, u32[]{:S(2)}) collective-permute-start(bf16[4,16,512]{2,1,0:T(8,128)(2,1)S(1)} %get-tuple-element.43), channel_id=1, source_target_pairs={{0,32},{32,64},{64,96},{96,0},{128,160},{160,192},{192,224},{224,1... | collective-permute-start | bytes 196616 | tf_op jit(solution)/shard_map/ppermute | solution.py:38
  29.5 26.4 %copy-start.1 = (bf16[1,256,512]{2,1,0:T(8,128)(2,1)S(1)}, bf16[1,256,512]{2,1,0:T(8,128)(2,1)}, u32[]{:S(2)}) copy-start(bf16[1,256,512]{2,1,0:T(8,128)(2,1)} %param.8) | copy-start | bytes 786436
  29.5 6.6 %collective-permute-start.2 = (bf16[4,16,512]{2,1,0:T(8,128)(2,1)S(1)}, bf16[4,16,512]{2,1,0:T(8,128)(2,1)S(1)}, u32[]{:S(2)}, u32[]{:S(2)}) collective-permute-start(bf16[4,16,512]{2,1,0:T(8,128)(2,1)S(1)} %get-tuple-element.44), channel_id=1, source_target_pairs={{0,64},{32,96},{64,0},{96,32},{128,192},{160,224},{192,128},{224,1... | collective-permute-start | bytes 196616 | tf_op jit(solution)/shard_map/ppermute | solution.py:38
  35.3 15.4 %copy-start.15 = (bf16[4,16,512]{2,1,0:T(8,128)(2,1)}, bf16[4,16,512]{2,1,0:T(8,128)(2,1)S(1)}, u32[]{:S(2)}) copy-start(bf16[4,16,512]{2,1,0:T(8,128)(2,1)S(1)} %collective-permute-done.1.refs_1_) | copy-start | bytes 196612
  36.1 14.6 %copy-start.16 = (bf16[4,16,512]{2,1,0:T(8,128)(2,1)}, bf16[4,16,512]{2,1,0:T(8,128)(2,1)S(1)}, u32[]{:S(2)}) copy-start(bf16[4,16,512]{2,1,0:T(8,128)(2,1)S(1)} %collective-permute-done.2.refs_2_) | copy-start | bytes 196612
  36.2 19.8 %collective-permute-start.5 = (bf16[256,512]{1,0:T(8,128)(2,1)S(1)}, bf16[256,512]{1,0:T(8,128)(2,1)S(1)}, u32[]{:S(2)}, u32[]{:S(2)}) collective-permute-start(bf16[256,512]{1,0:T(8,128)(2,1)S(1)} %collective-permute-done.w1_ref), channel_id=1, source_target_pairs={{0,8},{1,25},{2,10},{3,27},{4,12},{5,29},{6,14},{7,31},{8,16},{9,1... | collective-permute-start | bytes 786440 | tf_op jit(solution)/shard_map/ppermute | solution.py:31
  44.3 6.4 %collective-permute-start.3 = (bf16[4,16,512]{2,1,0:T(8,128)(2,1)S(1)}, bf16[4,16,512]{2,1,0:T(8,128)(2,1)S(1)}, u32[]{:S(2)}, u32[]{:S(2)}) collective-permute-start(bf16[4,16,512]{2,1,0:T(8,128)(2,1)S(1)} %get-tuple-element.47), channel_id=1, source_target_pairs={{0,96},{32,0},{64,32},{96,64},{128,224},{160,128},{192,160},{224,1... | collective-permute-start | bytes 196616 | tf_op jit(solution)/shard_map/ppermute | solution.py:38
  50.7 0.6 copy-start.17
  58.2 21.3 %copy-start.10 = (bf16[1,128,512]{2,1,0:T(8,128)(2,1)S(1)}, bf16[1,128,512]{2,1,0:T(8,128)(2,1)}, u32[]{:S(2)}) copy-start(bf16[1,128,512]{2,1,0:T(8,128)(2,1)} %param.14) | copy-start | bytes 393220
  58.2 21.3 %copy-start.18 = (f32[1,128]{1,0:T(1,128)S(1)}, f32[1,128]{1,0:T(1,128)}, u32[]{:S(2)}) copy-start(f32[1,128]{1,0:T(1,128)} %mask.1) | copy-start | bytes 1540
  58.2 21.1 %all-to-all-start.1 = ((bf16[8,128,512]{2,1,0:T(8,128)(2,1)}), bf16[8,128,512]{2,1,0:T(8,128)(2,1)S(1)}, u32[]{:S(2)}, u32[]{:S(2)}) async-start(bf16[8,128,512]{2,1,0:T(8,128)(2,1)} %project.1), calls=%async_computation.1 | async-start | bytes 2097152 | tf_op jit(solution)/shard_map/all_to_all | solution.py:203
  62.9 10.2 %collective-permute-start.8 = (f32[16,512]{1,0:T(8,128)}, f32[16,512]{1,0:T(8,128)S(1)}, u32[]{:S(2)}, u32[]{:S(2)}) collective-permute-start(f32[16,512]{1,0:T(8,128)} %get-tuple-element.63), channel_id=1, source_target_pairs={{0,384},{32,416},{64,448},{96,480},{128,0},{160,32},{192,64},{224,... | collective-permute-start | bytes 98312 | tf_op jit(solution)/shard_map/ppermute | solution.py:38
  69.0 5.8 %collective-permute-start.7 = (f32[16,512]{1,0:T(8,128)}, f32[16,512]{1,0:T(8,128)S(1)}, u32[]{:S(2)}, u32[]{:S(2)}) collective-permute-start(f32[16,512]{1,0:T(8,128)} %get-tuple-element.62), channel_id=1, source_target_pairs={{0,256},{32,288},{64,320},{96,352},{128,384},{160,416},{192,448},{... | collective-permute-start | bytes 98312 | tf_op jit(solution)/shard_map/ppermute | solution.py:38
  70.9 7.0 %collective-permute-start.6 = (f32[16,512]{1,0:T(8,128)}, f32[16,512]{1,0:T(8,128)S(1)}, u32[]{:S(2)}, u32[]{:S(2)}) collective-permute-start(f32[16,512]{1,0:T(8,128)} %get-tuple-element.61), channel_id=1, source_target_pairs={{0,128},{32,160},{64,192},{96,224},{128,256},{160,288},{192,320},{... | collective-permute-start | bytes 98312 | tf_op jit(solution)/shard_map/ppermute | solution.py:38
  79.4 7.2 %copy-start.14 = (f32[16,512]{1,0:T(8,128)S(1)}, f32[16,512]{1,0:T(8,128)}, u32[]{:S(2)}) copy-start(f32[16,512]{1,0:T(8,128)} %get-tuple-element.67) | copy-start | bytes 98308
  80.7 21.0 %all-to-all-start.2 = ((bf16[8,128,512]{2,1,0:T(8,128)(2,1)}), bf16[8,128,512]{2,1,0:T(8,128)(2,1)S(1)}, u32[]{:S(2)}, u32[]{:S(2)}) async-start(bf16[8,128,512]{2,1,0:T(8,128)(2,1)} %broadcast_in_dim.15), calls=%async_computation.2 | async-start | bytes 2097152 | tf_op jit(solution)/shard_map/all_to_all | solution.py:203
  86.6 9.0 %collective-permute-start.9 = (f32[16,512]{1,0:T(8,128)S(1)}, f32[16,512]{1,0:T(8,128)S(1)}, u32[]{:S(2)}, u32[]{:S(2)}) collective-permute-start(f32[16,512]{1,0:T(8,128)S(1)} %copy-done.14), channel_id=1, source_target_pairs={{0,128},{32,160},{64,192},{96,224},{128,256},{160,288},{192,320},{... | collective-permute-start | bytes 98312 | tf_op jit(solution)/shard_map/ppermute | solution.py:38
  88.5 7.1 %collective-permute-start.10 = (f32[16,512]{1,0:T(8,128)S(1)}, f32[16,512]{1,0:T(8,128)S(1)}, u32[]{:S(2)}, u32[]{:S(2)}) collective-permute-start(f32[16,512]{1,0:T(8,128)S(1)} %copy-done.14), channel_id=1, source_target_pairs={{0,256},{32,288},{64,320},{96,352},{128,384},{160,416},{192,448},{... | collective-permute-start | bytes 98312 | tf_op jit(solution)/shard_map/ppermute | solution.py:38
  92.0 5.5 %collective-permute-start.11 = (f32[16,512]{1,0:T(8,128)S(1)}, f32[16,512]{1,0:T(8,128)S(1)}, u32[]{:S(2)}, u32[]{:S(2)}) collective-permute-start(f32[16,512]{1,0:T(8,128)S(1)} %copy-done.14), channel_id=1, source_target_pairs={{0,384},{32,416},{64,448},{96,480},{128,0},{160,32},{192,64},{224,... | collective-permute-start | bytes 98312 | tf_op jit(solution)/shard_map/ppermute | solution.py:38
  102.2 19.2 %collective-permute-start.12 = (bf16[256,512]{1,0:T(8,128)(2,1)S(1)}, bf16[256,512]{1,0:T(8,128)(2,1)S(1)}, u32[]{:S(2)}, u32[]{:S(2)}) collective-permute-start(bf16[256,512]{1,0:T(8,128)(2,1)S(1)} %gradient.2), channel_id=1, source_target_pairs={{0,8},{1,25},{2,10},{3,27},{4,12},{5,29},{6,14},{7,31},{8,16},{9,1... | collective-permute-start | bytes 786440 | tf_op jit(solution)/shard_map/ppermute | solution.py:31
  109.7 18.2 %copy-start.9 = (f32[4,16,512]{2,1,0:T(8,128)}, f32[4,16,512]{2,1,0:T(8,128)S(1)}, u32[]{:S(2)}) copy-start(f32[4,16,512]{2,1,0:T(8,128)S(1)} %pad_maximum_fusion.refs_0_) | copy-start | bytes 393220
  109.7 10.8 %collective-permute-start.13 = (f32[4,16,512]{2,1,0:T(8,128)S(1)}, f32[4,16,512]{2,1,0:T(8,128)S(1)}, u32[]{:S(2)}, u32[]{:S(2)}) collective-permute-start(f32[4,16,512]{2,1,0:T(8,128)S(1)} %pad_maximum_fusion.refs_0_), channel_id=1, source_target_pairs={{0,32},{32,64},{64,96},{96,0},{128,160},{160,192},{192,224},{224,1... | collective-permute-start | bytes 393224 | tf_op jit(solution)/shard_map/ppermute | solution.py:38
  112.9 8.5 %collective-permute-start.14 = (f32[4,16,512]{2,1,0:T(8,128)S(1)}, f32[4,16,512]{2,1,0:T(8,128)S(1)}, u32[]{:S(2)}, u32[]{:S(2)}) collective-permute-start(f32[4,16,512]{2,1,0:T(8,128)S(1)} %pad_maximum_fusion.refs_0_), channel_id=1, source_target_pairs={{0,64},{32,96},{64,0},{96,32},{128,192},{160,224},{192,128},{224,1... | collective-permute-start | bytes 393224 | tf_op jit(solution)/shard_map/ppermute | solution.py:38
  117.6 0.8 copy-start.4
  118.4 30.5 %copy-start.7 = (f32[1,256,512]{2,1,0:T(8,128)S(1)}, f32[1,256,512]{2,1,0:T(8,128)}, u32[]{:S(2)}) copy-start(f32[1,256,512]{2,1,0:T(8,128)} %param.9) | copy-start | bytes 1572868
  118.4 30.5 %copy-start.8 = (f32[1,256,512]{2,1,0:T(8,128)S(1)}, f32[1,256,512]{2,1,0:T(8,128)}, u32[]{:S(2)}) copy-start(f32[1,256,512]{2,1,0:T(8,128)} %param.10) | copy-start | bytes 1572868
  118.4 30.5 %copy-start.5 = (f32[256,512]{1,0:T(8,128)S(1)}, f32[256,512]{1,0:T(8,128)}, u32[]{:S(2)}) copy-start(f32[256,512]{1,0:T(8,128)} %copy-done.4) | copy-start | bytes 1572868
  118.4 18.1 %collective-permute-start.17 = (bf16[256,512]{1,0:T(8,128)(2,1)S(1)}, bf16[256,512]{1,0:T(8,128)(2,1)S(1)}, u32[]{:S(2)}, u32[]{:S(2)}) collective-permute-start(bf16[256,512]{1,0:T(8,128)(2,1)S(1)} %convert_element_type.45), channel_id=1, source_target_pairs={{0,24},{1,9},{2,26},{3,11},{4,28},{5,13},{6,30},{7,15},{8,0},{9,17... | collective-permute-start | bytes 786440 | tf_op jit(solution)/shard_map/ppermute | solution.py:31
  120.5 11.2 %copy-start.11 = (f32[4,16,512]{2,1,0:T(8,128)}, f32[4,16,512]{2,1,0:T(8,128)S(1)}, u32[]{:S(2)}) copy-start(f32[4,16,512]{2,1,0:T(8,128)S(1)} %collective-permute-done.13.refs_1_) | copy-start | bytes 393220
  121.4 10.3 %copy-start.12 = (f32[4,16,512]{2,1,0:T(8,128)}, f32[4,16,512]{2,1,0:T(8,128)S(1)}, u32[]{:S(2)}) copy-start(f32[4,16,512]{2,1,0:T(8,128)S(1)} %collective-permute-done.14.refs_2_) | copy-start | bytes 393220
  121.5 27.4 %collective-permute-start.16 = (bf16[256,512]{1,0:T(8,128)(2,1)S(1)}, bf16[256,512]{1,0:T(8,128)(2,1)S(1)}, u32[]{:S(2)}, u32[]{:S(2)}) collective-permute-start(bf16[256,512]{1,0:T(8,128)(2,1)S(1)} %add_convert_fusion), channel_id=1, source_target_pairs={{0,8},{1,25},{2,10},{3,27},{4,12},{5,29},{6,14},{7,31},{8,16},{9,1... | collective-permute-start | bytes 786440 | tf_op jit(solution)/shard_map/ppermute | solution.py:31
  127.9 6.0 %collective-permute-start.15 = (f32[4,16,512]{2,1,0:T(8,128)S(1)}, f32[4,16,512]{2,1,0:T(8,128)S(1)}, u32[]{:S(2)}, u32[]{:S(2)}) collective-permute-start(f32[4,16,512]{2,1,0:T(8,128)S(1)} %pad_maximum_fusion.refs_0_), channel_id=1, source_target_pairs={{0,96},{32,0},{64,32},{96,64},{128,224},{160,128},{192,160},{224,1... | collective-permute-start | bytes 393224 | tf_op jit(solution)/shard_map/ppermute | solution.py:38
  133.9 0.6 copy-start.13

commit v6 on v5

--- a/solution.py
+++ b/solution.py
@@ -86,7 +86,7 @@
     packed, *shares = pl.pallas_call(
         pack_kernel,
         out_shape=[
-            jax.ShapeDtypeStruct((PLANE, rows, SLABS * width), tokens.dtype),
+            pltpu.HBM((PLANE, rows, SLABS * width), tokens.dtype),
             *[share] * 4,
         ],
         in_specs=[pl.BlockSpec(memory_space=pltpu.HBM)] * 2,
@@ -98,7 +98,7 @@
         ],
         compiler_params=pltpu.CompilerParams(vmem_limit_bytes=16 << 20),
         name="pack_columns",
-    )(tokens, weights)
+    )(pltpu.with_memory_space_constraint(tokens, pltpu.HBM), weights)
     return packed, shares
 
 
@@ -237,11 +237,6 @@
 
     partials[0], *sums = lax.optimization_barrier((partials[0], *sums))
     sums[1:] = [shift_replica(sums[i], i, 0) for i in (1, 2, 3)]
-    weight_mean = (sums[0] + sums[1] + sums[2] + sums[3]) / workers
-    pseudo_grad = anchor - weight_mean
-    new_momentum = NESTEROV * momentum + pseudo_grad
-    new_anchor = anchor - OUTER_RATE * (pseudo_grad + NESTEROV * new_momentum)
-
     part_width = out_width // PARTS
 
     def residual_of(mine, h):
@@ -252,8 +247,12 @@
 
     received = to_plane(partials[0])
     out = residual_of(received, 0)
-    out, shared = lax.optimization_barrier((out, new_anchor))
-    shared = [shared] + [shift_replica(shared, i, 0) for i in (1, 2, 3)]
+    out, *sums = lax.optimization_barrier((out, *sums))
+    weight_mean = (sums[0] + sums[1] + sums[2] + sums[3]) / workers
+    pseudo_grad = anchor - weight_mean
+    new_momentum = NESTEROV * momentum + pseudo_grad
+    new_anchor = anchor - OUTER_RATE * (pseudo_grad + NESTEROV * new_momentum)
+    shared = [new_anchor] + [shift_replica(new_anchor, i, 0) for i in (1, 2, 3)]
     received = to_plane(out)
     received, *shared = lax.optimization_barrier((received, *shared))
     (far,) = gradient_of(columns, received, (3,), width, part_width, jnp.bfloat16)

time: 152 us -> 150 us (0.987)
  waiting for transfers between devices: 31.7 us -> 28.2 us
  local copies, waits for them, and re-layouts: 7.69 us -> 4.8 us
  starting transfers between devices: 97.7 us -> 99.7 us
  Pallas kernels: 9.06 us -> 11 us
    ppermute x12, waiting for transfers between devices: 12 us -> 8.69 us  [shift_replica(): return lax.ppermute(value, 'replica', pairs)]
    unnamed x38 -> x40, local copies, waits for them, and re-layouts: 6.61 us -> 3.7 us
    ppermute x6, starting transfers between devices: 39.3 us -> 41.4 us  [shift_ring(): return lax.ppermute(value, 'fsdp', pairs)]
    pallas_call x1, Pallas kernels: 0.64 us -> 2.48 us  [pack(): pl.pallas_call(pack_kernel, out_shape=[pltpu.HBM((PLANE, rows, SLABS * wi...]
    all_to_all x3, starting transfers between devices: 15.9 us -> 14.2 us  [to_plane(): return lax.all_to_all(value, 'fsdp', 0, 0, axis_index_groups=PLANES)]
  transfers between devices with their start and end apart: 21 -> 21, of which waited for: 10 -> 11; matrix products, arithmetic and copies ran while one was open for 1% -> 1% of each run, Pallas kernels for 4% -> 6%
where the time goes in v6:
time: 150 us; the launch traced here: 149 us
  starting transfers between devices  99.7 us (66%)
  waiting for transfers between devices  28.2 us (19%)
  Pallas kernels  11 us (7%)
  local copies, waits for them, and re-layouts  4.8 us (3%)
  other arithmetic  4.17 us (3%)
    ppermute x12, starting transfers between devices, shift_replica(): return lax.ppermute(value, 'replica', pairs)  44 us
    ppermute x6, starting transfers between devices, shift_ring(): return lax.ppermute(value, 'fsdp', pairs)  41.4 us
    ppermute x6, waiting for transfers between devices, shift_ring(): return lax.ppermute(value, 'fsdp', pairs)  14.4 us
    all_to_all x3, starting transfers between devices, to_plane(): return lax.all_to_all(value, 'fsdp', 0, 0, axis_index_groups=PLANES)  14.2 us
    ppermute x12, waiting for transfers between devices, shift_replica(): return lax.ppermute(value, 'replica', pairs)  8.69 us
    all_to_all x3, waiting for transfers between devices, to_plane(): return lax.all_to_all(value, 'fsdp', 0, 0, axis_index_groups=PLANES)  5.18 us
    unnamed x40, local copies, waits for them, and re-layouts  3.7 us
  transfers between devices with their start and end apart: 21, of which 11 were waited for; matrix products, arithmetic and copies ran while one was open for 1% of the time, Pallas kernels for 6%

profile of v6, /device:TPU:1, one launch (start us, length us, event | category | flops | bytes accessed | tf_op | source)
XLA Modules:
  0.0 148.9 jit_solution(2150294792481206891)
XLA Ops:
  0.6 13.3 %collective-permute-start = (bf16[256,512]{1,0:T(8,128)(2,1)}, bf16[256,512]{1,0:T(8,128)(2,1)S(1)}, u32[]{:S(2)}, u32[]{:S(2)}) collective-permute-start(bf16[256,512]{1,0:T(8,128)(2,1)} %bitcast.41), channel_id=1, source_target_pairs={{0,8},{1,25},{2,10},{3,27},{4,12},{5,29},{6,14},{7,31},{8,16},{9,1... | collective-permute-start | bytes 786440 | tf_op jit(solution)/shard_map/ppermute | solution.py:31
  13.9 1.9 %collective-permute-start.4 = (bf16[256,512]{1,0:T(8,128)(2,1)}, bf16[256,512]{1,0:T(8,128)(2,1)S(1)}, u32[]{:S(2)}, u32[]{:S(2)}) collective-permute-start(bf16[256,512]{1,0:T(8,128)(2,1)} %bitcast.42), channel_id=1, source_target_pairs={{0,24},{1,9},{2,26},{3,11},{4,28},{5,13},{6,30},{7,15},{8,0},{9,17... | collective-permute-start | bytes 786440 | tf_op jit(solution)/shard_map/ppermute | solution.py:31
  15.9 0.0 copy-start
  15.9 0.9 copy-done
  16.8 2.5 %pack_columns.1 = (bf16[8,128,1024]{2,1,0:T(8,128)(2,1)}, bf16[4,16,512]{2,1,0:T(8,128)(2,1)S(1)}, bf16[4,16,512]{2,1,0:T(8,128)(2,1)S(1)}, bf16[4,16,512]{2,1,0:T(8,128)(2,1)S(1)}, bf16[4,16,512]{2,1,0:T(8,128)(2,1)S(1)}) custom-call(bf16[128,8192]{1,0:T(8,128)(2,1)} %bitcast.45, bf16[4,4,16,512]{3,2,1,0:T(8,128)(2,1)S(1)} %bitcast.43), custom_call_target="tpu_custom_call" | custom-call | tf_op jit(solution)/shard_map/pack_columns/pallas_call | solution.py:86
  19.3 0.0 copy-start.4
  19.3 0.6 copy-done.4
  19.9 5.3 %all-to-all-start = ((bf16[8,128,1024]{2,1,0:T(8,128)(2,1)}), bf16[8,128,1024]{2,1,0:T(8,128)(2,1)S(1)}, u32[]{:S(2)}, u32[]{:S(2)}) async-start(bf16[8,128,1024]{2,1,0:T(8,128)(2,1)} %get-tuple-element.44), calls=%async_computation | async-start | bytes 4194304 | tf_op jit(solution)/shard_map/all_to_all | solution.py:203
  25.2 3.2 %collective-permute-start.1 = (bf16[4,16,512]{2,1,0:T(8,128)(2,1)S(1)}, bf16[4,16,512]{2,1,0:T(8,128)(2,1)S(1)}, u32[]{:S(2)}, u32[]{:S(2)}) collective-permute-start(bf16[4,16,512]{2,1,0:T(8,128)(2,1)S(1)} %get-tuple-element.46), channel_id=1, source_target_pairs={{0,32},{32,64},{64,96},{96,0},{128,160},{160,192},{192,224},{224,1... | collective-permute-start | bytes 196616 | tf_op jit(solution)/shard_map/ppermute | solution.py:38
  28.4 0.0 copy-start.1
  28.4 4.7 %collective-permute-start.2 = (bf16[4,16,512]{2,1,0:T(8,128)(2,1)S(1)}, bf16[4,16,512]{2,1,0:T(8,128)(2,1)S(1)}, u32[]{:S(2)}, u32[]{:S(2)}) collective-permute-start(bf16[4,16,512]{2,1,0:T(8,128)(2,1)S(1)} %get-tuple-element.47), channel_id=1, source_target_pairs={{0,64},{32,96},{64,0},{96,32},{128,192},{160,224},{192,128},{224,1... | collective-permute-start | bytes 196616 | tf_op jit(solution)/shard_map/ppermute | solution.py:38
  33.1 1.2 mask.1
  34.3 0.0 collective-permute-done.1.refs_1_
  34.3 0.7 collective-permute-done.2.refs_2_
  35.1 0.0 collective-permute-done.w1_ref
  35.1 9.2 %collective-permute-start.5 = (bf16[256,512]{1,0:T(8,128)(2,1)S(1)}, bf16[256,512]{1,0:T(8,128)(2,1)S(1)}, u32[]{:S(2)}, u32[]{:S(2)}) collective-permute-start(bf16[256,512]{1,0:T(8,128)(2,1)S(1)} %collective-permute-done.w1_ref), channel_id=1, source_target_pairs={{0,8},{1,25},{2,10},{3,27},{4,12},{5,29},{6,14},{7,31},{8,16},{9,1... | collective-permute-start | bytes 786440 | tf_op jit(solution)/shard_map/ppermute | solution.py:31
  44.3 4.9 %collective-permute-start.3 = (bf16[4,16,512]{2,1,0:T(8,128)(2,1)S(1)}, bf16[4,16,512]{2,1,0:T(8,128)(2,1)S(1)}, u32[]{:S(2)}, u32[]{:S(2)}) collective-permute-start(bf16[4,16,512]{2,1,0:T(8,128)(2,1)S(1)} %get-tuple-element.50), channel_id=1, source_target_pairs={{0,96},{32,0},{64,32},{96,64},{128,224},{160,128},{192,160},{224,1... | collective-permute-start | bytes 196616 | tf_op jit(solution)/shard_map/ppermute | solution.py:38
  49.2 1.5 %collective-permute-done.3.refs_3_ = bf16[4,16,512]{2,1,0:T(8,128)(2,1)S(1)} collective-permute-done((bf16[4,16,512]{2,1,0:T(8,128)(2,1)S(1)}, bf16[4,16,512]{2,1,0:T(8,128)(2,1)S(1)}, u32[]{:S(2)}, u32[]{:S(2)}) %collective-permute-start.3) | collective-permute-done | bytes 65568 | tf_op jit(solution)/shard_map/ppermute | solution.py:38
  50.7 0.6 copy-done.15
  51.3 1.6 %add_shares.1 = (f32[16,512]{1,0:T(8,128)}, f32[16,512]{1,0:T(8,128)}, f32[16,512]{1,0:T(8,128)}, f32[16,512]{1,0:T(8,128)}) custom-call(bf16[4,16,512]{2,1,0:T(8,128)(2,1)} %copy-done.4, bf16[4,16,512]{2,1,0:T(8,128)(2,1)} %copy-done.13, bf16[4,16,512]{2,1,0:T(8,128)(2,1)} %copy-done.14, bf16[4,16,512]{2,1,0:T(8,128)(2,1)} %copy-done.15), custom_call_target="tpu_custom_call" | custom-call | tf_op jit(solution)/shard_map/add_shares/pallas_call | solution.py:116
  52.9 2.3 %collective-permute-done.5.w3_ref = bf16[256,512]{1,0:T(8,128)(2,1)S(1)} collective-permute-done((bf16[256,512]{1,0:T(8,128)(2,1)S(1)}, bf16[256,512]{1,0:T(8,128)(2,1)S(1)}, u32[]{:S(2)}, u32[]{:S(2)}) %collective-permute-start.5) | collective-permute-done | bytes 262176 | tf_op jit(solution)/shard_map/ppermute | solution.py:31
  55.3 2.3 %project.1 = bf16[8,128,512]{2,1,0:T(8,128)(2,1)} custom-call(bf16[1024,1024]{1,0:T(8,128)(2,1)S(1)} %bitcast.38, bf16[256,512]{1,0:T(8,128)(2,1)S(1)} %bitcast.44, bf16[256,512]{1,0:T(8,128)(2,1)S(1)} %collective-permute-done.w1_ref, bf16[256,512]{1,0:T(8,128)(2,1)S(1)} %collective-permute-done.4.w2_ref, bf16[256,512]{1,0:T(8,128)(2,1)S(1)} %collective-permute-done.5.w3_ref), custom_call_target="tpu_custom_call" | custom-call | tf_op jit(solution)/shard_map/project/pallas_call | solution.py:172
  57.5 4.5 %all-to-all-start.1 = ((bf16[8,128,512]{2,1,0:T(8,128)(2,1)}), bf16[8,128,512]{2,1,0:T(8,128)(2,1)S(1)}, u32[]{:S(2)}, u32[]{:S(2)}) async-start(bf16[8,128,512]{2,1,0:T(8,128)(2,1)} %project.1), calls=%async_computation.1 | async-start | bytes 2097152 | tf_op jit(solution)/shard_map/all_to_all | solution.py:203
  62.1 2.2 %collective-permute-start.6 = (f32[16,512]{1,0:T(8,128)}, f32[16,512]{1,0:T(8,128)}, u32[]{:S(2)}, u32[]{:S(2)}) collective-permute-start(f32[16,512]{1,0:T(8,128)} %get-tuple-element.64), channel_id=1, source_target_pairs={{0,128},{32,160},{64,192},{96,224},{128,256},{160,288},{192,320},{... | collective-permute-start | bytes 98312 | tf_op jit(solution)/shard_map/ppermute | solution.py:38
  64.3 6.2 %collective-permute-start.7 = (f32[16,512]{1,0:T(8,128)}, f32[16,512]{1,0:T(8,128)}, u32[]{:S(2)}, u32[]{:S(2)}) collective-permute-start(f32[16,512]{1,0:T(8,128)} %get-tuple-element.65), channel_id=1, source_target_pairs={{0,256},{32,288},{64,320},{96,352},{128,384},{160,416},{192,448},{... | collective-permute-start | bytes 98312 | tf_op jit(solution)/shard_map/ppermute | solution.py:38
  70.5 1.9 %collective-permute-start.8 = (f32[16,512]{1,0:T(8,128)}, f32[16,512]{1,0:T(8,128)}, u32[]{:S(2)}, u32[]{:S(2)}) collective-permute-start(f32[16,512]{1,0:T(8,128)} %get-tuple-element.66), channel_id=1, source_target_pairs={{0,384},{32,416},{64,448},{96,480},{128,0},{160,32},{192,64},{224,... | collective-permute-start | bytes 98312 | tf_op jit(solution)/shard_map/ppermute | solution.py:38
  72.4 4.7 %all-to-all-done.1 = bf16[8,128,512]{2,1,0:T(8,128)(2,1)S(1)} async-done(((bf16[8,128,512]{2,1,0:T(8,128)(2,1)}), bf16[8,128,512]{2,1,0:T(8,128)(2,1)S(1)}, u32[]{:S(2)}, u32[]{:S(2)}) %all-to-all-start.1) | async-done | bytes 1048608 | tf_op jit(solution)/shard_map/all_to_all | solution.py:203
  77.2 0.2 convert_reduce_fusion
  77.3 0.0 copy-start.16
  77.3 0.0 copy-start.17
  77.3 0.0 copy-start.18
  77.4 0.1 fusion.12
  77.5 0.0 collective-permute-done.6
  77.5 0.0 collective-permute-done.7
  77.5 1.1 broadcast_in_dim.15
  78.6 4.5 %all-to-all-start.2 = ((bf16[8,128,512]{2,1,0:T(8,128)(2,1)}), bf16[8,128,512]{2,1,0:T(8,128)(2,1)S(1)}, u32[]{:S(2)}, u32[]{:S(2)}) async-start(bf16[8,128,512]{2,1,0:T(8,128)(2,1)} %broadcast_in_dim.15), calls=%async_computation.2 | async-start | bytes 2097152 | tf_op jit(solution)/shard_map/all_to_all | solution.py:203
  83.1 1.4 multiply_subtract_fusion
  84.5 2.1 %collective-permute-start.9 = (f32[16,512]{1,0:T(8,128)S(1)}, f32[16,512]{1,0:T(8,128)S(1)}, u32[]{:S(2)}, u32[]{:S(2)}) collective-permute-start(f32[16,512]{1,0:T(8,128)S(1)} %get-tuple-element.73), channel_id=1, source_target_pairs={{0,128},{32,160},{64,192},{96,224},{128,256},{160,288},{192,320},{... | collective-permute-start | bytes 98312 | tf_op jit(solution)/shard_map/ppermute | solution.py:38
  86.6 6.2 %collective-permute-start.10 = (f32[16,512]{1,0:T(8,128)S(1)}, f32[16,512]{1,0:T(8,128)S(1)}, u32[]{:S(2)}, u32[]{:S(2)}) collective-permute-start(f32[16,512]{1,0:T(8,128)S(1)} %get-tuple-element.73), channel_id=1, source_target_pairs={{0,256},{32,288},{64,320},{96,352},{128,384},{160,416},{192,448},{... | collective-permute-start | bytes 98312 | tf_op jit(solution)/shard_map/ppermute | solution.py:38
  92.8 1.9 %collective-permute-start.11 = (f32[16,512]{1,0:T(8,128)S(1)}, f32[16,512]{1,0:T(8,128)S(1)}, u32[]{:S(2)}, u32[]{:S(2)}) collective-permute-start(f32[16,512]{1,0:T(8,128)S(1)} %get-tuple-element.73), channel_id=1, source_target_pairs={{0,384},{32,416},{64,448},{96,480},{128,0},{160,32},{192,64},{224,... | collective-permute-start | bytes 98312 | tf_op jit(solution)/shard_map/ppermute | solution.py:38
  94.7 0.0 collective-permute-done.9
  94.7 0.2 collective-permute-done.10
  95.0 2.8 %collective-permute-done.11 = f32[16,512]{1,0:T(8,128)S(1)} collective-permute-done((f32[16,512]{1,0:T(8,128)S(1)}, f32[16,512]{1,0:T(8,128)S(1)}, u32[]{:S(2)}, u32[]{:S(2)}) %collective-permute-start.11) | collective-permute-done | bytes 32800 | tf_op jit(solution)/shard_map/ppermute | solution.py:38
  97.7 0.4 all-to-all-done.2.rows_ref
  98.2 0.5 gradient.2
  98.7 7.7 %collective-permute-start.12 = (bf16[256,512]{1,0:T(8,128)(2,1)S(1)}, bf16[256,512]{1,0:T(8,128)(2,1)S(1)}, u32[]{:S(2)}, u32[]{:S(2)}) collective-permute-start(bf16[256,512]{1,0:T(8,128)(2,1)S(1)} %gradient.2), channel_id=1, source_target_pairs={{0,8},{1,25},{2,10},{3,27},{4,12},{5,29},{6,14},{7,31},{8,16},{9,1... | collective-permute-start | bytes 786440 | tf_op jit(solution)/shard_map/ppermute | solution.py:31
  106.4 0.0 copy-start.7
  106.4 3.2 %collective-permute-start.13 = (f32[4,16,512]{2,1,0:T(8,128)S(1)}, f32[4,16,512]{2,1,0:T(8,128)S(1)}, u32[]{:S(2)}, u32[]{:S(2)}) collective-permute-start(f32[4,16,512]{2,1,0:T(8,128)S(1)} %pad_maximum_fusion.refs_0_), channel_id=1, source_target_pairs={{0,32},{32,64},{64,96},{96,0},{128,160},{160,192},{192,224},{224,1... | collective-permute-start | bytes 393224 | tf_op jit(solution)/shard_map/ppermute | solution.py:38
  109.6 4.9 %collective-permute-start.14 = (f32[4,16,512]{2,1,0:T(8,128)S(1)}, f32[4,16,512]{2,1,0:T(8,128)S(1)}, u32[]{:S(2)}, u32[]{:S(2)}) collective-permute-start(f32[4,16,512]{2,1,0:T(8,128)S(1)} %pad_maximum_fusion.refs_0_), channel_id=1, source_target_pairs={{0,64},{32,96},{64,0},{96,32},{128,192},{160,224},{192,128},{224,1... | collective-permute-start | bytes 393224 | tf_op jit(solution)/shard_map/ppermute | solution.py:38
  114.6 1.0 gradient.3
  115.6 0.0 copy-start.2
  115.6 0.8 copy-done.2
  116.4 2.1 %collective-permute-start.17 = (bf16[256,512]{1,0:T(8,128)(2,1)S(1)}, bf16[256,512]{1,0:T(8,128)(2,1)S(1)}, u32[]{:S(2)}, u32[]{:S(2)}) collective-permute-start(bf16[256,512]{1,0:T(8,128)(2,1)S(1)} %convert_element_type.45), channel_id=1, source_target_pairs={{0,24},{1,9},{2,26},{3,11},{4,28},{5,13},{6,30},{7,15},{8,0},{9,17... | collective-permute-start | bytes 786440 | tf_op jit(solution)/shard_map/ppermute | solution.py:31
  118.5 0.0 collective-permute-done.13.refs_1_
  118.5 0.1 collective-permute-done.14.refs_2_
  118.6 0.1 add_convert_fusion
  118.7 7.2 %collective-permute-start.16 = (bf16[256,512]{1,0:T(8,128)(2,1)S(1)}, bf16[256,512]{1,0:T(8,128)(2,1)S(1)}, u32[]{:S(2)}, u32[]{:S(2)}) collective-permute-start(bf16[256,512]{1,0:T(8,128)(2,1)S(1)} %add_convert_fusion), channel_id=1, source_target_pairs={{0,8},{1,25},{2,10},{3,27},{4,12},{5,29},{6,14},{7,31},{8,16},{9,1... | collective-permute-start | bytes 786440 | tf_op jit(solution)/shard_map/ppermute | solution.py:31
  125.9 2.7 %collective-permute-start.15 = (f32[4,16,512]{2,1,0:T(8,128)S(1)}, f32[4,16,512]{2,1,0:T(8,128)S(1)}, u32[]{:S(2)}, u32[]{:S(2)}) collective-permute-start(f32[4,16,512]{2,1,0:T(8,128)S(1)} %pad_maximum_fusion.refs_0_), channel_id=1, source_target_pairs={{0,96},{32,0},{64,32},{96,64},{128,224},{160,128},{192,160},{224,1... | collective-permute-start | bytes 393224 | tf_op jit(solution)/shard_map/ppermute | solution.py:38
  128.6 3.3 %collective-permute-done.15.refs_3_ = f32[4,16,512]{2,1,0:T(8,128)S(1)} collective-permute-done((f32[4,16,512]{2,1,0:T(8,128)S(1)}, f32[4,16,512]{2,1,0:T(8,128)S(1)}, u32[]{:S(2)}, u32[]{:S(2)}) %collective-permute-start.15) | collective-permute-done | bytes 131104 | tf_op jit(solution)/shard_map/ppermute | solution.py:38
  131.9 0.6 copy-done.11
  132.6 2.0 %place_shares.1 = f32[256,512]{1,0:T(8,128)} custom-call(f32[4,16,512]{2,1,0:T(8,128)} %copy-done.7, f32[4,16,512]{2,1,0:T(8,128)} %copy-done.9, f32[4,16,512]{2,1,0:T(8,128)} %copy-done.10, f32[4,16,512]{2,1,0:T(8,128)} %copy-done.11), custom_call_target="tpu_custom_call" | custom-call | tf_op jit(solution)/shard_map/place_shares/pallas_call | solution.py:135
  134.5 6.3 %collective-permute-done.17 = bf16[256,512]{1,0:T(8,128)(2,1)S(1)} collective-permute-done((bf16[256,512]{1,0:T(8,128)(2,1)S(1)}, bf16[256,512]{1,0:T(8,128)(2,1)S(1)}, u32[]{:S(2)}, u32[]{:S(2)}) %collective-permute-start.17) | collective-permute-done | bytes 262176 | tf_op jit(solution)/shard_map/ppermute | solution.py:31
  140.8 5.7 %collective-permute-done.16 = bf16[256,512]{1,0:T(8,128)(2,1)S(1)} collective-permute-done((bf16[256,512]{1,0:T(8,128)(2,1)S(1)}, bf16[256,512]{1,0:T(8,128)(2,1)S(1)}, u32[]{:S(2)}, u32[]{:S(2)}) %collective-permute-start.16) | collective-permute-done | bytes 262176 | tf_op jit(solution)/shard_map/ppermute | solution.py:31
  146.6 2.4 %fusion.7 = (f32[1,256,512]{2,1,0:T(8,128)}, bf16[1,256,512]{2,1,0:T(8,128)(2,1)}) fusion(f32[1,256,512]{2,1,0:T(8,128)S(1)} %copy-done.5, f32[256,512]{1,0:T(8,128)S(1)} %copy-done.3, bf16[256,512]{1,0:T(8,128)(2,1)S(1)} %collective-permute-done.17, bf16[256,512]{1,0:T(8,128)(2,1)S(1)} %collective-permute-done.16, f32[256,512]{1,0:T(8,128)} %place_shares.1, ...), kind=kLoop, calls=%fused_computation.15 | loop fusion | flops 3014656 | bytes 3670016 | tf_op jit(solution)/shard_map/broadcast_in_dim | solution.py:275
  (33 shorter events, 0.1 us)
Async XLA Ops:
  0.6 34.4 %collective-permute-start = (bf16[256,512]{1,0:T(8,128)(2,1)}, bf16[256,512]{1,0:T(8,128)(2,1)S(1)}, u32[]{:S(2)}, u32[]{:S(2)}) collective-permute-start(bf16[256,512]{1,0:T(8,128)(2,1)} %bitcast.41), channel_id=1, source_target_pairs={{0,8},{1,25},{2,10},{3,27},{4,12},{5,29},{6,14},{7,31},{8,16},{9,1... | collective-permute-start | bytes 786440 | tf_op jit(solution)/shard_map/ppermute | solution.py:31
  13.9 39.0 %collective-permute-start.4 = (bf16[256,512]{1,0:T(8,128)(2,1)}, bf16[256,512]{1,0:T(8,128)(2,1)S(1)}, u32[]{:S(2)}, u32[]{:S(2)}) collective-permute-start(bf16[256,512]{1,0:T(8,128)(2,1)} %bitcast.42), channel_id=1, source_target_pairs={{0,24},{1,9},{2,26},{3,11},{4,28},{5,13},{6,30},{7,15},{8,0},{9,17... | collective-permute-start | bytes 786440 | tf_op jit(solution)/shard_map/ppermute | solution.py:31
  15.9 1.0 copy-start
  19.3 0.6 copy-start.4
  19.9 33.0 %all-to-all-start = ((bf16[8,128,1024]{2,1,0:T(8,128)(2,1)}), bf16[8,128,1024]{2,1,0:T(8,128)(2,1)S(1)}, u32[]{:S(2)}, u32[]{:S(2)}) async-start(bf16[8,128,1024]{2,1,0:T(8,128)(2,1)} %get-tuple-element.44), calls=%async_computation | async-start | bytes 4194304 | tf_op jit(solution)/shard_map/all_to_all | solution.py:203
  25.2 9.1 %collective-permute-start.1 = (bf16[4,16,512]{2,1,0:T(8,128)(2,1)S(1)}, bf16[4,16,512]{2,1,0:T(8,128)(2,1)S(1)}, u32[]{:S(2)}, u32[]{:S(2)}) collective-permute-start(bf16[4,16,512]{2,1,0:T(8,128)(2,1)S(1)} %get-tuple-element.46), channel_id=1, source_target_pairs={{0,32},{32,64},{64,96},{96,0},{128,160},{160,192},{192,224},{224,1... | collective-permute-start | bytes 196616 | tf_op jit(solution)/shard_map/ppermute | solution.py:38
  28.4 26.9 %copy-start.1 = (bf16[1,256,512]{2,1,0:T(8,128)(2,1)S(1)}, bf16[1,256,512]{2,1,0:T(8,128)(2,1)}, u32[]{:S(2)}) copy-start(bf16[1,256,512]{2,1,0:T(8,128)(2,1)} %param.8) | copy-start | bytes 786436
  28.4 6.6 %collective-permute-start.2 = (bf16[4,16,512]{2,1,0:T(8,128)(2,1)S(1)}, bf16[4,16,512]{2,1,0:T(8,128)(2,1)S(1)}, u32[]{:S(2)}, u32[]{:S(2)}) collective-permute-start(bf16[4,16,512]{2,1,0:T(8,128)(2,1)S(1)} %get-tuple-element.47), channel_id=1, source_target_pairs={{0,64},{32,96},{64,0},{96,32},{128,192},{160,224},{192,128},{224,1... | collective-permute-start | bytes 196616 | tf_op jit(solution)/shard_map/ppermute | solution.py:38
  34.3 16.4 %copy-start.13 = (bf16[4,16,512]{2,1,0:T(8,128)(2,1)}, bf16[4,16,512]{2,1,0:T(8,128)(2,1)S(1)}, u32[]{:S(2)}) copy-start(bf16[4,16,512]{2,1,0:T(8,128)(2,1)S(1)} %collective-permute-done.1.refs_1_) | copy-start | bytes 196612
  35.0 15.7 %copy-start.14 = (bf16[4,16,512]{2,1,0:T(8,128)(2,1)}, bf16[4,16,512]{2,1,0:T(8,128)(2,1)S(1)}, u32[]{:S(2)}) copy-start(bf16[4,16,512]{2,1,0:T(8,128)(2,1)S(1)} %collective-permute-done.2.refs_2_) | copy-start | bytes 196612
  35.1 20.2 %collective-permute-start.5 = (bf16[256,512]{1,0:T(8,128)(2,1)S(1)}, bf16[256,512]{1,0:T(8,128)(2,1)S(1)}, u32[]{:S(2)}, u32[]{:S(2)}) collective-permute-start(bf16[256,512]{1,0:T(8,128)(2,1)S(1)} %collective-permute-done.w1_ref), channel_id=1, source_target_pairs={{0,8},{1,25},{2,10},{3,27},{4,12},{5,29},{6,14},{7,31},{8,16},{9,1... | collective-permute-start | bytes 786440 | tf_op jit(solution)/shard_map/ppermute | solution.py:31
  44.3 6.4 %collective-permute-start.3 = (bf16[4,16,512]{2,1,0:T(8,128)(2,1)S(1)}, bf16[4,16,512]{2,1,0:T(8,128)(2,1)S(1)}, u32[]{:S(2)}, u32[]{:S(2)}) collective-permute-start(bf16[4,16,512]{2,1,0:T(8,128)(2,1)S(1)} %get-tuple-element.50), channel_id=1, source_target_pairs={{0,96},{32,0},{64,32},{96,64},{128,224},{160,128},{192,160},{224,1... | collective-permute-start | bytes 196616 | tf_op jit(solution)/shard_map/ppermute | solution.py:38
  50.7 0.6 copy-start.15
  57.5 19.8 %copy-start.8 = (bf16[1,128,512]{2,1,0:T(8,128)(2,1)S(1)}, bf16[1,128,512]{2,1,0:T(8,128)(2,1)}, u32[]{:S(2)}) copy-start(bf16[1,128,512]{2,1,0:T(8,128)(2,1)} %param.14) | copy-start | bytes 393220
  57.5 19.8 %copy-start.19 = (f32[1,128]{1,0:T(1,128)S(1)}, f32[1,128]{1,0:T(1,128)}, u32[]{:S(2)}) copy-start(f32[1,128]{1,0:T(1,128)} %mask.1) | copy-start | bytes 1540
  57.5 19.6 %all-to-all-start.1 = ((bf16[8,128,512]{2,1,0:T(8,128)(2,1)}), bf16[8,128,512]{2,1,0:T(8,128)(2,1)S(1)}, u32[]{:S(2)}, u32[]{:S(2)}) async-start(bf16[8,128,512]{2,1,0:T(8,128)(2,1)} %project.1), calls=%async_computation.1 | async-start | bytes 2097152 | tf_op jit(solution)/shard_map/all_to_all | solution.py:203
  62.1 15.4 %collective-permute-start.6 = (f32[16,512]{1,0:T(8,128)}, f32[16,512]{1,0:T(8,128)}, u32[]{:S(2)}, u32[]{:S(2)}) collective-permute-start(f32[16,512]{1,0:T(8,128)} %get-tuple-element.64), channel_id=1, source_target_pairs={{0,128},{32,160},{64,192},{96,224},{128,256},{160,288},{192,320},{... | collective-permute-start | bytes 98312 | tf_op jit(solution)/shard_map/ppermute | solution.py:38
  64.3 13.2 %collective-permute-start.7 = (f32[16,512]{1,0:T(8,128)}, f32[16,512]{1,0:T(8,128)}, u32[]{:S(2)}, u32[]{:S(2)}) collective-permute-start(f32[16,512]{1,0:T(8,128)} %get-tuple-element.65), channel_id=1, source_target_pairs={{0,256},{32,288},{64,320},{96,352},{128,384},{160,416},{192,448},{... | collective-permute-start | bytes 98312 | tf_op jit(solution)/shard_map/ppermute | solution.py:38
  70.5 7.0 %collective-permute-start.8 = (f32[16,512]{1,0:T(8,128)}, f32[16,512]{1,0:T(8,128)}, u32[]{:S(2)}, u32[]{:S(2)}) collective-permute-start(f32[16,512]{1,0:T(8,128)} %get-tuple-element.66), channel_id=1, source_target_pairs={{0,384},{32,416},{64,448},{96,480},{128,0},{160,32},{192,64},{224,... | collective-permute-start | bytes 98312 | tf_op jit(solution)/shard_map/ppermute | solution.py:38
  77.3 5.8 %copy-start.16 = (f32[16,512]{1,0:T(8,128)S(1)}, f32[16,512]{1,0:T(8,128)}, u32[]{:S(2)}) copy-start(f32[16,512]{1,0:T(8,128)} %param.11) | copy-start | bytes 98308
  77.3 5.8 %copy-start.17 = (f32[16,512]{1,0:T(8,128)S(1)}, f32[16,512]{1,0:T(8,128)}, u32[]{:S(2)}) copy-start(f32[16,512]{1,0:T(8,128)} %param.12) | copy-start | bytes 98308
  77.3 5.7 %copy-start.18 = (f32[16,512]{1,0:T(8,128)S(1)}, f32[16,512]{1,0:T(8,128)}, u32[]{:S(2)}) copy-start(f32[16,512]{1,0:T(8,128)} %get-tuple-element.68) | copy-start | bytes 98308
  78.6 19.6 %all-to-all-start.2 = ((bf16[8,128,512]{2,1,0:T(8,128)(2,1)}), bf16[8,128,512]{2,1,0:T(8,128)(2,1)S(1)}, u32[]{:S(2)}, u32[]{:S(2)}) async-start(bf16[8,128,512]{2,1,0:T(8,128)(2,1)} %broadcast_in_dim.15), calls=%async_computation.2 | async-start | bytes 2097152 | tf_op jit(solution)/shard_map/all_to_all | solution.py:203
  84.5 31.1 %copy-start.12 = (f32[16,512]{1,0:T(8,128)}, f32[16,512]{1,0:T(8,128)S(1)}, u32[]{:S(2)}) copy-start(f32[16,512]{1,0:T(8,128)S(1)} %get-tuple-element.73) | copy-start | bytes 98308
  84.5 10.2 %collective-permute-start.9 = (f32[16,512]{1,0:T(8,128)S(1)}, f32[16,512]{1,0:T(8,128)S(1)}, u32[]{:S(2)}, u32[]{:S(2)}) collective-permute-start(f32[16,512]{1,0:T(8,128)S(1)} %get-tuple-element.73), channel_id=1, source_target_pairs={{0,128},{32,160},{64,192},{96,224},{128,256},{160,288},{192,320},{... | collective-permute-start | bytes 98312 | tf_op jit(solution)/shard_map/ppermute | solution.py:38
  86.6 8.4 %collective-permute-start.10 = (f32[16,512]{1,0:T(8,128)S(1)}, f32[16,512]{1,0:T(8,128)S(1)}, u32[]{:S(2)}, u32[]{:S(2)}) collective-permute-start(f32[16,512]{1,0:T(8,128)S(1)} %get-tuple-element.73), channel_id=1, source_target_pairs={{0,256},{32,288},{64,320},{96,352},{128,384},{160,416},{192,448},{... | collective-permute-start | bytes 98312 | tf_op jit(solution)/shard_map/ppermute | solution.py:38
  92.8 5.0 %collective-permute-start.11 = (f32[16,512]{1,0:T(8,128)S(1)}, f32[16,512]{1,0:T(8,128)S(1)}, u32[]{:S(2)}, u32[]{:S(2)}) collective-permute-start(f32[16,512]{1,0:T(8,128)S(1)} %get-tuple-element.73), channel_id=1, source_target_pairs={{0,384},{32,416},{64,448},{96,480},{128,0},{160,32},{192,64},{224,... | collective-permute-start | bytes 98312 | tf_op jit(solution)/shard_map/ppermute | solution.py:38
  98.7 19.9 %collective-permute-start.12 = (bf16[256,512]{1,0:T(8,128)(2,1)S(1)}, bf16[256,512]{1,0:T(8,128)(2,1)S(1)}, u32[]{:S(2)}, u32[]{:S(2)}) collective-permute-start(bf16[256,512]{1,0:T(8,128)(2,1)S(1)} %gradient.2), channel_id=1, source_target_pairs={{0,8},{1,25},{2,10},{3,27},{4,12},{5,29},{6,14},{7,31},{8,16},{9,1... | collective-permute-start | bytes 786440 | tf_op jit(solution)/shard_map/ppermute | solution.py:31
  106.4 19.5 %copy-start.7 = (f32[4,16,512]{2,1,0:T(8,128)}, f32[4,16,512]{2,1,0:T(8,128)S(1)}, u32[]{:S(2)}) copy-start(f32[4,16,512]{2,1,0:T(8,128)S(1)} %pad_maximum_fusion.refs_0_) | copy-start | bytes 393220
  106.4 12.1 %collective-permute-start.13 = (f32[4,16,512]{2,1,0:T(8,128)S(1)}, f32[4,16,512]{2,1,0:T(8,128)S(1)}, u32[]{:S(2)}, u32[]{:S(2)}) collective-permute-start(f32[4,16,512]{2,1,0:T(8,128)S(1)} %pad_maximum_fusion.refs_0_), channel_id=1, source_target_pairs={{0,32},{32,64},{64,96},{96,0},{128,160},{160,192},{192,224},{224,1... | collective-permute-start | bytes 393224 | tf_op jit(solution)/shard_map/ppermute | solution.py:38
  109.6 9.0 %collective-permute-start.14 = (f32[4,16,512]{2,1,0:T(8,128)S(1)}, f32[4,16,512]{2,1,0:T(8,128)S(1)}, u32[]{:S(2)}, u32[]{:S(2)}) collective-permute-start(f32[4,16,512]{2,1,0:T(8,128)S(1)} %pad_maximum_fusion.refs_0_), channel_id=1, source_target_pairs={{0,64},{32,96},{64,0},{96,32},{128,192},{160,224},{192,128},{224,1... | collective-permute-start | bytes 393224 | tf_op jit(solution)/shard_map/ppermute | solution.py:38
  115.6 0.8 copy-start.2
  116.4 30.2 %copy-start.5 = (f32[1,256,512]{2,1,0:T(8,128)S(1)}, f32[1,256,512]{2,1,0:T(8,128)}, u32[]{:S(2)}) copy-start(f32[1,256,512]{2,1,0:T(8,128)} %param.9) | copy-start | bytes 1572868
  116.4 30.2 %copy-start.6 = (f32[1,256,512]{2,1,0:T(8,128)S(1)}, f32[1,256,512]{2,1,0:T(8,128)}, u32[]{:S(2)}) copy-start(f32[1,256,512]{2,1,0:T(8,128)} %param.10) | copy-start | bytes 1572868
  116.4 30.2 %copy-start.3 = (f32[256,512]{1,0:T(8,128)S(1)}, f32[256,512]{1,0:T(8,128)}, u32[]{:S(2)}) copy-start(f32[256,512]{1,0:T(8,128)} %copy-done.2) | copy-start | bytes 1572868
  116.4 24.4 %collective-permute-start.17 = (bf16[256,512]{1,0:T(8,128)(2,1)S(1)}, bf16[256,512]{1,0:T(8,128)(2,1)S(1)}, u32[]{:S(2)}, u32[]{:S(2)}) collective-permute-start(bf16[256,512]{1,0:T(8,128)(2,1)S(1)} %convert_element_type.45), channel_id=1, source_target_pairs={{0,24},{1,9},{2,26},{3,11},{4,28},{5,13},{6,30},{7,15},{8,0},{9,17... | collective-permute-start | bytes 786440 | tf_op jit(solution)/shard_map/ppermute | solution.py:31
  118.5 10.1 %copy-start.9 = (f32[4,16,512]{2,1,0:T(8,128)}, f32[4,16,512]{2,1,0:T(8,128)S(1)}, u32[]{:S(2)}) copy-start(f32[4,16,512]{2,1,0:T(8,128)S(1)} %collective-permute-done.13.refs_1_) | copy-start | bytes 393220
  118.6 10.0 %copy-start.10 = (f32[4,16,512]{2,1,0:T(8,128)}, f32[4,16,512]{2,1,0:T(8,128)S(1)}, u32[]{:S(2)}) copy-start(f32[4,16,512]{2,1,0:T(8,128)S(1)} %collective-permute-done.14.refs_2_) | copy-start | bytes 393220
  118.7 27.9 %collective-permute-start.16 = (bf16[256,512]{1,0:T(8,128)(2,1)S(1)}, bf16[256,512]{1,0:T(8,128)(2,1)S(1)}, u32[]{:S(2)}, u32[]{:S(2)}) collective-permute-start(bf16[256,512]{1,0:T(8,128)(2,1)S(1)} %add_convert_fusion), channel_id=1, source_target_pairs={{0,8},{1,25},{2,10},{3,27},{4,12},{5,29},{6,14},{7,31},{8,16},{9,1... | collective-permute-start | bytes 786440 | tf_op jit(solution)/shard_map/ppermute | solution.py:31
  125.9 6.0 %collective-permute-start.15 = (f32[4,16,512]{2,1,0:T(8,128)S(1)}, f32[4,16,512]{2,1,0:T(8,128)S(1)}, u32[]{:S(2)}, u32[]{:S(2)}) collective-permute-start(f32[4,16,512]{2,1,0:T(8,128)S(1)} %pad_maximum_fusion.refs_0_), channel_id=1, source_target_pairs={{0,96},{32,0},{64,32},{96,64},{128,224},{160,128},{192,160},{224,1... | collective-permute-start | bytes 393224 | tf_op jit(solution)/shard_map/ppermute | solution.py:38
  131.9 0.7 copy-start.11

commit v7 on v6

--- a/solution.py
+++ b/solution.py
@@ -98,7 +98,7 @@
         ],
         compiler_params=pltpu.CompilerParams(vmem_limit_bytes=16 << 20),
         name="pack_columns",
-    )(pltpu.with_memory_space_constraint(tokens, pltpu.HBM), weights)
+    )(*[pltpu.with_memory_space_constraint(v, pltpu.HBM) for v in (tokens, weights)])
     return packed, shares
 
 
@@ -117,7 +117,7 @@
         add_kernel,
         out_shape=[jax.ShapeDtypeStruct(shares[0].shape[1:], jnp.float32)] * 4,
         name="add_shares",
-    )(*shares)
+    )(*[pltpu.with_memory_space_constraint(v, pltpu.VMEM) for v in shares])
 
 
 def place_kernel(*refs):
@@ -136,7 +136,7 @@
         place_kernel,
         out_shape=jax.ShapeDtypeStruct((16 * rows, out_width), shares[0].dtype),
         name="place_shares",
-    )(*shares)
+    )(*[pltpu.with_memory_space_constraint(v, pltpu.VMEM) for v in shares])
 
 
 def mask_kernel(keep_ref, mask_ref):
@@ -229,7 +229,7 @@
     shares[1:] = [shift_replica(shares[i], 0, i) for i in (1, 2, 3)]
 
     previous, following = shift_ring(initial, 1), shift_ring(initial, -1)
-    previous, mask, *shares[1:3] = lax.optimization_barrier((previous, mask, *shares[1:3]))
+    previous, mask, *shares[1:2] = lax.optimization_barrier((previous, mask, *shares[1:2]))
     opposite = shift_ring(previous, 1)
     sums = add_shares(shares)
     columns, *sums = lax.optimization_barrier((columns, *sums))

time: 150 us -> 150 us (level)
  waiting for transfers between devices: 28.2 us -> 35.8 us
  local copies, waits for them, and re-layouts: 4.8 us -> 1.91 us
  Pallas kernels: 11 us -> 8.95 us
  starting transfers between devices: 99.7 us -> 97.7 us
    all_to_all x3, waiting for transfers between devices: 5.18 us -> 9.68 us  [to_plane(): return lax.all_to_all(value, 'fsdp', 0, 0, axis_index_groups=PLANES)]
    ppermute x12, starting transfers between devices: 44 us -> 39.7 us  [shift_replica(): return lax.ppermute(value, 'replica', pairs)]
    unnamed x40 -> x26, local copies, waits for them, and re-layouts: 3.7 us -> 0.84 us
    ppermute x6, waiting for transfers between devices: 14.4 us -> 16.7 us  [shift_ring(): return lax.ppermute(value, 'fsdp', pairs)]
    ppermute x6, starting transfers between devices: 41.4 us -> 43.6 us  [shift_ring(): return lax.ppermute(value, 'fsdp', pairs)]
  transfers between devices with their start and end apart: 21 -> 21, of which waited for: 11 -> 9; matrix products, arithmetic and copies ran while one was open for 1% -> 1% of each run, Pallas kernels for 6% -> 4%
where the time goes in v7:
time: 150 us; the launch traced here: 149 us
  starting transfers between devices  97.7 us (65%)
  waiting for transfers between devices  35.8 us (24%)
  Pallas kernels  8.95 us (6%)
  other arithmetic  3.38 us (2%)
  local copies, waits for them, and re-layouts  1.91 us (1%)
    ppermute x6, starting transfers between devices, shift_ring(): return lax.ppermute(value, 'fsdp', pairs)  43.6 us
    ppermute x12, starting transfers between devices, shift_replica(): return lax.ppermute(value, 'replica', pairs)  39.7 us
    ppermute x6, waiting for transfers between devices, shift_ring(): return lax.ppermute(value, 'fsdp', pairs)  16.7 us
    all_to_all x3, starting transfers between devices, to_plane(): return lax.all_to_all(value, 'fsdp', 0, 0, axis_index_groups=PLANES)  14.4 us
    all_to_all x3, waiting for transfers between devices, to_plane(): return lax.all_to_all(value, 'fsdp', 0, 0, axis_index_groups=PLANES)  9.68 us
    ppermute x12, waiting for transfers between devices, shift_replica(): return lax.ppermute(value, 'replica', pairs)  9.44 us
  transfers between devices with their start and end apart: 21, of which 9 were waited for; matrix products, arithmetic and copies ran while one was open for 1% of the time, Pallas kernels for 4%

profile of v7, /device:TPU:1, one launch (start us, length us, event | category | flops | bytes accessed | tf_op | source)
XLA Modules:
  0.0 148.7 jit_solution(7995219198034484661)
XLA Ops:
  0.6 13.3 %collective-permute-start = (bf16[256,512]{1,0:T(8,128)(2,1)}, bf16[256,512]{1,0:T(8,128)(2,1)S(1)}, u32[]{:S(2)}, u32[]{:S(2)}) collective-permute-start(bf16[256,512]{1,0:T(8,128)(2,1)} %bitcast.41), channel_id=1, source_target_pairs={{0,8},{1,25},{2,10},{3,27},{4,12},{5,29},{6,14},{7,31},{8,16},{9,1... | collective-permute-start | bytes 786440 | tf_op jit(solution)/shard_map/ppermute | solution.py:31
  13.9 1.9 %collective-permute-start.4 = (bf16[256,512]{1,0:T(8,128)(2,1)}, bf16[256,512]{1,0:T(8,128)(2,1)S(1)}, u32[]{:S(2)}, u32[]{:S(2)}) collective-permute-start(bf16[256,512]{1,0:T(8,128)(2,1)} %bitcast.42), channel_id=1, source_target_pairs={{0,24},{1,9},{2,26},{3,11},{4,28},{5,13},{6,30},{7,15},{8,0},{9,17... | collective-permute-start | bytes 786440 | tf_op jit(solution)/shard_map/ppermute | solution.py:31
  15.9 2.5 %pack_columns.1 = (bf16[8,128,1024]{2,1,0:T(8,128)(2,1)}, bf16[4,16,512]{2,1,0:T(8,128)(2,1)S(1)}, bf16[4,16,512]{2,1,0:T(8,128)(2,1)S(1)}, bf16[4,16,512]{2,1,0:T(8,128)(2,1)S(1)}, bf16[4,16,512]{2,1,0:T(8,128)(2,1)S(1)}) custom-call(bf16[128,8192]{1,0:T(8,128)(2,1)} %bitcast.45, bf16[4,4,16,512]{3,2,1,0:T(8,128)(2,1)} %bitcast.43), custom_call_target="tpu_custom_call" | custom-call | tf_op jit(solution)/shard_map/pack_columns/pallas_call | solution.py:86
  18.4 5.3 %all-to-all-start = ((bf16[8,128,1024]{2,1,0:T(8,128)(2,1)}), bf16[8,128,1024]{2,1,0:T(8,128)(2,1)S(1)}, u32[]{:S(2)}, u32[]{:S(2)}) async-start(bf16[8,128,1024]{2,1,0:T(8,128)(2,1)} %get-tuple-element.43), calls=%async_computation | async-start | bytes 4194304 | tf_op jit(solution)/shard_map/all_to_all | solution.py:203
  23.6 3.3 %collective-permute-start.1 = (bf16[4,16,512]{2,1,0:T(8,128)(2,1)S(1)}, bf16[4,16,512]{2,1,0:T(8,128)(2,1)S(1)}, u32[]{:S(2)}, u32[]{:S(2)}) collective-permute-start(bf16[4,16,512]{2,1,0:T(8,128)(2,1)S(1)} %get-tuple-element.45), channel_id=1, source_target_pairs={{0,32},{32,64},{64,96},{96,0},{128,160},{160,192},{192,224},{224,1... | collective-permute-start | bytes 196616 | tf_op jit(solution)/shard_map/ppermute | solution.py:38
  27.0 1.2 mask.1
  28.2 2.5 %collective-permute-done.1.refs_1_ = bf16[4,16,512]{2,1,0:T(8,128)(2,1)S(1)} collective-permute-done((bf16[4,16,512]{2,1,0:T(8,128)(2,1)S(1)}, bf16[4,16,512]{2,1,0:T(8,128)(2,1)S(1)}, u32[]{:S(2)}, u32[]{:S(2)}) %collective-permute-start.1) | collective-permute-done | bytes 65568 | tf_op jit(solution)/shard_map/ppermute | solution.py:38
  30.7 0.6 collective-permute-done.w1_ref
  31.3 13.0 %collective-permute-start.5 = (bf16[256,512]{1,0:T(8,128)(2,1)S(1)}, bf16[256,512]{1,0:T(8,128)(2,1)S(1)}, u32[]{:S(2)}, u32[]{:S(2)}) collective-permute-start(bf16[256,512]{1,0:T(8,128)(2,1)S(1)} %collective-permute-done.w1_ref), channel_id=1, source_target_pairs={{0,8},{1,25},{2,10},{3,27},{4,12},{5,29},{6,14},{7,31},{8,16},{9,1... | collective-permute-start | bytes 786440 | tf_op jit(solution)/shard_map/ppermute | solution.py:31
  44.3 5.1 %collective-permute-start.2 = (bf16[4,16,512]{2,1,0:T(8,128)(2,1)S(1)}, bf16[4,16,512]{2,1,0:T(8,128)(2,1)S(1)}, u32[]{:S(2)}, u32[]{:S(2)}) collective-permute-start(bf16[4,16,512]{2,1,0:T(8,128)(2,1)S(1)} %get-tuple-element.47), channel_id=1, source_target_pairs={{0,64},{32,96},{64,0},{96,32},{128,192},{160,224},{192,128},{224,1... | collective-permute-start | bytes 196616 | tf_op jit(solution)/shard_map/ppermute | solution.py:38
  49.4 2.7 %collective-permute-start.3 = (bf16[4,16,512]{2,1,0:T(8,128)(2,1)S(1)}, bf16[4,16,512]{2,1,0:T(8,128)(2,1)S(1)}, u32[]{:S(2)}, u32[]{:S(2)}) collective-permute-start(bf16[4,16,512]{2,1,0:T(8,128)(2,1)S(1)} %get-tuple-element.48), channel_id=1, source_target_pairs={{0,96},{32,0},{64,32},{96,64},{128,224},{160,128},{192,160},{224,1... | collective-permute-start | bytes 196616 | tf_op jit(solution)/shard_map/ppermute | solution.py:38
  52.1 0.0 collective-permute-done.2.refs_2_
  52.1 3.2 %collective-permute-done.3.refs_3_ = bf16[4,16,512]{2,1,0:T(8,128)(2,1)S(1)} collective-permute-done((bf16[4,16,512]{2,1,0:T(8,128)(2,1)S(1)}, bf16[4,16,512]{2,1,0:T(8,128)(2,1)S(1)}, u32[]{:S(2)}, u32[]{:S(2)}) %collective-permute-start.3) | collective-permute-done | bytes 65568 | tf_op jit(solution)/shard_map/ppermute | solution.py:38
  55.2 0.7 add_shares.1
  55.9 0.0 all-to-all-done
  55.9 0.0 collective-permute-done.4.w2_ref
  55.9 0.0 collective-permute-done.5.w3_ref
  55.9 0.0 copy-done
  55.9 2.2 %project.1 = bf16[8,128,512]{2,1,0:T(8,128)(2,1)} custom-call(bf16[1024,1024]{1,0:T(8,128)(2,1)S(1)} %bitcast.38, bf16[256,512]{1,0:T(8,128)(2,1)S(1)} %bitcast.44, bf16[256,512]{1,0:T(8,128)(2,1)S(1)} %collective-permute-done.w1_ref, bf16[256,512]{1,0:T(8,128)(2,1)S(1)} %collective-permute-done.4.w2_ref, bf16[256,512]{1,0:T(8,128)(2,1)S(1)} %collective-permute-done.5.w3_ref), custom_call_target="tpu_custom_call" | custom-call | tf_op jit(solution)/shard_map/project/pallas_call | solution.py:172
  58.1 4.8 %all-to-all-start.1 = ((bf16[8,128,512]{2,1,0:T(8,128)(2,1)}), bf16[8,128,512]{2,1,0:T(8,128)(2,1)S(1)}, u32[]{:S(2)}, u32[]{:S(2)}) async-start(bf16[8,128,512]{2,1,0:T(8,128)(2,1)} %project.1), calls=%async_computation.1 | async-start | bytes 2097152 | tf_op jit(solution)/shard_map/all_to_all | solution.py:203
  63.0 1.9 %collective-permute-start.6 = (f32[16,512]{1,0:T(8,128)}, f32[16,512]{1,0:T(8,128)S(1)}, u32[]{:S(2)}, u32[]{:S(2)}) collective-permute-start(f32[16,512]{1,0:T(8,128)} %get-tuple-element.62), channel_id=1, source_target_pairs={{0,128},{32,160},{64,192},{96,224},{128,256},{160,288},{192,320},{... | collective-permute-start | bytes 98312 | tf_op jit(solution)/shard_map/ppermute | solution.py:38
  64.9 3.6 %collective-permute-start.7 = (f32[16,512]{1,0:T(8,128)}, f32[16,512]{1,0:T(8,128)S(1)}, u32[]{:S(2)}, u32[]{:S(2)}) collective-permute-start(f32[16,512]{1,0:T(8,128)} %get-tuple-element.63), channel_id=1, source_target_pairs={{0,256},{32,288},{64,320},{96,352},{128,384},{160,416},{192,448},{... | collective-permute-start | bytes 98312 | tf_op jit(solution)/shard_map/ppermute | solution.py:38
  68.5 3.5 %collective-permute-start.8 = (f32[16,512]{1,0:T(8,128)S(1)}, f32[16,512]{1,0:T(8,128)S(1)}, u32[]{:S(2)}, u32[]{:S(2)}) collective-permute-start(f32[16,512]{1,0:T(8,128)S(1)} %copy-done.12), channel_id=1, source_target_pairs={{0,384},{32,416},{64,448},{96,480},{128,0},{160,32},{192,64},{224,... | collective-permute-start | bytes 98312 | tf_op jit(solution)/shard_map/ppermute | solution.py:38
  72.0 6.1 %all-to-all-done.1 = bf16[8,128,512]{2,1,0:T(8,128)(2,1)S(1)} async-done(((bf16[8,128,512]{2,1,0:T(8,128)(2,1)}), bf16[8,128,512]{2,1,0:T(8,128)(2,1)S(1)}, u32[]{:S(2)}, u32[]{:S(2)}) %all-to-all-start.1) | async-done | bytes 1048608 | tf_op jit(solution)/shard_map/all_to_all | solution.py:203
  78.1 0.1 convert_reduce_fusion
  78.2 0.0 copy-start.8
  78.2 0.0 copy-start.9
  78.2 0.0 copy-start.10
  78.3 0.1 fusion.12
  78.4 0.0 collective-permute-done.6
  78.4 0.0 collective-permute-done.7
  78.4 0.0 collective-permute-done.8
  78.4 1.1 broadcast_in_dim.15
  79.5 4.3 %all-to-all-start.2 = ((bf16[8,128,512]{2,1,0:T(8,128)(2,1)}), bf16[8,128,512]{2,1,0:T(8,128)(2,1)S(1)}, u32[]{:S(2)}, u32[]{:S(2)}) async-start(bf16[8,128,512]{2,1,0:T(8,128)(2,1)} %broadcast_in_dim.15), calls=%async_computation.2 | async-start | bytes 2097152 | tf_op jit(solution)/shard_map/all_to_all | solution.py:203
  83.8 0.0 copy-done.9
  83.8 0.0 copy-done.10
  83.8 0.6 multiply_subtract_fusion
  84.5 1.9 %collective-permute-start.9 = (f32[16,512]{1,0:T(8,128)S(1)}, f32[16,512]{1,0:T(8,128)S(1)}, u32[]{:S(2)}, u32[]{:S(2)}) collective-permute-start(f32[16,512]{1,0:T(8,128)S(1)} %get-tuple-element.71), channel_id=1, source_target_pairs={{0,128},{32,160},{64,192},{96,224},{128,256},{160,288},{192,320},{... | collective-permute-start | bytes 98312 | tf_op jit(solution)/shard_map/ppermute | solution.py:38
  86.4 3.6 %collective-permute-start.10 = (f32[16,512]{1,0:T(8,128)S(1)}, f32[16,512]{1,0:T(8,128)S(1)}, u32[]{:S(2)}, u32[]{:S(2)}) collective-permute-start(f32[16,512]{1,0:T(8,128)S(1)} %get-tuple-element.71), channel_id=1, source_target_pairs={{0,256},{32,288},{64,320},{96,352},{128,384},{160,416},{192,448},{... | collective-permute-start | bytes 98312 | tf_op jit(solution)/shard_map/ppermute | solution.py:38
  90.0 3.5 %collective-permute-start.11 = (f32[16,512]{1,0:T(8,128)S(1)}, f32[16,512]{1,0:T(8,128)S(1)}, u32[]{:S(2)}, u32[]{:S(2)}) collective-permute-start(f32[16,512]{1,0:T(8,128)S(1)} %get-tuple-element.71), channel_id=1, source_target_pairs={{0,384},{32,416},{64,448},{96,480},{128,0},{160,32},{192,64},{224,... | collective-permute-start | bytes 98312 | tf_op jit(solution)/shard_map/ppermute | solution.py:38
  93.5 0.0 collective-permute-done.9
  93.5 0.0 collective-permute-done.10
  93.5 1.8 %collective-permute-done.11 = f32[16,512]{1,0:T(8,128)S(1)} collective-permute-done((f32[16,512]{1,0:T(8,128)S(1)}, f32[16,512]{1,0:T(8,128)S(1)}, u32[]{:S(2)}, u32[]{:S(2)}) %collective-permute-start.11) | collective-permute-done | bytes 32800 | tf_op jit(solution)/shard_map/ppermute | solution.py:38
  95.3 3.6 %all-to-all-done.2.rows_ref = bf16[8,128,512]{2,1,0:T(8,128)(2,1)S(1)} async-done(((bf16[8,128,512]{2,1,0:T(8,128)(2,1)}), bf16[8,128,512]{2,1,0:T(8,128)(2,1)S(1)}, u32[]{:S(2)}, u32[]{:S(2)}) %all-to-all-start.2) | async-done | bytes 1048608 | tf_op jit(solution)/shard_map/all_to_all | solution.py:203
  98.9 0.5 gradient.2
  99.4 6.0 %collective-permute-start.12 = (bf16[256,512]{1,0:T(8,128)(2,1)S(1)}, bf16[256,512]{1,0:T(8,128)(2,1)S(1)}, u32[]{:S(2)}, u32[]{:S(2)}) collective-permute-start(bf16[256,512]{1,0:T(8,128)(2,1)S(1)} %gradient.2), channel_id=1, source_target_pairs={{0,8},{1,25},{2,10},{3,27},{4,12},{5,29},{6,14},{7,31},{8,16},{9,1... | collective-permute-start | bytes 786440 | tf_op jit(solution)/shard_map/ppermute | solution.py:31
  105.5 2.0 %collective-permute-start.13 = (f32[4,16,512]{2,1,0:T(8,128)S(1)}, f32[4,16,512]{2,1,0:T(8,128)S(1)}, u32[]{:S(2)}, u32[]{:S(2)}) collective-permute-start(f32[4,16,512]{2,1,0:T(8,128)S(1)} %pad_maximum_fusion.refs_0_), channel_id=1, source_target_pairs={{0,32},{32,64},{64,96},{96,0},{128,160},{160,192},{192,224},{224,1... | collective-permute-start | bytes 393224 | tf_op jit(solution)/shard_map/ppermute | solution.py:38
  107.5 4.5 %collective-permute-start.14 = (f32[4,16,512]{2,1,0:T(8,128)S(1)}, f32[4,16,512]{2,1,0:T(8,128)S(1)}, u32[]{:S(2)}, u32[]{:S(2)}) collective-permute-start(f32[4,16,512]{2,1,0:T(8,128)S(1)} %pad_maximum_fusion.refs_0_), channel_id=1, source_target_pairs={{0,64},{32,96},{64,0},{96,32},{128,192},{160,224},{192,128},{224,1... | collective-permute-start | bytes 393224 | tf_op jit(solution)/shard_map/ppermute | solution.py:38
  112.0 1.0 gradient.3
  113.0 0.0 copy-start.2
  113.0 0.8 copy-done.2
  113.9 4.8 %collective-permute-start.17 = (bf16[256,512]{1,0:T(8,128)(2,1)S(1)}, bf16[256,512]{1,0:T(8,128)(2,1)S(1)}, u32[]{:S(2)}, u32[]{:S(2)}) collective-permute-start(bf16[256,512]{1,0:T(8,128)(2,1)S(1)} %convert_element_type.45), channel_id=1, source_target_pairs={{0,24},{1,9},{2,26},{3,11},{4,28},{5,13},{6,30},{7,15},{8,0},{9,17... | collective-permute-start | bytes 786440 | tf_op jit(solution)/shard_map/ppermute | solution.py:31
  118.6 0.0 collective-permute-done.13.refs_1_
  118.7 0.0 collective-permute-done.14.refs_2_
  118.7 0.0 collective-permute-done.12
  118.7 0.1 add_convert_fusion
  118.8 4.6 %collective-permute-start.16 = (bf16[256,512]{1,0:T(8,128)(2,1)S(1)}, bf16[256,512]{1,0:T(8,128)(2,1)S(1)}, u32[]{:S(2)}, u32[]{:S(2)}) collective-permute-start(bf16[256,512]{1,0:T(8,128)(2,1)S(1)} %add_convert_fusion), channel_id=1, source_target_pairs={{0,8},{1,25},{2,10},{3,27},{4,12},{5,29},{6,14},{7,31},{8,16},{9,1... | collective-permute-start | bytes 786440 | tf_op jit(solution)/shard_map/ppermute | solution.py:31
  123.3 4.1 %collective-permute-start.15 = (f32[4,16,512]{2,1,0:T(8,128)S(1)}, f32[4,16,512]{2,1,0:T(8,128)S(1)}, u32[]{:S(2)}, u32[]{:S(2)}) collective-permute-start(f32[4,16,512]{2,1,0:T(8,128)S(1)} %pad_maximum_fusion.refs_0_), channel_id=1, source_target_pairs={{0,96},{32,0},{64,32},{96,64},{128,224},{160,128},{192,160},{224,1... | collective-permute-start | bytes 393224 | tf_op jit(solution)/shard_map/ppermute | solution.py:38
  127.5 1.9 %collective-permute-done.15.refs_3_ = f32[4,16,512]{2,1,0:T(8,128)S(1)} collective-permute-done((f32[4,16,512]{2,1,0:T(8,128)S(1)}, f32[4,16,512]{2,1,0:T(8,128)S(1)}, u32[]{:S(2)}, u32[]{:S(2)}) %collective-permute-start.15) | collective-permute-done | bytes 131104 | tf_op jit(solution)/shard_map/ppermute | solution.py:38
  129.4 0.8 place_shares.1
  130.2 11.8 %collective-permute-done.17 = bf16[256,512]{1,0:T(8,128)(2,1)S(1)} collective-permute-done((bf16[256,512]{1,0:T(8,128)(2,1)S(1)}, bf16[256,512]{1,0:T(8,128)(2,1)S(1)}, u32[]{:S(2)}, u32[]{:S(2)}) %collective-permute-start.17) | collective-permute-done | bytes 262176 | tf_op jit(solution)/shard_map/ppermute | solution.py:31
  142.0 4.3 %collective-permute-done.16 = bf16[256,512]{1,0:T(8,128)(2,1)S(1)} collective-permute-done((bf16[256,512]{1,0:T(8,128)(2,1)S(1)}, bf16[256,512]{1,0:T(8,128)(2,1)S(1)}, u32[]{:S(2)}, u32[]{:S(2)}) %collective-permute-start.16) | collective-permute-done | bytes 262176 | tf_op jit(solution)/shard_map/ppermute | solution.py:31
  146.3 0.0 copy-done.4
  146.4 2.4 %fusion.7 = (f32[1,256,512]{2,1,0:T(8,128)}, bf16[1,256,512]{2,1,0:T(8,128)(2,1)}) fusion(f32[1,256,512]{2,1,0:T(8,128)S(1)} %copy-done.4, f32[256,512]{1,0:T(8,128)S(1)} %copy-done.3, bf16[256,512]{1,0:T(8,128)(2,1)S(1)} %collective-permute-done.17, bf16[256,512]{1,0:T(8,128)(2,1)S(1)} %collective-permute-done.16, f32[256,512]{1,0:T(8,128)} %place_shares.1, ...), kind=kLoop, calls=%fused_computation.15 | loop fusion | flops 3014656 | bytes 3670016 | tf_op jit(solution)/shard_map/broadcast_in_dim | solution.py:275
  (19 shorter events, 0.1 us)
Async XLA Ops:
  0.6 30.6 %collective-permute-start = (bf16[256,512]{1,0:T(8,128)(2,1)}, bf16[256,512]{1,0:T(8,128)(2,1)S(1)}, u32[]{:S(2)}, u32[]{:S(2)}) collective-permute-start(bf16[256,512]{1,0:T(8,128)(2,1)} %bitcast.41), channel_id=1, source_target_pairs={{0,8},{1,25},{2,10},{3,27},{4,12},{5,29},{6,14},{7,31},{8,16},{9,1... | collective-permute-start | bytes 786440 | tf_op jit(solution)/shard_map/ppermute | solution.py:31
  13.9 42.0 %collective-permute-start.4 = (bf16[256,512]{1,0:T(8,128)(2,1)}, bf16[256,512]{1,0:T(8,128)(2,1)S(1)}, u32[]{:S(2)}, u32[]{:S(2)}) collective-permute-start(bf16[256,512]{1,0:T(8,128)(2,1)} %bitcast.42), channel_id=1, source_target_pairs={{0,24},{1,9},{2,26},{3,11},{4,28},{5,13},{6,30},{7,15},{8,0},{9,17... | collective-permute-start | bytes 786440 | tf_op jit(solution)/shard_map/ppermute | solution.py:31
  18.4 37.5 %all-to-all-start = ((bf16[8,128,1024]{2,1,0:T(8,128)(2,1)}), bf16[8,128,1024]{2,1,0:T(8,128)(2,1)S(1)}, u32[]{:S(2)}, u32[]{:S(2)}) async-start(bf16[8,128,1024]{2,1,0:T(8,128)(2,1)} %get-tuple-element.43), calls=%async_computation | async-start | bytes 4194304 | tf_op jit(solution)/shard_map/all_to_all | solution.py:203
  23.6 32.3 %copy-start = (bf16[1,256,512]{2,1,0:T(8,128)(2,1)S(1)}, bf16[1,256,512]{2,1,0:T(8,128)(2,1)}, u32[]{:S(2)}) copy-start(bf16[1,256,512]{2,1,0:T(8,128)(2,1)} %param.8) | copy-start | bytes 786436
  23.6 7.1 %collective-permute-start.1 = (bf16[4,16,512]{2,1,0:T(8,128)(2,1)S(1)}, bf16[4,16,512]{2,1,0:T(8,128)(2,1)S(1)}, u32[]{:S(2)}, u32[]{:S(2)}) collective-permute-start(bf16[4,16,512]{2,1,0:T(8,128)(2,1)S(1)} %get-tuple-element.45), channel_id=1, source_target_pairs={{0,32},{32,64},{64,96},{96,0},{128,160},{160,192},{192,224},{224,1... | collective-permute-start | bytes 196616 | tf_op jit(solution)/shard_map/ppermute | solution.py:38
  31.3 24.6 %collective-permute-start.5 = (bf16[256,512]{1,0:T(8,128)(2,1)S(1)}, bf16[256,512]{1,0:T(8,128)(2,1)S(1)}, u32[]{:S(2)}, u32[]{:S(2)}) collective-permute-start(bf16[256,512]{1,0:T(8,128)(2,1)S(1)} %collective-permute-done.w1_ref), channel_id=1, source_target_pairs={{0,8},{1,25},{2,10},{3,27},{4,12},{5,29},{6,14},{7,31},{8,16},{9,1... | collective-permute-start | bytes 786440 | tf_op jit(solution)/shard_map/ppermute | solution.py:31
  44.3 7.8 %collective-permute-start.2 = (bf16[4,16,512]{2,1,0:T(8,128)(2,1)S(1)}, bf16[4,16,512]{2,1,0:T(8,128)(2,1)S(1)}, u32[]{:S(2)}, u32[]{:S(2)}) collective-permute-start(bf16[4,16,512]{2,1,0:T(8,128)(2,1)S(1)} %get-tuple-element.47), channel_id=1, source_target_pairs={{0,64},{32,96},{64,0},{96,32},{128,192},{160,224},{192,128},{224,1... | collective-permute-start | bytes 196616 | tf_op jit(solution)/shard_map/ppermute | solution.py:38
  49.4 5.9 %collective-permute-start.3 = (bf16[4,16,512]{2,1,0:T(8,128)(2,1)S(1)}, bf16[4,16,512]{2,1,0:T(8,128)(2,1)S(1)}, u32[]{:S(2)}, u32[]{:S(2)}) collective-permute-start(bf16[4,16,512]{2,1,0:T(8,128)(2,1)S(1)} %get-tuple-element.48), channel_id=1, source_target_pairs={{0,96},{32,0},{64,32},{96,64},{128,224},{160,128},{192,160},{224,1... | collective-permute-start | bytes 196616 | tf_op jit(solution)/shard_map/ppermute | solution.py:38
  58.1 10.4 %copy-start.12 = (f32[16,512]{1,0:T(8,128)S(1)}, f32[16,512]{1,0:T(8,128)}, u32[]{:S(2)}) copy-start(f32[16,512]{1,0:T(8,128)} %get-tuple-element.64) | copy-start | bytes 98308
  58.1 20.1 %copy-start.6 = (bf16[1,128,512]{2,1,0:T(8,128)(2,1)S(1)}, bf16[1,128,512]{2,1,0:T(8,128)(2,1)}, u32[]{:S(2)}) copy-start(bf16[1,128,512]{2,1,0:T(8,128)(2,1)} %param.14) | copy-start | bytes 393220
  58.1 20.1 %copy-start.11 = (f32[1,128]{1,0:T(1,128)S(1)}, f32[1,128]{1,0:T(1,128)}, u32[]{:S(2)}) copy-start(f32[1,128]{1,0:T(1,128)} %mask.1) | copy-start | bytes 1540
  58.1 19.9 %all-to-all-start.1 = ((bf16[8,128,512]{2,1,0:T(8,128)(2,1)}), bf16[8,128,512]{2,1,0:T(8,128)(2,1)S(1)}, u32[]{:S(2)}, u32[]{:S(2)}) async-start(bf16[8,128,512]{2,1,0:T(8,128)(2,1)} %project.1), calls=%async_computation.1 | async-start | bytes 2097152 | tf_op jit(solution)/shard_map/all_to_all | solution.py:203
  63.0 15.4 %collective-permute-start.6 = (f32[16,512]{1,0:T(8,128)}, f32[16,512]{1,0:T(8,128)S(1)}, u32[]{:S(2)}, u32[]{:S(2)}) collective-permute-start(f32[16,512]{1,0:T(8,128)} %get-tuple-element.62), channel_id=1, source_target_pairs={{0,128},{32,160},{64,192},{96,224},{128,256},{160,288},{192,320},{... | collective-permute-start | bytes 98312 | tf_op jit(solution)/shard_map/ppermute | solution.py:38
  64.9 13.5 %collective-permute-start.7 = (f32[16,512]{1,0:T(8,128)}, f32[16,512]{1,0:T(8,128)S(1)}, u32[]{:S(2)}, u32[]{:S(2)}) collective-permute-start(f32[16,512]{1,0:T(8,128)} %get-tuple-element.63), channel_id=1, source_target_pairs={{0,256},{32,288},{64,320},{96,352},{128,384},{160,416},{192,448},{... | collective-permute-start | bytes 98312 | tf_op jit(solution)/shard_map/ppermute | solution.py:38
  68.5 9.9 %collective-permute-start.8 = (f32[16,512]{1,0:T(8,128)S(1)}, f32[16,512]{1,0:T(8,128)S(1)}, u32[]{:S(2)}, u32[]{:S(2)}) collective-permute-start(f32[16,512]{1,0:T(8,128)S(1)} %copy-done.12), channel_id=1, source_target_pairs={{0,384},{32,416},{64,448},{96,480},{128,0},{160,32},{192,64},{224,... | collective-permute-start | bytes 98312 | tf_op jit(solution)/shard_map/ppermute | solution.py:38
  78.2 5.6 %copy-start.8 = (f32[16,512]{1,0:T(8,128)S(1)}, f32[16,512]{1,0:T(8,128)}, u32[]{:S(2)}) copy-start(f32[16,512]{1,0:T(8,128)} %param.11) | copy-start | bytes 98308
  78.2 5.6 %copy-start.9 = (f32[16,512]{1,0:T(8,128)S(1)}, f32[16,512]{1,0:T(8,128)}, u32[]{:S(2)}) copy-start(f32[16,512]{1,0:T(8,128)} %param.12) | copy-start | bytes 98308
  78.2 5.6 %copy-start.10 = (f32[16,512]{1,0:T(8,128)S(1)}, f32[16,512]{1,0:T(8,128)}, u32[]{:S(2)}) copy-start(f32[16,512]{1,0:T(8,128)} %get-tuple-element.66) | copy-start | bytes 98308
  79.5 19.4 %all-to-all-start.2 = ((bf16[8,128,512]{2,1,0:T(8,128)(2,1)}), bf16[8,128,512]{2,1,0:T(8,128)(2,1)S(1)}, u32[]{:S(2)}, u32[]{:S(2)}) async-start(bf16[8,128,512]{2,1,0:T(8,128)(2,1)} %broadcast_in_dim.15), calls=%async_computation.2 | async-start | bytes 2097152 | tf_op jit(solution)/shard_map/all_to_all | solution.py:203
  84.5 21.0 %copy-start.7 = (f32[16,512]{1,0:T(8,128)}, f32[16,512]{1,0:T(8,128)S(1)}, u32[]{:S(2)}) copy-start(f32[16,512]{1,0:T(8,128)S(1)} %get-tuple-element.71) | copy-start | bytes 98308
  84.5 9.0 %collective-permute-start.9 = (f32[16,512]{1,0:T(8,128)S(1)}, f32[16,512]{1,0:T(8,128)S(1)}, u32[]{:S(2)}, u32[]{:S(2)}) collective-permute-start(f32[16,512]{1,0:T(8,128)S(1)} %get-tuple-element.71), channel_id=1, source_target_pairs={{0,128},{32,160},{64,192},{96,224},{128,256},{160,288},{192,320},{... | collective-permute-start | bytes 98312 | tf_op jit(solution)/shard_map/ppermute | solution.py:38
  86.4 7.1 %collective-permute-start.10 = (f32[16,512]{1,0:T(8,128)S(1)}, f32[16,512]{1,0:T(8,128)S(1)}, u32[]{:S(2)}, u32[]{:S(2)}) collective-permute-start(f32[16,512]{1,0:T(8,128)S(1)} %get-tuple-element.71), channel_id=1, source_target_pairs={{0,256},{32,288},{64,320},{96,352},{128,384},{160,416},{192,448},{... | collective-permute-start | bytes 98312 | tf_op jit(solution)/shard_map/ppermute | solution.py:38
  90.0 5.3 %collective-permute-start.11 = (f32[16,512]{1,0:T(8,128)S(1)}, f32[16,512]{1,0:T(8,128)S(1)}, u32[]{:S(2)}, u32[]{:S(2)}) collective-permute-start(f32[16,512]{1,0:T(8,128)S(1)} %get-tuple-element.71), channel_id=1, source_target_pairs={{0,384},{32,416},{64,448},{96,480},{128,0},{160,32},{192,64},{224,... | collective-permute-start | bytes 98312 | tf_op jit(solution)/shard_map/ppermute | solution.py:38
  99.4 19.3 %collective-permute-start.12 = (bf16[256,512]{1,0:T(8,128)(2,1)S(1)}, bf16[256,512]{1,0:T(8,128)(2,1)S(1)}, u32[]{:S(2)}, u32[]{:S(2)}) collective-permute-start(bf16[256,512]{1,0:T(8,128)(2,1)S(1)} %gradient.2), channel_id=1, source_target_pairs={{0,8},{1,25},{2,10},{3,27},{4,12},{5,29},{6,14},{7,31},{8,16},{9,1... | collective-permute-start | bytes 786440 | tf_op jit(solution)/shard_map/ppermute | solution.py:31
  105.5 13.2 %collective-permute-start.13 = (f32[4,16,512]{2,1,0:T(8,128)S(1)}, f32[4,16,512]{2,1,0:T(8,128)S(1)}, u32[]{:S(2)}, u32[]{:S(2)}) collective-permute-start(f32[4,16,512]{2,1,0:T(8,128)S(1)} %pad_maximum_fusion.refs_0_), channel_id=1, source_target_pairs={{0,32},{32,64},{64,96},{96,0},{128,160},{160,192},{192,224},{224,1... | collective-permute-start | bytes 393224 | tf_op jit(solution)/shard_map/ppermute | solution.py:38
  107.5 11.2 %collective-permute-start.14 = (f32[4,16,512]{2,1,0:T(8,128)S(1)}, f32[4,16,512]{2,1,0:T(8,128)S(1)}, u32[]{:S(2)}, u32[]{:S(2)}) collective-permute-start(f32[4,16,512]{2,1,0:T(8,128)S(1)} %pad_maximum_fusion.refs_0_), channel_id=1, source_target_pairs={{0,64},{32,96},{64,0},{96,32},{128,192},{160,224},{192,128},{224,1... | collective-permute-start | bytes 393224 | tf_op jit(solution)/shard_map/ppermute | solution.py:38
  113.0 0.8 copy-start.2
  113.8 32.5 %copy-start.1 = (bf16[1,256,512]{2,1,0:T(8,128)(2,1)S(1)}, bf16[1,256,512]{2,1,0:T(8,128)(2,1)}, u32[]{:S(2)}) copy-start(bf16[1,256,512]{2,1,0:T(8,128)(2,1)} %param.8) | copy-start | bytes 786436
  113.8 32.5 %copy-start.4 = (f32[1,256,512]{2,1,0:T(8,128)S(1)}, f32[1,256,512]{2,1,0:T(8,128)}, u32[]{:S(2)}) copy-start(f32[1,256,512]{2,1,0:T(8,128)} %param.9) | copy-start | bytes 1572868
  113.8 32.5 %copy-start.5 = (f32[1,256,512]{2,1,0:T(8,128)S(1)}, f32[1,256,512]{2,1,0:T(8,128)}, u32[]{:S(2)}) copy-start(f32[1,256,512]{2,1,0:T(8,128)} %param.10) | copy-start | bytes 1572868
  113.8 32.5 %copy-start.3 = (f32[256,512]{1,0:T(8,128)S(1)}, f32[256,512]{1,0:T(8,128)}, u32[]{:S(2)}) copy-start(f32[256,512]{1,0:T(8,128)} %copy-done.2) | copy-start | bytes 1572868
  113.9 28.1 %collective-permute-start.17 = (bf16[256,512]{1,0:T(8,128)(2,1)S(1)}, bf16[256,512]{1,0:T(8,128)(2,1)S(1)}, u32[]{:S(2)}, u32[]{:S(2)}) collective-permute-start(bf16[256,512]{1,0:T(8,128)(2,1)S(1)} %convert_element_type.45), channel_id=1, source_target_pairs={{0,24},{1,9},{2,26},{3,11},{4,28},{5,13},{6,30},{7,15},{8,0},{9,17... | collective-permute-start | bytes 786440 | tf_op jit(solution)/shard_map/ppermute | solution.py:31
  118.8 27.6 %collective-permute-start.16 = (bf16[256,512]{1,0:T(8,128)(2,1)S(1)}, bf16[256,512]{1,0:T(8,128)(2,1)S(1)}, u32[]{:S(2)}, u32[]{:S(2)}) collective-permute-start(bf16[256,512]{1,0:T(8,128)(2,1)S(1)} %add_convert_fusion), channel_id=1, source_target_pairs={{0,8},{1,25},{2,10},{3,27},{4,12},{5,29},{6,14},{7,31},{8,16},{9,1... | collective-permute-start | bytes 786440 | tf_op jit(solution)/shard_map/ppermute | solution.py:31
  123.3 6.1 %collective-permute-start.15 = (f32[4,16,512]{2,1,0:T(8,128)S(1)}, f32[4,16,512]{2,1,0:T(8,128)S(1)}, u32[]{:S(2)}, u32[]{:S(2)}) collective-permute-start(f32[4,16,512]{2,1,0:T(8,128)S(1)} %pad_maximum_fusion.refs_0_), channel_id=1, source_target_pairs={{0,96},{32,0},{64,32},{96,64},{128,224},{160,128},{192,160},{224,1... | collective-permute-start | bytes 393224 | tf_op jit(solution)/shard_map/ppermute | solution.py:38

commit v8 on v7

--- a/solution.py
+++ b/solution.py
@@ -193,7 +193,10 @@
 def gradient_of(columns, residuals, slabs, width, part_width, dtype):
     return pl.pallas_call(
         functools.partial(gradient_kernel, slabs),
-        out_shape=[jax.ShapeDtypeStruct((width, part_width), dtype)] * len(slabs),
+        out_shape=[
+            (pltpu.HBM if k == 0 else jax.ShapeDtypeStruct)((width, part_width), dtype)
+            for k in slabs
+        ],
         compiler_params=pltpu.CompilerParams(vmem_limit_bytes=32 << 20),
         name="gradient",
     )(columns, residuals)

time: 150 us -> 149 us (level)
  transfers between devices with their start and end apart: 21 -> 21, of which waited for: 9 -> 9; matrix products, arithmetic and copies ran while one was open for 1% -> 1% of each run, Pallas kernels for 4% -> 5%
where the time goes in v8:
time: 149 us; the launch traced here: 148 us
  starting transfers between devices  98 us (66%)
  waiting for transfers between devices  35.5 us (24%)
  Pallas kernels  9.54 us (6%)
  other arithmetic  3.38 us (2%)
    ppermute x6, starting transfers between devices, shift_ring(): return lax.ppermute(value, 'fsdp', pairs)  43.6 us
    ppermute x12, starting transfers between devices, shift_replica(): return lax.ppermute(value, 'replica', pairs)  40 us
    ppermute x6, waiting for transfers between devices, shift_ring(): return lax.ppermute(value, 'fsdp', pairs)  16.4 us
    all_to_all x3, starting transfers between devices, to_plane(): return lax.all_to_all(value, 'fsdp', 0, 0, axis_index_groups=PLANES)  14.4 us
    all_to_all x3, waiting for transfers between devices, to_plane(): return lax.all_to_all(value, 'fsdp', 0, 0, axis_index_groups=PLANES)  9.68 us
    ppermute x12, waiting for transfers between devices, shift_replica(): return lax.ppermute(value, 'replica', pairs)  9.43 us
  transfers between devices with their start and end apart: 21, of which 9 were waited for; matrix products, arithmetic and copies ran while one was open for 1% of the time, Pallas kernels for 5%

profile of v8, /device:TPU:1, one launch (start us, length us, event | category | flops | bytes accessed | tf_op | source)
XLA Modules:
  0.0 148.5 jit_solution(16888477142247926633)
XLA Ops:
  0.6 13.3 %collective-permute-start = (bf16[256,512]{1,0:T(8,128)(2,1)}, bf16[256,512]{1,0:T(8,128)(2,1)S(1)}, u32[]{:S(2)}, u32[]{:S(2)}) collective-permute-start(bf16[256,512]{1,0:T(8,128)(2,1)} %bitcast.41), channel_id=1, source_target_pairs={{0,8},{1,25},{2,10},{3,27},{4,12},{5,29},{6,14},{7,31},{8,16},{9,1... | collective-permute-start | bytes 786440 | tf_op jit(solution)/shard_map/ppermute | solution.py:31
  13.9 1.9 %collective-permute-start.4 = (bf16[256,512]{1,0:T(8,128)(2,1)}, bf16[256,512]{1,0:T(8,128)(2,1)S(1)}, u32[]{:S(2)}, u32[]{:S(2)}) collective-permute-start(bf16[256,512]{1,0:T(8,128)(2,1)} %bitcast.42), channel_id=1, source_target_pairs={{0,24},{1,9},{2,26},{3,11},{4,28},{5,13},{6,30},{7,15},{8,0},{9,17... | collective-permute-start | bytes 786440 | tf_op jit(solution)/shard_map/ppermute | solution.py:31
  15.9 2.5 %pack_columns.1 = (bf16[8,128,1024]{2,1,0:T(8,128)(2,1)}, bf16[4,16,512]{2,1,0:T(8,128)(2,1)S(1)}, bf16[4,16,512]{2,1,0:T(8,128)(2,1)S(1)}, bf16[4,16,512]{2,1,0:T(8,128)(2,1)S(1)}, bf16[4,16,512]{2,1,0:T(8,128)(2,1)S(1)}) custom-call(bf16[128,8192]{1,0:T(8,128)(2,1)} %bitcast.45, bf16[4,4,16,512]{3,2,1,0:T(8,128)(2,1)} %bitcast.43), custom_call_target="tpu_custom_call" | custom-call | tf_op jit(solution)/shard_map/pack_columns/pallas_call | solution.py:86
  18.4 5.3 %all-to-all-start = ((bf16[8,128,1024]{2,1,0:T(8,128)(2,1)}), bf16[8,128,1024]{2,1,0:T(8,128)(2,1)S(1)}, u32[]{:S(2)}, u32[]{:S(2)}) async-start(bf16[8,128,1024]{2,1,0:T(8,128)(2,1)} %get-tuple-element.43), calls=%async_computation | async-start | bytes 4194304 | tf_op jit(solution)/shard_map/all_to_all | solution.py:206
  23.7 3.3 %collective-permute-start.1 = (bf16[4,16,512]{2,1,0:T(8,128)(2,1)S(1)}, bf16[4,16,512]{2,1,0:T(8,128)(2,1)S(1)}, u32[]{:S(2)}, u32[]{:S(2)}) collective-permute-start(bf16[4,16,512]{2,1,0:T(8,128)(2,1)S(1)} %get-tuple-element.45), channel_id=1, source_target_pairs={{0,32},{32,64},{64,96},{96,0},{128,160},{160,192},{192,224},{224,1... | collective-permute-start | bytes 196616 | tf_op jit(solution)/shard_map/ppermute | solution.py:38
  27.0 1.2 mask.1
  28.2 2.5 %collective-permute-done.1.refs_1_ = bf16[4,16,512]{2,1,0:T(8,128)(2,1)S(1)} collective-permute-done((bf16[4,16,512]{2,1,0:T(8,128)(2,1)S(1)}, bf16[4,16,512]{2,1,0:T(8,128)(2,1)S(1)}, u32[]{:S(2)}, u32[]{:S(2)}) %collective-permute-start.1) | collective-permute-done | bytes 65568 | tf_op jit(solution)/shard_map/ppermute | solution.py:38
  30.7 0.5 collective-permute-done.w1_ref
  31.3 13.0 %collective-permute-start.5 = (bf16[256,512]{1,0:T(8,128)(2,1)S(1)}, bf16[256,512]{1,0:T(8,128)(2,1)S(1)}, u32[]{:S(2)}, u32[]{:S(2)}) collective-permute-start(bf16[256,512]{1,0:T(8,128)(2,1)S(1)} %collective-permute-done.w1_ref), channel_id=1, source_target_pairs={{0,8},{1,25},{2,10},{3,27},{4,12},{5,29},{6,14},{7,31},{8,16},{9,1... | collective-permute-start | bytes 786440 | tf_op jit(solution)/shard_map/ppermute | solution.py:31
  44.3 5.1 %collective-permute-start.2 = (bf16[4,16,512]{2,1,0:T(8,128)(2,1)S(1)}, bf16[4,16,512]{2,1,0:T(8,128)(2,1)S(1)}, u32[]{:S(2)}, u32[]{:S(2)}) collective-permute-start(bf16[4,16,512]{2,1,0:T(8,128)(2,1)S(1)} %get-tuple-element.47), channel_id=1, source_target_pairs={{0,64},{32,96},{64,0},{96,32},{128,192},{160,224},{192,128},{224,1... | collective-permute-start | bytes 196616 | tf_op jit(solution)/shard_map/ppermute | solution.py:38
  49.4 2.7 %collective-permute-start.3 = (bf16[4,16,512]{2,1,0:T(8,128)(2,1)S(1)}, bf16[4,16,512]{2,1,0:T(8,128)(2,1)S(1)}, u32[]{:S(2)}, u32[]{:S(2)}) collective-permute-start(bf16[4,16,512]{2,1,0:T(8,128)(2,1)S(1)} %get-tuple-element.48), channel_id=1, source_target_pairs={{0,96},{32,0},{64,32},{96,64},{128,224},{160,128},{192,160},{224,1... | collective-permute-start | bytes 196616 | tf_op jit(solution)/shard_map/ppermute | solution.py:38
  52.1 0.0 collective-permute-done.2.refs_2_
  52.1 3.2 %collective-permute-done.3.refs_3_ = bf16[4,16,512]{2,1,0:T(8,128)(2,1)S(1)} collective-permute-done((bf16[4,16,512]{2,1,0:T(8,128)(2,1)S(1)}, bf16[4,16,512]{2,1,0:T(8,128)(2,1)S(1)}, u32[]{:S(2)}, u32[]{:S(2)}) %collective-permute-start.3) | collective-permute-done | bytes 65568 | tf_op jit(solution)/shard_map/ppermute | solution.py:38
  55.2 0.7 add_shares.1
  55.9 0.0 all-to-all-done
  55.9 0.0 collective-permute-done.4.w2_ref
  55.9 0.0 collective-permute-done.5.w3_ref
  55.9 0.0 copy-done
  55.9 2.2 %project.1 = bf16[8,128,512]{2,1,0:T(8,128)(2,1)} custom-call(bf16[1024,1024]{1,0:T(8,128)(2,1)S(1)} %bitcast.38, bf16[256,512]{1,0:T(8,128)(2,1)S(1)} %bitcast.44, bf16[256,512]{1,0:T(8,128)(2,1)S(1)} %collective-permute-done.w1_ref, bf16[256,512]{1,0:T(8,128)(2,1)S(1)} %collective-permute-done.4.w2_ref, bf16[256,512]{1,0:T(8,128)(2,1)S(1)} %collective-permute-done.5.w3_ref), custom_call_target="tpu_custom_call" | custom-call | tf_op jit(solution)/shard_map/project/pallas_call | solution.py:172
  58.1 4.8 %all-to-all-start.1 = ((bf16[8,128,512]{2,1,0:T(8,128)(2,1)}), bf16[8,128,512]{2,1,0:T(8,128)(2,1)S(1)}, u32[]{:S(2)}, u32[]{:S(2)}) async-start(bf16[8,128,512]{2,1,0:T(8,128)(2,1)} %project.1), calls=%async_computation.1 | async-start | bytes 2097152 | tf_op jit(solution)/shard_map/all_to_all | solution.py:206
  63.0 1.9 %collective-permute-start.6 = (f32[16,512]{1,0:T(8,128)}, f32[16,512]{1,0:T(8,128)S(1)}, u32[]{:S(2)}, u32[]{:S(2)}) collective-permute-start(f32[16,512]{1,0:T(8,128)} %get-tuple-element.62), channel_id=1, source_target_pairs={{0,128},{32,160},{64,192},{96,224},{128,256},{160,288},{192,320},{... | collective-permute-start | bytes 98312 | tf_op jit(solution)/shard_map/ppermute | solution.py:38
  64.9 3.6 %collective-permute-start.7 = (f32[16,512]{1,0:T(8,128)}, f32[16,512]{1,0:T(8,128)S(1)}, u32[]{:S(2)}, u32[]{:S(2)}) collective-permute-start(f32[16,512]{1,0:T(8,128)} %get-tuple-element.63), channel_id=1, source_target_pairs={{0,256},{32,288},{64,320},{96,352},{128,384},{160,416},{192,448},{... | collective-permute-start | bytes 98312 | tf_op jit(solution)/shard_map/ppermute | solution.py:38
  68.5 0.0 copy-done.11
  68.5 3.5 %collective-permute-start.8 = (f32[16,512]{1,0:T(8,128)S(1)}, f32[16,512]{1,0:T(8,128)S(1)}, u32[]{:S(2)}, u32[]{:S(2)}) collective-permute-start(f32[16,512]{1,0:T(8,128)S(1)} %copy-done.11), channel_id=1, source_target_pairs={{0,384},{32,416},{64,448},{96,480},{128,0},{160,32},{192,64},{224,... | collective-permute-start | bytes 98312 | tf_op jit(solution)/shard_map/ppermute | solution.py:38
  72.0 6.1 %all-to-all-done.1 = bf16[8,128,512]{2,1,0:T(8,128)(2,1)S(1)} async-done(((bf16[8,128,512]{2,1,0:T(8,128)(2,1)}), bf16[8,128,512]{2,1,0:T(8,128)(2,1)S(1)}, u32[]{:S(2)}, u32[]{:S(2)}) %all-to-all-start.1) | async-done | bytes 1048608 | tf_op jit(solution)/shard_map/all_to_all | solution.py:206
  78.1 0.1 convert_reduce_fusion
  78.2 0.0 copy-start.7
  78.2 0.0 copy-start.8
  78.2 0.0 copy-start.9
  78.2 0.0 copy-done.5
  78.2 0.0 copy-done.10
  78.3 0.1 fusion.12
  78.4 0.0 collective-permute-done.6
  78.4 0.0 collective-permute-done.7
  78.4 0.0 collective-permute-done.8
  78.4 1.1 broadcast_in_dim.15
  79.4 4.3 %all-to-all-start.2 = ((bf16[8,128,512]{2,1,0:T(8,128)(2,1)}), bf16[8,128,512]{2,1,0:T(8,128)(2,1)S(1)}, u32[]{:S(2)}, u32[]{:S(2)}) async-start(bf16[8,128,512]{2,1,0:T(8,128)(2,1)} %broadcast_in_dim.15), calls=%async_computation.2 | async-start | bytes 2097152 | tf_op jit(solution)/shard_map/all_to_all | solution.py:206
  83.8 0.0 copy-done.7
  83.8 0.6 multiply_subtract_fusion
  84.4 1.9 %collective-permute-start.9 = (f32[16,512]{1,0:T(8,128)S(1)}, f32[16,512]{1,0:T(8,128)S(1)}, u32[]{:S(2)}, u32[]{:S(2)}) collective-permute-start(f32[16,512]{1,0:T(8,128)S(1)} %get-tuple-element.71), channel_id=1, source_target_pairs={{0,128},{32,160},{64,192},{96,224},{128,256},{160,288},{192,320},{... | collective-permute-start | bytes 98312 | tf_op jit(solution)/shard_map/ppermute | solution.py:38
  86.3 3.6 %collective-permute-start.10 = (f32[16,512]{1,0:T(8,128)S(1)}, f32[16,512]{1,0:T(8,128)S(1)}, u32[]{:S(2)}, u32[]{:S(2)}) collective-permute-start(f32[16,512]{1,0:T(8,128)S(1)} %get-tuple-element.71), channel_id=1, source_target_pairs={{0,256},{32,288},{64,320},{96,352},{128,384},{160,416},{192,448},{... | collective-permute-start | bytes 98312 | tf_op jit(solution)/shard_map/ppermute | solution.py:38
  90.0 3.5 %collective-permute-start.11 = (f32[16,512]{1,0:T(8,128)S(1)}, f32[16,512]{1,0:T(8,128)S(1)}, u32[]{:S(2)}, u32[]{:S(2)}) collective-permute-start(f32[16,512]{1,0:T(8,128)S(1)} %get-tuple-element.71), channel_id=1, source_target_pairs={{0,384},{32,416},{64,448},{96,480},{128,0},{160,32},{192,64},{224,... | collective-permute-start | bytes 98312 | tf_op jit(solution)/shard_map/ppermute | solution.py:38
  93.4 0.0 collective-permute-done.9
  93.5 0.0 collective-permute-done.10
  93.5 1.8 %collective-permute-done.11 = f32[16,512]{1,0:T(8,128)S(1)} collective-permute-done((f32[16,512]{1,0:T(8,128)S(1)}, f32[16,512]{1,0:T(8,128)S(1)}, u32[]{:S(2)}, u32[]{:S(2)}) %collective-permute-start.11) | collective-permute-done | bytes 32800 | tf_op jit(solution)/shard_map/ppermute | solution.py:38
  95.3 3.6 %all-to-all-done.2.rows_ref = bf16[8,128,512]{2,1,0:T(8,128)(2,1)S(1)} async-done(((bf16[8,128,512]{2,1,0:T(8,128)(2,1)}), bf16[8,128,512]{2,1,0:T(8,128)(2,1)S(1)}, u32[]{:S(2)}, u32[]{:S(2)}) %all-to-all-start.2) | async-done | bytes 1048608 | tf_op jit(solution)/shard_map/all_to_all | solution.py:206
  98.9 0.5 gradient.2
  99.4 6.0 %collective-permute-start.12 = (bf16[256,512]{1,0:T(8,128)(2,1)S(1)}, bf16[256,512]{1,0:T(8,128)(2,1)S(1)}, u32[]{:S(2)}, u32[]{:S(2)}) collective-permute-start(bf16[256,512]{1,0:T(8,128)(2,1)S(1)} %gradient.2), channel_id=1, source_target_pairs={{0,8},{1,25},{2,10},{3,27},{4,12},{5,29},{6,14},{7,31},{8,16},{9,1... | collective-permute-start | bytes 786440 | tf_op jit(solution)/shard_map/ppermute | solution.py:31
  105.4 2.0 %collective-permute-start.13 = (f32[4,16,512]{2,1,0:T(8,128)S(1)}, f32[4,16,512]{2,1,0:T(8,128)S(1)}, u32[]{:S(2)}, u32[]{:S(2)}) collective-permute-start(f32[4,16,512]{2,1,0:T(8,128)S(1)} %pad_maximum_fusion.refs_0_), channel_id=1, source_target_pairs={{0,32},{32,64},{64,96},{96,0},{128,160},{160,192},{192,224},{224,1... | collective-permute-start | bytes 393224 | tf_op jit(solution)/shard_map/ppermute | solution.py:38
  107.5 4.5 %collective-permute-start.14 = (f32[4,16,512]{2,1,0:T(8,128)S(1)}, f32[4,16,512]{2,1,0:T(8,128)S(1)}, u32[]{:S(2)}, u32[]{:S(2)}) collective-permute-start(f32[4,16,512]{2,1,0:T(8,128)S(1)} %pad_maximum_fusion.refs_0_), channel_id=1, source_target_pairs={{0,64},{32,96},{64,0},{96,32},{128,192},{160,224},{192,128},{224,1... | collective-permute-start | bytes 393224 | tf_op jit(solution)/shard_map/ppermute | solution.py:38
  112.0 1.6 %gradient.3 = (f32[256,512]{1,0:T(8,128)}, f32[256,512]{1,0:T(8,128)S(1)}, f32[256,512]{1,0:T(8,128)S(1)}) custom-call(bf16[1024,1024]{1,0:T(8,128)(2,1)S(1)} %bitcast.40, bf16[8,128,512]{2,1,0:T(8,128)(2,1)S(1)} %all-to-all-done.2.rows_ref), custom_call_target="tpu_custom_call" | custom-call | tf_op jit(solution)/shard_map/gradient/pallas_call | solution.py:194
  113.6 4.8 %collective-permute-start.17 = (bf16[256,512]{1,0:T(8,128)(2,1)S(1)}, bf16[256,512]{1,0:T(8,128)(2,1)S(1)}, u32[]{:S(2)}, u32[]{:S(2)}) collective-permute-start(bf16[256,512]{1,0:T(8,128)(2,1)S(1)} %convert_element_type.45), channel_id=1, source_target_pairs={{0,24},{1,9},{2,26},{3,11},{4,28},{5,13},{6,30},{7,15},{8,0},{9,17... | collective-permute-start | bytes 786440 | tf_op jit(solution)/shard_map/ppermute | solution.py:31
  118.4 0.0 collective-permute-done.13.refs_1_
  118.4 0.0 collective-permute-done.14.refs_2_
  118.4 0.0 collective-permute-done.12
  118.4 0.1 add_convert_fusion
  118.5 4.6 %collective-permute-start.16 = (bf16[256,512]{1,0:T(8,128)(2,1)S(1)}, bf16[256,512]{1,0:T(8,128)(2,1)S(1)}, u32[]{:S(2)}, u32[]{:S(2)}) collective-permute-start(bf16[256,512]{1,0:T(8,128)(2,1)S(1)} %add_convert_fusion), channel_id=1, source_target_pairs={{0,8},{1,25},{2,10},{3,27},{4,12},{5,29},{6,14},{7,31},{8,16},{9,1... | collective-permute-start | bytes 786440 | tf_op jit(solution)/shard_map/ppermute | solution.py:31
  123.1 4.4 %collective-permute-start.15 = (f32[4,16,512]{2,1,0:T(8,128)S(1)}, f32[4,16,512]{2,1,0:T(8,128)S(1)}, u32[]{:S(2)}, u32[]{:S(2)}) collective-permute-start(f32[4,16,512]{2,1,0:T(8,128)S(1)} %pad_maximum_fusion.refs_0_), channel_id=1, source_target_pairs={{0,96},{32,0},{64,32},{96,64},{128,224},{160,128},{192,160},{224,1... | collective-permute-start | bytes 393224 | tf_op jit(solution)/shard_map/ppermute | solution.py:38
  127.4 1.9 %collective-permute-done.15.refs_3_ = f32[4,16,512]{2,1,0:T(8,128)S(1)} collective-permute-done((f32[4,16,512]{2,1,0:T(8,128)S(1)}, f32[4,16,512]{2,1,0:T(8,128)S(1)}, u32[]{:S(2)}, u32[]{:S(2)}) %collective-permute-start.15) | collective-permute-done | bytes 131104 | tf_op jit(solution)/shard_map/ppermute | solution.py:38
  129.4 0.8 place_shares.1
  130.2 11.9 %collective-permute-done.17 = bf16[256,512]{1,0:T(8,128)(2,1)S(1)} collective-permute-done((bf16[256,512]{1,0:T(8,128)(2,1)S(1)}, bf16[256,512]{1,0:T(8,128)(2,1)S(1)}, u32[]{:S(2)}, u32[]{:S(2)}) %collective-permute-start.17) | collective-permute-done | bytes 262176 | tf_op jit(solution)/shard_map/ppermute | solution.py:31
  142.1 3.9 %collective-permute-done.16 = bf16[256,512]{1,0:T(8,128)(2,1)S(1)} collective-permute-done((bf16[256,512]{1,0:T(8,128)(2,1)S(1)}, bf16[256,512]{1,0:T(8,128)(2,1)S(1)}, u32[]{:S(2)}, u32[]{:S(2)}) %collective-permute-start.16) | collective-permute-done | bytes 262176 | tf_op jit(solution)/shard_map/ppermute | solution.py:31
  146.1 0.0 copy-done.2
  146.1 2.4 %fusion.7 = (f32[1,256,512]{2,1,0:T(8,128)}, bf16[1,256,512]{2,1,0:T(8,128)(2,1)}) fusion(f32[1,256,512]{2,1,0:T(8,128)S(1)} %copy-done.2, f32[256,512]{1,0:T(8,128)S(1)} %copy-done.4, bf16[256,512]{1,0:T(8,128)(2,1)S(1)} %collective-permute-done.17, bf16[256,512]{1,0:T(8,128)(2,1)S(1)} %collective-permute-done.16, f32[256,512]{1,0:T(8,128)} %place_shares.1, ...), kind=kLoop, calls=%fused_computation.15 | loop fusion | flops 3014656 | bytes 3670016 | tf_op jit(solution)/shard_map/broadcast_in_dim | solution.py:278
  (17 shorter events, 0.1 us)
Async XLA Ops:
  0.6 30.6 %collective-permute-start = (bf16[256,512]{1,0:T(8,128)(2,1)}, bf16[256,512]{1,0:T(8,128)(2,1)S(1)}, u32[]{:S(2)}, u32[]{:S(2)}) collective-permute-start(bf16[256,512]{1,0:T(8,128)(2,1)} %bitcast.41), channel_id=1, source_target_pairs={{0,8},{1,25},{2,10},{3,27},{4,12},{5,29},{6,14},{7,31},{8,16},{9,1... | collective-permute-start | bytes 786440 | tf_op jit(solution)/shard_map/ppermute | solution.py:31
  13.9 42.0 %collective-permute-start.4 = (bf16[256,512]{1,0:T(8,128)(2,1)}, bf16[256,512]{1,0:T(8,128)(2,1)S(1)}, u32[]{:S(2)}, u32[]{:S(2)}) collective-permute-start(bf16[256,512]{1,0:T(8,128)(2,1)} %bitcast.42), channel_id=1, source_target_pairs={{0,24},{1,9},{2,26},{3,11},{4,28},{5,13},{6,30},{7,15},{8,0},{9,17... | collective-permute-start | bytes 786440 | tf_op jit(solution)/shard_map/ppermute | solution.py:31
  18.4 37.5 %all-to-all-start = ((bf16[8,128,1024]{2,1,0:T(8,128)(2,1)}), bf16[8,128,1024]{2,1,0:T(8,128)(2,1)S(1)}, u32[]{:S(2)}, u32[]{:S(2)}) async-start(bf16[8,128,1024]{2,1,0:T(8,128)(2,1)} %get-tuple-element.43), calls=%async_computation | async-start | bytes 4194304 | tf_op jit(solution)/shard_map/all_to_all | solution.py:206
  23.7 32.2 %copy-start = (bf16[1,256,512]{2,1,0:T(8,128)(2,1)S(1)}, bf16[1,256,512]{2,1,0:T(8,128)(2,1)}, u32[]{:S(2)}) copy-start(bf16[1,256,512]{2,1,0:T(8,128)(2,1)} %param.8) | copy-start | bytes 786436
  23.7 7.1 %collective-permute-start.1 = (bf16[4,16,512]{2,1,0:T(8,128)(2,1)S(1)}, bf16[4,16,512]{2,1,0:T(8,128)(2,1)S(1)}, u32[]{:S(2)}, u32[]{:S(2)}) collective-permute-start(bf16[4,16,512]{2,1,0:T(8,128)(2,1)S(1)} %get-tuple-element.45), channel_id=1, source_target_pairs={{0,32},{32,64},{64,96},{96,0},{128,160},{160,192},{192,224},{224,1... | collective-permute-start | bytes 196616 | tf_op jit(solution)/shard_map/ppermute | solution.py:38
  31.3 24.6 %collective-permute-start.5 = (bf16[256,512]{1,0:T(8,128)(2,1)S(1)}, bf16[256,512]{1,0:T(8,128)(2,1)S(1)}, u32[]{:S(2)}, u32[]{:S(2)}) collective-permute-start(bf16[256,512]{1,0:T(8,128)(2,1)S(1)} %collective-permute-done.w1_ref), channel_id=1, source_target_pairs={{0,8},{1,25},{2,10},{3,27},{4,12},{5,29},{6,14},{7,31},{8,16},{9,1... | collective-permute-start | bytes 786440 | tf_op jit(solution)/shard_map/ppermute | solution.py:31
  44.3 7.8 %collective-permute-start.2 = (bf16[4,16,512]{2,1,0:T(8,128)(2,1)S(1)}, bf16[4,16,512]{2,1,0:T(8,128)(2,1)S(1)}, u32[]{:S(2)}, u32[]{:S(2)}) collective-permute-start(bf16[4,16,512]{2,1,0:T(8,128)(2,1)S(1)} %get-tuple-element.47), channel_id=1, source_target_pairs={{0,64},{32,96},{64,0},{96,32},{128,192},{160,224},{192,128},{224,1... | collective-permute-start | bytes 196616 | tf_op jit(solution)/shard_map/ppermute | solution.py:38
  49.4 5.9 %collective-permute-start.3 = (bf16[4,16,512]{2,1,0:T(8,128)(2,1)S(1)}, bf16[4,16,512]{2,1,0:T(8,128)(2,1)S(1)}, u32[]{:S(2)}, u32[]{:S(2)}) collective-permute-start(bf16[4,16,512]{2,1,0:T(8,128)(2,1)S(1)} %get-tuple-element.48), channel_id=1, source_target_pairs={{0,96},{32,0},{64,32},{96,64},{128,224},{160,128},{192,160},{224,1... | collective-permute-start | bytes 196616 | tf_op jit(solution)/shard_map/ppermute | solution.py:38
  58.1 10.4 %copy-start.11 = (f32[16,512]{1,0:T(8,128)S(1)}, f32[16,512]{1,0:T(8,128)}, u32[]{:S(2)}) copy-start(f32[16,512]{1,0:T(8,128)} %get-tuple-element.64) | copy-start | bytes 98308
  58.1 20.1 %copy-start.5 = (bf16[1,128,512]{2,1,0:T(8,128)(2,1)S(1)}, bf16[1,128,512]{2,1,0:T(8,128)(2,1)}, u32[]{:S(2)}) copy-start(bf16[1,128,512]{2,1,0:T(8,128)(2,1)} %param.14) | copy-start | bytes 393220
  58.1 20.1 %copy-start.10 = (f32[1,128]{1,0:T(1,128)S(1)}, f32[1,128]{1,0:T(1,128)}, u32[]{:S(2)}) copy-start(f32[1,128]{1,0:T(1,128)} %mask.1) | copy-start | bytes 1540
  58.1 19.9 %all-to-all-start.1 = ((bf16[8,128,512]{2,1,0:T(8,128)(2,1)}), bf16[8,128,512]{2,1,0:T(8,128)(2,1)S(1)}, u32[]{:S(2)}, u32[]{:S(2)}) async-start(bf16[8,128,512]{2,1,0:T(8,128)(2,1)} %project.1), calls=%async_computation.1 | async-start | bytes 2097152 | tf_op jit(solution)/shard_map/all_to_all | solution.py:206
  63.0 15.4 %collective-permute-start.6 = (f32[16,512]{1,0:T(8,128)}, f32[16,512]{1,0:T(8,128)S(1)}, u32[]{:S(2)}, u32[]{:S(2)}) collective-permute-start(f32[16,512]{1,0:T(8,128)} %get-tuple-element.62), channel_id=1, source_target_pairs={{0,128},{32,160},{64,192},{96,224},{128,256},{160,288},{192,320},{... | collective-permute-start | bytes 98312 | tf_op jit(solution)/shard_map/ppermute | solution.py:38
  64.9 13.5 %collective-permute-start.7 = (f32[16,512]{1,0:T(8,128)}, f32[16,512]{1,0:T(8,128)S(1)}, u32[]{:S(2)}, u32[]{:S(2)}) collective-permute-start(f32[16,512]{1,0:T(8,128)} %get-tuple-element.63), channel_id=1, source_target_pairs={{0,256},{32,288},{64,320},{96,352},{128,384},{160,416},{192,448},{... | collective-permute-start | bytes 98312 | tf_op jit(solution)/shard_map/ppermute | solution.py:38
  68.5 9.9 %collective-permute-start.8 = (f32[16,512]{1,0:T(8,128)S(1)}, f32[16,512]{1,0:T(8,128)S(1)}, u32[]{:S(2)}, u32[]{:S(2)}) collective-permute-start(f32[16,512]{1,0:T(8,128)S(1)} %copy-done.11), channel_id=1, source_target_pairs={{0,384},{32,416},{64,448},{96,480},{128,0},{160,32},{192,64},{224,... | collective-permute-start | bytes 98312 | tf_op jit(solution)/shard_map/ppermute | solution.py:38
  78.2 5.6 %copy-start.7 = (f32[16,512]{1,0:T(8,128)S(1)}, f32[16,512]{1,0:T(8,128)}, u32[]{:S(2)}) copy-start(f32[16,512]{1,0:T(8,128)} %param.11) | copy-start | bytes 98308
  78.2 5.6 %copy-start.8 = (f32[16,512]{1,0:T(8,128)S(1)}, f32[16,512]{1,0:T(8,128)}, u32[]{:S(2)}) copy-start(f32[16,512]{1,0:T(8,128)} %param.12) | copy-start | bytes 98308
  78.2 5.6 %copy-start.9 = (f32[16,512]{1,0:T(8,128)S(1)}, f32[16,512]{1,0:T(8,128)}, u32[]{:S(2)}) copy-start(f32[16,512]{1,0:T(8,128)} %get-tuple-element.66) | copy-start | bytes 98308
  79.4 19.4 %all-to-all-start.2 = ((bf16[8,128,512]{2,1,0:T(8,128)(2,1)}), bf16[8,128,512]{2,1,0:T(8,128)(2,1)S(1)}, u32[]{:S(2)}, u32[]{:S(2)}) async-start(bf16[8,128,512]{2,1,0:T(8,128)(2,1)} %broadcast_in_dim.15), calls=%async_computation.2 | async-start | bytes 2097152 | tf_op jit(solution)/shard_map/all_to_all | solution.py:206
  84.4 21.0 %copy-start.6 = (f32[16,512]{1,0:T(8,128)}, f32[16,512]{1,0:T(8,128)S(1)}, u32[]{:S(2)}) copy-start(f32[16,512]{1,0:T(8,128)S(1)} %get-tuple-element.71) | copy-start | bytes 98308
  84.4 9.0 %collective-permute-start.9 = (f32[16,512]{1,0:T(8,128)S(1)}, f32[16,512]{1,0:T(8,128)S(1)}, u32[]{:S(2)}, u32[]{:S(2)}) collective-permute-start(f32[16,512]{1,0:T(8,128)S(1)} %get-tuple-element.71), channel_id=1, source_target_pairs={{0,128},{32,160},{64,192},{96,224},{128,256},{160,288},{192,320},{... | collective-permute-start | bytes 98312 | tf_op jit(solution)/shard_map/ppermute | solution.py:38
  86.3 7.1 %collective-permute-start.10 = (f32[16,512]{1,0:T(8,128)S(1)}, f32[16,512]{1,0:T(8,128)S(1)}, u32[]{:S(2)}, u32[]{:S(2)}) collective-permute-start(f32[16,512]{1,0:T(8,128)S(1)} %get-tuple-element.71), channel_id=1, source_target_pairs={{0,256},{32,288},{64,320},{96,352},{128,384},{160,416},{192,448},{... | collective-permute-start | bytes 98312 | tf_op jit(solution)/shard_map/ppermute | solution.py:38
  90.0 5.3 %collective-permute-start.11 = (f32[16,512]{1,0:T(8,128)S(1)}, f32[16,512]{1,0:T(8,128)S(1)}, u32[]{:S(2)}, u32[]{:S(2)}) collective-permute-start(f32[16,512]{1,0:T(8,128)S(1)} %get-tuple-element.71), channel_id=1, source_target_pairs={{0,384},{32,416},{64,448},{96,480},{128,0},{160,32},{192,64},{224,... | collective-permute-start | bytes 98312 | tf_op jit(solution)/shard_map/ppermute | solution.py:38
  99.4 19.0 %collective-permute-start.12 = (bf16[256,512]{1,0:T(8,128)(2,1)S(1)}, bf16[256,512]{1,0:T(8,128)(2,1)S(1)}, u32[]{:S(2)}, u32[]{:S(2)}) collective-permute-start(bf16[256,512]{1,0:T(8,128)(2,1)S(1)} %gradient.2), channel_id=1, source_target_pairs={{0,8},{1,25},{2,10},{3,27},{4,12},{5,29},{6,14},{7,31},{8,16},{9,1... | collective-permute-start | bytes 786440 | tf_op jit(solution)/shard_map/ppermute | solution.py:31
  105.4 12.9 %collective-permute-start.13 = (f32[4,16,512]{2,1,0:T(8,128)S(1)}, f32[4,16,512]{2,1,0:T(8,128)S(1)}, u32[]{:S(2)}, u32[]{:S(2)}) collective-permute-start(f32[4,16,512]{2,1,0:T(8,128)S(1)} %pad_maximum_fusion.refs_0_), channel_id=1, source_target_pairs={{0,32},{32,64},{64,96},{96,0},{128,160},{160,192},{192,224},{224,1... | collective-permute-start | bytes 393224 | tf_op jit(solution)/shard_map/ppermute | solution.py:38
  107.5 10.9 %collective-permute-start.14 = (f32[4,16,512]{2,1,0:T(8,128)S(1)}, f32[4,16,512]{2,1,0:T(8,128)S(1)}, u32[]{:S(2)}, u32[]{:S(2)}) collective-permute-start(f32[4,16,512]{2,1,0:T(8,128)S(1)} %pad_maximum_fusion.refs_0_), channel_id=1, source_target_pairs={{0,64},{32,96},{64,0},{96,32},{128,192},{160,224},{192,128},{224,1... | collective-permute-start | bytes 393224 | tf_op jit(solution)/shard_map/ppermute | solution.py:38
  113.6 32.5 %copy-start.1 = (bf16[1,256,512]{2,1,0:T(8,128)(2,1)S(1)}, bf16[1,256,512]{2,1,0:T(8,128)(2,1)}, u32[]{:S(2)}) copy-start(bf16[1,256,512]{2,1,0:T(8,128)(2,1)} %param.8) | copy-start | bytes 786436
  113.6 32.5 %copy-start.2 = (f32[1,256,512]{2,1,0:T(8,128)S(1)}, f32[1,256,512]{2,1,0:T(8,128)}, u32[]{:S(2)}) copy-start(f32[1,256,512]{2,1,0:T(8,128)} %param.9) | copy-start | bytes 1572868
  113.6 32.5 %copy-start.3 = (f32[1,256,512]{2,1,0:T(8,128)S(1)}, f32[1,256,512]{2,1,0:T(8,128)}, u32[]{:S(2)}) copy-start(f32[1,256,512]{2,1,0:T(8,128)} %param.10) | copy-start | bytes 1572868
  113.6 32.5 %copy-start.4 = (f32[256,512]{1,0:T(8,128)S(1)}, f32[256,512]{1,0:T(8,128)}, u32[]{:S(2)}) copy-start(f32[256,512]{1,0:T(8,128)} %get-tuple-element.78) | copy-start | bytes 1572868
  113.6 28.5 %collective-permute-start.17 = (bf16[256,512]{1,0:T(8,128)(2,1)S(1)}, bf16[256,512]{1,0:T(8,128)(2,1)S(1)}, u32[]{:S(2)}, u32[]{:S(2)}) collective-permute-start(bf16[256,512]{1,0:T(8,128)(2,1)S(1)} %convert_element_type.45), channel_id=1, source_target_pairs={{0,24},{1,9},{2,26},{3,11},{4,28},{5,13},{6,30},{7,15},{8,0},{9,17... | collective-permute-start | bytes 786440 | tf_op jit(solution)/shard_map/ppermute | solution.py:31
  118.5 27.6 %collective-permute-start.16 = (bf16[256,512]{1,0:T(8,128)(2,1)S(1)}, bf16[256,512]{1,0:T(8,128)(2,1)S(1)}, u32[]{:S(2)}, u32[]{:S(2)}) collective-permute-start(bf16[256,512]{1,0:T(8,128)(2,1)S(1)} %add_convert_fusion), channel_id=1, source_target_pairs={{0,8},{1,25},{2,10},{3,27},{4,12},{5,29},{6,14},{7,31},{8,16},{9,1... | collective-permute-start | bytes 786440 | tf_op jit(solution)/shard_map/ppermute | solution.py:31
  123.1 6.3 %collective-permute-start.15 = (f32[4,16,512]{2,1,0:T(8,128)S(1)}, f32[4,16,512]{2,1,0:T(8,128)S(1)}, u32[]{:S(2)}, u32[]{:S(2)}) collective-permute-start(f32[4,16,512]{2,1,0:T(8,128)S(1)} %pad_maximum_fusion.refs_0_), channel_id=1, source_target_pairs={{0,96},{32,0},{64,32},{96,64},{128,224},{160,128},{192,160},{224,1... | collective-permute-start | bytes 393224 | tf_op jit(solution)/shard_map/ppermute | solution.py:38
